TPU v7x, 32 devices: a whole 2x2x4 slice. The times are simulated.
32 devices in a mesh: src: 4 (over z), shard: 4 (over y, core), slab: 2 (over x).
Axes of the slice: x: 2, y: 2, z: 4, core: 2. Of those that a mesh axis runs over, the one named last changes fastest.
Arguments:
- src_feat: bfloat16 [4, 64, 64, 256], P('src', 'slab', 'shard'), may hold values from -6 to 6
- coords: int32 [4, 2], P('src'), may hold values from 0 to 6
- offsets: int32 [2], P('slab'), may hold values from 0 to 2128
- weights: bfloat16 [4, 2, 9, 512, 128], P('src'), may hold values from -0.09375 to 0.09375
Outputs:
- target_feat: bfloat16 [4, 64, 64, 256], P('src', 'slab', 'shard')
All inputs are finite; a program needn't handle non-finite values.
Results may differ from a plain program's by a relative error of at most 0.0047.
Values may be sent and summed in bfloat16 or wider, within the bound.
No kernel may reach another device: no remote copies, remote signals or barrier semaphores. Data moves between devices by JAX's collectives and lax.ppermute only.
A program may use at most 64 MiB of HBM per device.

v0:
```python
import math

import jax
import jax.numpy as jnp
from jax import lax
from jax.sharding import PartitionSpec as P


def with_halo(shard, sides, width):
    for axis, dim in sides:
        size, length = (lax.axis_size(axis), shard.shape[dim])
        up = [(i, (i + 1) % size) for i in range(size - 1)]
        down = [(j, i) for i, j in up]
        last = lax.slice_in_dim(shard, length - width, length, axis=dim)
        leading = lax.slice_in_dim(shard, 0, width, axis=dim)
        before = lax.ppermute(last, axis, up)
        after = lax.ppermute(leading, axis, down)
        shard = jnp.concatenate([before, shard, after], axis=dim)
    return shard


def encoding(rowpos, chan_count):
    channel_idx = jnp.arange(chan_count, dtype=jnp.int32)
    halves = (channel_idx // 2).astype(jnp.float32)
    frequency = jnp.exp(-math.log(1000.0) * halves / (chan_count / 2))
    phases = (channel_idx % 2).astype(jnp.float32) * (math.pi / 2)
    return jnp.sin(rowpos.astype(jnp.float32)[:, None] * frequency[None, :] + phases[None, :])


def blend_weights(coords):
    vertical = coords[:, 0].astype(jnp.float32) / 6.0
    across = coords[:, 1].astype(jnp.float32) / 6.0
    return jnp.stack(
        [
            (1.0 - vertical) * (1.0 - across),
            (1.0 - vertical) * across,
            vertical * (1.0 - across),
            vertical * across,
        ],
        axis=1,
    )


def local(src_feat, coords, offsets, weights):
    row_count = src_feat.shape[1]
    col_count = src_feat.shape[2]
    chan_count = src_feat.shape[3]
    rowpos = offsets[0] + jnp.arange(row_count, dtype=jnp.int32)
    encoded = encoding(rowpos, chan_count)
    posed = (src_feat.astype(jnp.float32) + encoded[None, :, None, :]).astype(jnp.bfloat16)
    all_views = lax.all_gather(posed, "src", axis=0, tiled=True)
    padded = with_halo(all_views, (("shard", 2), ("slab", 1)), 1)
    view_count = padded.shape[0]
    targets = weights.shape[0]
    groups = weights.shape[1]
    out_width = weights.shape[4]
    per_group = view_count // groups
    grouped = padded.reshape(groups, per_group, row_count + 2, col_count + 2, chan_count)
    grouped = grouped.transpose(0, 2, 3, 1, 4).reshape(
        groups, row_count + 2, col_count + 2, per_group * chan_count
    )
    convolved = jnp.zeros((targets, groups, row_count, col_count, out_width), jnp.float32)
    for tap_index in range(9):
        tap_row = tap_index // 3
        tap_col = tap_index % 3
        window = grouped[:, tap_row : tap_row + row_count, tap_col : tap_col + col_count, :]
        convolved = convolved + jnp.einsum(
            "grcn,tgno->tgrco", window, weights[:, :, tap_index], preferred_element_type=jnp.float32
        )
    convolved = convolved.transpose(0, 2, 3, 1, 4).reshape(
        targets, row_count, col_count, groups * out_width
    )
    mixing = blend_weights(coords)
    own_views = padded[:, 1:-1, 1:-1, :]
    blended = jnp.zeros((targets, row_count, col_count, chan_count), jnp.float32)
    for view_index in range(view_count):
        blended = (
            blended
            + mixing[:, view_index, None, None, None]
            * own_views[view_index].astype(jnp.float32)[None]
        )
    return (blended + jax.nn.silu(convolved)).astype(jnp.bfloat16)


def solution(mesh):
    in_specs = (
        P("src", "slab", "shard", None),
        P("src", None),
        P("slab"),
        P("src", None, None, None, None),
    )
    out_specs = P("src", "slab", "shard", None)
    return jax.shard_map(local, mesh=mesh, in_specs=in_specs, out_specs=out_specs, check_vma=False)
```

profile of v0, /device:TPU:1, one launch (start us, length us, event | category | flops | bytes accessed | tf_op | source)
XLA Modules:
  0.0 84.8 jit_solution(17575932375642231468)
XLA Ops:
  6.5 0.0 copy-start.2
  6.5 0.0 all-gather.2.cloned.1.call-start
  7.2 0.2 add_sine_fusion
  7.4 1.7 %add_convert_fusion.1 = bf16[1,32,16,256]{3,2,1,0:T(8,128)(2,1)} fusion(bf16[1,32,16,256]{3,2,1,0:T(8,128)(2,1)} %param.4, f32[32,256]{1,0:T(8,128)S(1)} %add_sine_fusion), kind=kLoop, calls=%fused_computation.22 | loop fusion | flops 393216 | bytes 557056 | tf_op jit(solution)/shard_map/convert_element_type | solution.py:50
  9.1 0.0 all-gather.2.cloned.1.call-update
  9.1 30.0 %all-gather.2.cloned.1.call-done = bf16[4,32,16,256]{3,2,1,0:T(8,128)(2,1)} async-done(((bf16[1,32,16,256]{3,2,1,0:T(8,128)(2,1)}), bf16[4,32,16,256]{3,2,1,0:T(8,128)(2,1)}) %all-gather.2.cloned.1.call-update) | async-done | bytes 1048592 | tf_op jit(solution)/shard_map/all_gather | solution.py:51
  39.2 0.0 copy-start
  39.2 1.5 %fusion.37 = (bf16[4,32,1,256]{3,2,1,0:T(2,128)(2,1)S(1)}, bf16[4,32,1,256]{3,2,1,0:T(2,128)(2,1)S(1)}) fusion(bf16[4,32,16,256]{3,2,1,0:T(8,128)(2,1)} %all-gather.2.cloned.1.call-done), kind=kLoop, calls=%fused_computation.59 | loop fusion | bytes 262144 | tf_op jit(solution)/shard_map/slice | solution.py:14
  40.7 3.8 %collective-permute-start = (bf16[4,32,1,256]{3,2,1,0:T(2,128)(2,1)S(1)}, bf16[4,32,1,256]{3,2,1,0:T(2,128)(2,1)S(1)}, u32[]{:S(2)}, u32[]{:S(2)}) collective-permute-start(bf16[4,32,1,256]{3,2,1,0:T(2,128)(2,1)S(1)} %get-tuple-element.16), channel_id=1, source_target_pairs={{0,2},{2,4},{4,6},{1,3},{3,5},{5,7},{8,10},{10,12},{12,14},{9,11},... | collective-permute-start | bytes 196616 | tf_op jit(solution)/shard_map/ppermute | solution.py:16
  44.5 1.9 %collective-permute-start.1 = (bf16[4,32,1,256]{3,2,1,0:T(2,128)(2,1)S(1)}, bf16[4,32,1,256]{3,2,1,0:T(2,128)(2,1)S(1)}, u32[]{:S(2)}, u32[]{:S(2)}) collective-permute-start(bf16[4,32,1,256]{3,2,1,0:T(2,128)(2,1)S(1)} %get-tuple-element.17), channel_id=1, source_target_pairs={{2,0},{4,2},{6,4},{3,1},{5,3},{7,5},{10,8},{12,10},{14,12},{11,9},... | collective-permute-start | bytes 196616 | tf_op jit(solution)/shard_map/ppermute | solution.py:17
  46.4 0.0 collective-permute-done
  46.4 4.3 %collective-permute-done.1 = bf16[4,32,1,256]{3,2,1,0:T(2,128)(2,1)S(1)} collective-permute-done((bf16[4,32,1,256]{3,2,1,0:T(2,128)(2,1)S(1)}, bf16[4,32,1,256]{3,2,1,0:T(2,128)(2,1)S(1)}, u32[]{:S(2)}, u32[]{:S(2)}) %collective-permute-start.1) | collective-permute-done | bytes 65568 | tf_op jit(solution)/shard_map/ppermute | solution.py:17
  50.8 0.8 pad_maximum_fusion.3
  51.6 3.1 %collective-permute-start.2 = (bf16[4,1,18,256]{3,2,1,0:T(8,128)(2,1)S(1)}, bf16[4,1,18,256]{3,2,1,0:T(8,128)(2,1)S(1)}, u32[]{:S(2)}, u32[]{:S(2)}) collective-permute-start(bf16[4,1,18,256]{3,2,1,0:T(8,128)(2,1)S(1)} %get-tuple-element.5), channel_id=1, source_target_pairs={{0,1},{2,3},{4,5},{6,7},{8,9},{10,11},{12,13},{14,15},{16,17},{18,... | collective-permute-start | bytes 110600 | tf_op jit(solution)/shard_map/ppermute | solution.py:16
  54.7 1.3 %collective-permute-start.3 = (bf16[4,1,18,256]{3,2,1,0:T(8,128)(2,1)S(1)}, bf16[4,1,18,256]{3,2,1,0:T(8,128)(2,1)S(1)}, u32[]{:S(2)}, u32[]{:S(2)}) collective-permute-start(bf16[4,1,18,256]{3,2,1,0:T(8,128)(2,1)S(1)} %get-tuple-element.6), channel_id=1, source_target_pairs={{1,0},{3,2},{5,4},{7,6},{9,8},{11,10},{13,12},{15,14},{17,16},{19,... | collective-permute-start | bytes 110600 | tf_op jit(solution)/shard_map/ppermute | solution.py:17
  56.0 0.0 copy-done.2
  56.0 0.6 fusion.38
  58.0 0.0 collective-permute-done.2
  58.0 1.6 %collective-permute-done.3 = bf16[4,1,18,256]{3,2,1,0:T(8,128)(2,1)S(1)} collective-permute-done((bf16[4,1,18,256]{3,2,1,0:T(8,128)(2,1)S(1)}, bf16[4,1,18,256]{3,2,1,0:T(8,128)(2,1)S(1)}, u32[]{:S(2)}, u32[]{:S(2)}) %collective-permute-start.3) | collective-permute-done | bytes 36896 | tf_op jit(solution)/shard_map/ppermute | solution.py:17
  59.5 0.0 copy-done
  59.5 1.1 %pad_maximum_fusion = bf16[4,34,18,256]{3,2,1,0:T(8,128)(2,1)S(1)} fusion(bf16[4,1,18,256]{3,2,1,0:T(8,128)(2,1)S(1)} %collective-permute-done.3, bf16[4,32,1,256]{3,2,1,0:T(2,128)(2,1)S(1)} %collective-permute-done.1, bf16[4,32,16,256]{3,2,1,0:T(8,128)(2,1)S(1)} %copy-done, bf16[4,32,1,256]{3,2,1,0:T(2,128)(2,1)S(1)} %collective-permute-done, ...), kind=kLoop, calls=%fused_computation | loop fusion | flops 6266880 | bytes 2506752 | tf_op jit(solution)/shard_map/concatenate | solution.py:18
  60.6 1.0 %copy.130 = bf16[2,2,34,18,256]{4,1,0,3,2:T(2,128)(2,1)S(1)} copy(bf16[2,2,34,18,256]{4,3,2,1,0:T(8,128)(2,1)S(1)} %bitcast.102) | data formatting | bytes 2506752 | tf_op jit(solution)/shard_map/reshape | solution.py:58
  61.6 0.8 reshape.201
  62.5 0.0 copy-start.1
  62.5 10.1 %fusion.36 = (bf16[2,32,16,512]{3,0,2,1:T(2,128)(2,1)S(1)}, bf16[2,32,16,512]{3,0,2,1:T(2,128)(2,1)S(1)}, bf16[2,32,16,512]{3,0,2,1:T(2,128)(2,1)S(1)}, bf16[2,3...) fusion(bf16[2,34,18,512]{3,0,2,1:T(2,128)(2,1)S(1)} %reshape.201), kind=kLoop, calls=%fused_computation.58 | loop fusion | bytes 18874368 | tf_op jit(solution)/shard_map/slice | solution.py:66
  72.5 0.0 copy-done.1
  72.5 0.4 fusion.9
  73.0 0.4 convolution_add_fusion.7
  73.4 0.4 convolution_add_fusion.6
  73.9 0.4 convolution_add_fusion.5
  74.3 0.4 convolution_add_fusion.4
  74.8 0.4 convolution_add_fusion.3
  75.2 0.4 convolution_add_fusion.2
  75.7 0.4 convolution_add_fusion.1
  76.1 0.4 fusion
  76.6 0.4 copy.80
  77.0 1.0 %add_convert_fusion = bf16[1,32,16,256]{3,2,1,0:T(8,128)(2,1)} fusion(f32[1,32,16,256]{3,0,2,1:T(1,128)S(1)} %bitcast.104, bf16[4,32,16,256]{3,2,1,0:T(8,128)(2,1)S(1)} %copy-done, f32[]{:T(128)} %bitcast.6, f32[]{:T(128)} %bitcast.5, f32[]{:T(128)} %bitcast.4, f32[]{:T(128)} %bitcast.2), kind=kLoop, calls=%fused_computation.21 | loop fusion | flops 2228224 | bytes 1835024 | tf_op jit(solution)/shard_map/convert_element_type | solution.py:82
  (2 shorter events, 0.0 us)
Async XLA Ops:
  6.5 49.5 %copy-start.2 = (s32[1,2]{1,0:T(1,128)S(1)}, s32[1,2]{1,0:T(1,128)}, u32[]{:S(2)}) copy-start(s32[1,2]{1,0:T(1,128)} %param.5) | copy-start | bytes 28
  6.5 32.6 %all-gather.2.cloned.1.call-start = ((), (), s32[]{:S(2)}) async-start(), calls=%async_computation | async-start | bytes 1310720 | tf_op jit(solution)/shard_map/all_gather | solution.py:51
  39.2 20.4 %copy-start = (bf16[4,32,16,256]{3,2,1,0:T(8,128)(2,1)S(1)}, bf16[4,32,16,256]{3,2,1,0:T(8,128)(2,1)}, u32[]{:S(2)}) copy-start(bf16[4,32,16,256]{3,2,1,0:T(8,128)(2,1)} %all-gather.2.cloned.1.call-done) | copy-start | bytes 3145732
  40.7 5.7 %collective-permute-start = (bf16[4,32,1,256]{3,2,1,0:T(2,128)(2,1)S(1)}, bf16[4,32,1,256]{3,2,1,0:T(2,128)(2,1)S(1)}, u32[]{:S(2)}, u32[]{:S(2)}) collective-permute-start(bf16[4,32,1,256]{3,2,1,0:T(2,128)(2,1)S(1)} %get-tuple-element.16), channel_id=1, source_target_pairs={{0,2},{2,4},{4,6},{1,3},{3,5},{5,7},{8,10},{10,12},{12,14},{9,11},... | collective-permute-start | bytes 196616 | tf_op jit(solution)/shard_map/ppermute | solution.py:16
  44.5 6.3 %collective-permute-start.1 = (bf16[4,32,1,256]{3,2,1,0:T(2,128)(2,1)S(1)}, bf16[4,32,1,256]{3,2,1,0:T(2,128)(2,1)S(1)}, u32[]{:S(2)}, u32[]{:S(2)}) collective-permute-start(bf16[4,32,1,256]{3,2,1,0:T(2,128)(2,1)S(1)} %get-tuple-element.17), channel_id=1, source_target_pairs={{2,0},{4,2},{6,4},{3,1},{5,3},{7,5},{10,8},{12,10},{14,12},{11,9},... | collective-permute-start | bytes 196616 | tf_op jit(solution)/shard_map/ppermute | solution.py:17
  51.6 6.4 %collective-permute-start.2 = (bf16[4,1,18,256]{3,2,1,0:T(8,128)(2,1)S(1)}, bf16[4,1,18,256]{3,2,1,0:T(8,128)(2,1)S(1)}, u32[]{:S(2)}, u32[]{:S(2)}) collective-permute-start(bf16[4,1,18,256]{3,2,1,0:T(8,128)(2,1)S(1)} %get-tuple-element.5), channel_id=1, source_target_pairs={{0,1},{2,3},{4,5},{6,7},{8,9},{10,11},{12,13},{14,15},{16,17},{18,... | collective-permute-start | bytes 110600 | tf_op jit(solution)/shard_map/ppermute | solution.py:16
  54.7 4.8 %collective-permute-start.3 = (bf16[4,1,18,256]{3,2,1,0:T(8,128)(2,1)S(1)}, bf16[4,1,18,256]{3,2,1,0:T(8,128)(2,1)S(1)}, u32[]{:S(2)}, u32[]{:S(2)}) collective-permute-start(bf16[4,1,18,256]{3,2,1,0:T(8,128)(2,1)S(1)} %get-tuple-element.6), channel_id=1, source_target_pairs={{1,0},{3,2},{5,4},{7,6},{9,8},{11,10},{13,12},{15,14},{17,16},{19,... | collective-permute-start | bytes 110600 | tf_op jit(solution)/shard_map/ppermute | solution.py:17
  62.5 10.1 %copy-start.1 = (bf16[1,2,9,512,128]{4,3,2,1,0:T(8,128)(2,1)S(1)}, bf16[1,2,9,512,128]{4,3,2,1,0:T(8,128)(2,1)}, u32[]{:S(2)}) copy-start(bf16[1,2,9,512,128]{4,3,2,1,0:T(8,128)(2,1)} %param.7) | copy-start | bytes 7077892
Sparse Core Ops, SparseCore 0:
  9.3 29.8 all-gather.1
where the time goes:
time: 85.2 us; the launch traced here: 84.8 us
  waiting for transfers between devices  36 us (42%)
  between operations  15.6 us (18%)
  local copies, waits for them, and re-layouts  14.4 us (17%)
  starting transfers between devices  10.1 us (12%)
  other arithmetic  4.85 us (6%)
  matrix products  3.96 us (5%)
    all_gather x1, waiting for transfers between devices, local(): all_views = lax.all_gather(posed, 'src', axis=0, tiled=True)  30 us
    slice x1, local copies, waits for them, and re-layouts, local(): grouped[:, tap_row:tap_row + row_count, tap_col:tap_col + col_count, :]  10.1 us
    ppermute x2, starting transfers between devices, with_halo(): before = lax.ppermute(last, axis, up)  6.89 us
    ppermute x2, waiting for transfers between devices, with_halo(): after = lax.ppermute(leading, axis, down)  5.91 us
    dot_general x9, matrix products, local(): jnp.einsum('grcn,tgno->tgrco', window, weights[:, :, tap_index], preferre...  3.96 us
    ppermute x2, starting transfers between devices, with_halo(): after = lax.ppermute(leading, axis, down)  3.21 us
    convert_element_type x1, other arithmetic, local(): (src_feat.astype(jnp.float32) + encoded[None, :, None, :]).astype(jnp.bfl...  1.71 us
  transfers between devices with their start and end apart: 5, of which 3 were waited for; matrix products, arithmetic and copies ran while one was open for 1% of the time, Pallas kernels for 0%

commit v1 on v0

v1 whole, which is shorter than its diff:
```python
import functools
import math

import jax
import jax.numpy as jnp
from jax import lax
from jax.experimental import pallas as pl
from jax.experimental.pallas import tpu as pltpu
from jax.sharding import PartitionSpec as P

BF16, F32 = jnp.bfloat16, jnp.float32
VMEM_SPEC = pl.BlockSpec(memory_space=pltpu.VMEM)
SMEM_SPEC = pl.BlockSpec(memory_space=pltpu.SMEM)
LANES = 128
PITCH = 24


def encoding(rowpos, chan_count):
    channel_idx = jnp.arange(chan_count, dtype=jnp.int32)
    halves = (channel_idx // 2).astype(F32)
    frequency = jnp.exp(-math.log(1000.0) * halves / (chan_count / 2))
    phases = (channel_idx % 2).astype(F32) * (math.pi / 2)
    return jnp.sin(rowpos.astype(F32)[:, None] * frequency[None, :] + phases[None, :])


def blend_weights(coords):
    vertical = coords[:, 0].astype(F32) / 6.0
    across = coords[:, 1].astype(F32) / 6.0
    return jnp.stack(
        [
            (1.0 - vertical) * (1.0 - across),
            (1.0 - vertical) * across,
            vertical * (1.0 - across),
            vertical * across,
        ],
        axis=1,
    )


def tiles(chan):
    return [(c, slice(c * LANES, (c + 1) * LANES)) for c in range(chan // LANES)]


def borders_kernel(rows, cols, view, enc, first_col, last_col, edge_rows, wide):
    for h in range(rows):
        block = view[h * cols : (h + 1) * cols, :].astype(F32) + enc[h : h + 1, :]
        for c, lanes in tiles(view.shape[1]):
            wide[c, h * cols : (h + 1) * cols, :] = block[:, lanes]
        if h == 0:
            edge_rows[0:cols, :] = block.astype(BF16)
        if h == rows - 1:
            edge_rows[cols : 2 * cols, :] = block.astype(BF16)
    for c, lanes in tiles(view.shape[1]):
        first_col[:, lanes] = wide[c, pl.ds(0, rows, stride=cols), :].astype(BF16)
        last_col[:, lanes] = wide[c, pl.ds(cols - 1, rows, stride=cols), :].astype(BF16)


def corners(left, right, at):
    picked = [left[at : at + 1, :].astype(F32), right[at : at + 1, :].astype(F32)]
    fill = jnp.zeros((14, left.shape[1]), F32)
    return jnp.concatenate(picked + [fill], axis=0).astype(BF16)


def edges_kernel(rows, cols, pick, edge_rows, left, right, *outs):
    if pick:
        first = lax.axis_index(pick) == 0
        out = outs[0]
        out[0:cols, :] = jnp.where(first, edge_rows[cols : 2 * cols, :], edge_rows[0:cols, :])
        out[cols : cols + 16, :] = jnp.where(
            first, corners(left, right, rows - 1), corners(left, right, 0)
        )
    else:
        top, bottom = outs
        top[0:cols, :] = edge_rows[0:cols, :]
        top[cols : cols + 16, :] = corners(left, right, 0)
        bottom[0:cols, :] = edge_rows[cols : 2 * cols, :]
        bottom[cols : cols + 16, :] = corners(left, right, rows - 1)


def strip_kernel(*refs):
    out, at = refs[-1], 0
    for ref in refs[:-1]:
        out[at : at + ref.shape[0], :] = ref[...]
        at += ref.shape[0]


def unfold(rows, cols, pick, view, enc, strip, wide, windows, base, weight, start):
    chan = view.shape[1]
    extra = cols + 16
    before = strip[2 * rows : 2 * rows + extra, :].astype(F32)
    if pick:
        first = lax.axis_index(pick) == 0
        zero = jnp.zeros_like(before)
        before, after = jnp.where(first, zero, before), jnp.where(first, before, zero)
    else:
        after = strip[2 * rows + extra : 2 * rows + 2 * extra, :].astype(F32)
    for c, lanes in tiles(chan):
        for h, edge in ((0, before), (rows + 1, after)):
            at = h * PITCH + 8
            wide[c, at : at + cols, :] = edge[0:cols, lanes]
            wide[c, at - 1 : at, :] = edge[cols : cols + 1, lanes]
            wide[c, at + cols : at + cols + 1, :] = edge[cols + 1 : cols + 2, lanes]
        left, right = strip[0:rows, lanes].astype(F32), strip[rows : 2 * rows, lanes].astype(F32)
        wide[c, pl.ds(PITCH + 7, rows, stride=PITCH), :] = left
        wide[c, pl.ds(PITCH + 8 + cols, rows, stride=PITCH), :] = right
    for h in range(rows):
        here = slice(h * cols, (h + 1) * cols)
        posed = (view[here, :].astype(F32) + enc[h : h + 1, :]).astype(BF16).astype(F32)
        at = (h + 1) * PITCH + 8
        for c, lanes in tiles(chan):
            wide[c, at : at + cols, :] = posed[:, lanes]
        part = weight * posed
        base[here, :] = part if start else base[here, :] + part
    for h in range(rows + 2):
        at = h * PITCH + 7
        here = slice(h * cols, (h + 1) * cols)
        for b in range(3):
            for c in range(chan // LANES):
                to = b * chan + c * LANES
                windows[here, to : to + LANES] = wide[c, at + b : at + b + cols, :].astype(BF16)


def convolve(pixels, cols, windows, weights, view_index):
    chan = windows.shape[1] // 3
    group = lax.div(view_index, 2)
    at = pl.multiple_of(lax.rem(view_index, 2) * chan, chan)
    total = None
    for a in range(3):
        kernel = jnp.concatenate(
            [weights[group, 3 * a + b, pl.ds(at, chan), :] for b in range(3)], axis=0
        )
        part = jnp.dot(
            windows[a * cols : a * cols + pixels, :], kernel, preferred_element_type=F32
        )
        total = part if total is None else total + part
    return total


def silu(x):
    return x / (1.0 + jnp.exp(-x))


def early_kernel(rows, cols, pick, mixing, own, near, far, enc, strip0, strip1, strip2, weights,
                 base, joined, wide, windows):
    me = lax.axis_index("src")
    pixels = rows * cols
    width = joined.shape[1]
    index = [me, jnp.bitwise_xor(me, 1), jnp.bitwise_xor(me, 2)]
    sums = []
    for i, (view, strip) in enumerate(((own, strip0), (near, strip1), (far, strip2))):
        unfold(rows, cols, pick, view, enc, strip, wide, windows, base, mixing[index[i]], i == 0)
        sums.append(convolve(pixels, cols, windows, weights, index[i]))
    joined[...] = sums[2]
    here = pl.ds(pl.multiple_of(lax.div(me, 2) * width, width), width)
    base[:, here] = base[:, here] + silu(sums[0] + sums[1])


def late_kernel(rows, cols, pick, mixing, last, enc, strip, weights, base_in, joined, out,
                wide, windows, base):
    me = lax.axis_index("src")
    pixels = rows * cols
    width = joined.shape[1]
    index = jnp.bitwise_xor(me, 3)
    base[...] = base_in[...]
    unfold(rows, cols, pick, last, enc, strip, wide, windows, base, mixing[index], False)
    total = joined[...] + convolve(pixels, cols, windows, weights, index)
    here = pl.ds(pl.multiple_of(lax.div(index, 2) * width, width), width)
    base[:, here] = base[:, here] + silu(total)
    out[...] = base[...].astype(BF16)


def shape(rows, chan, dtype=BF16):
    return jax.ShapeDtypeStruct((rows, chan), dtype)


def call(kernel, ins, outs, scratch=(), smem=0, cost=None):
    return pl.pallas_call(
        kernel,
        out_shape=outs,
        in_specs=[SMEM_SPEC] * smem + [VMEM_SPEC] * (len(ins) - smem),
        out_specs=jax.tree.map(lambda _: VMEM_SPEC, outs),
        scratch_shapes=list(scratch),
        compiler_params=pltpu.CompilerParams(vmem_limit_bytes=32 * 1024 * 1024),
        cost_estimate=cost,
    )(*ins)


def local(src_feat, coords, offsets, weights):
    _, rows, cols, chan = src_feat.shape
    pixels = rows * cols
    width = weights.shape[4]
    own = src_feat.reshape(pixels, chan)

    def across(array, k):
        return lax.ppermute(array, "src", [(i, i ^ k) for i in range(4)])

    far = across(own, 2)
    near = across(own, 1)
    rowpos = offsets[0] + jnp.arange(rows, dtype=jnp.int32)
    enc = encoding(rowpos, chan)
    mixing = blend_weights(coords).reshape(4)

    first_col, last_col, edge_rows = call(
        functools.partial(borders_kernel, rows, cols),
        [own, enc],
        [shape(rows, chan), shape(rows, chan), shape(2 * cols, chan)],
        [pltpu.VMEM((chan // LANES, pixels, LANES), F32)],
    )
    shards, slabs = lax.axis_size("shard"), lax.axis_size("slab")
    up = [(i, i + 1) for i in range(shards - 1)]
    left = lax.ppermute(last_col, "shard", up)
    right = lax.ppermute(first_col, "shard", [(j, i) for i, j in up])
    pick = "slab" if slabs == 2 else None
    edge = shape(cols + 16, chan)
    edges = call(
        functools.partial(edges_kernel, rows, cols, pick),
        [edge_rows, left, right],
        [edge] if pick else [edge, edge],
    )
    if pick:
        beyond = [lax.ppermute(edges[0], "slab", [(0, 1), (1, 0)])]
    else:
        up = [(i, i + 1) for i in range(slabs - 1)]
        beyond = [
            lax.ppermute(edges[1], "slab", up),
            lax.ppermute(edges[0], "slab", [(j, i) for i, j in up]),
        ]
    strip_rows = 2 * rows + len(beyond) * (cols + 16)
    strip = call(strip_kernel, [left, right, *beyond], [shape(strip_rows, chan)])[0]
    strips = [strip] + [across(strip, k) for k in (1, 2, 3)]
    last = across(far, 1)

    scratch = [
        pltpu.VMEM((chan // LANES, (rows + 2) * PITCH + 8, LANES), F32),
        pltpu.VMEM(((rows + 2) * cols, 3 * chan), BF16),
    ]
    base, joined = call(
        functools.partial(early_kernel, rows, cols, pick),
        [mixing, own, near, far, enc, *strips[:3], weights[0]],
        [shape(pixels, chan, F32), shape(pixels, width, F32)],
        scratch,
        smem=1,
    )
    out = call(
        functools.partial(late_kernel, rows, cols, pick),
        [mixing, last, enc, strips[3], weights[0], base, joined],
        [shape(pixels, chan)],
        scratch + [pltpu.VMEM((pixels, chan), F32)],
        smem=1,
    )[0]
    return out.reshape(1, rows, cols, chan)


def solution(mesh):
    in_specs = (
        P("src", "slab", "shard", None),
        P("src", None),
        P("slab"),
        P("src", None, None, None, None),
    )
    out_specs = P("src", "slab", "shard", None)
    return jax.shard_map(local, mesh=mesh, in_specs=in_specs, out_specs=out_specs, check_vma=False)
```

time: 85.2 us -> 43.9 us (0.52)
  the two profiles are of different devices: /device:TPU:1 before, /device:TPU:25 now
where the time goes in v1:
time: 43.9 us; the launch traced here: 43.6 us
  waiting for transfers between devices  20.5 us (47%)
  starting transfers between devices  10.9 us (25%)
  Pallas kernels  5.11 us (12%)
  local copies, waits for them, and re-layouts  4.88 us (11%)
  between operations  2.06 us (5%)
    ppermute x6, waiting for transfers between devices, across(): return lax.ppermute(array, 'src', [(i, i ^ k) for i in range(4)])  17.3 us
    pallas_call x5, Pallas kernels, call(): pl.pallas_call(kernel, out_shape=outs, in_specs=[SMEM_SPEC] * smem + [VME...  5.11 us
    ppermute x6, starting transfers between devices, across(): return lax.ppermute(array, 'src', [(i, i ^ k) for i in range(4)])  4.14 us
    unnamed x8, local copies, waits for them, and re-layouts  3.56 us
    ppermute x1, starting transfers between devices, local(): left = lax.ppermute(last_col, 'shard', up)  3.53 us
    ppermute x1, waiting for transfers between devices, local(): right = lax.ppermute(first_col, 'shard', [(j, i) for i, j in up])  3.12 us
    ppermute x1, starting transfers between devices, local(): right = lax.ppermute(first_col, 'shard', [(j, i) for i, j in up])  1.92 us
    slice x1, local copies, waits for them, and re-layouts, blend_weights(): across = coords[:, 1].astype(F32) / 6.0  1.31 us
  transfers between devices with their start and end apart: 9, of which 3 were waited for; matrix products, arithmetic and copies ran while one was open for 4% of the time, Pallas kernels for 7%

profile of v1, /device:TPU:25, one launch (start us, length us, event | category | flops | bytes accessed | tf_op | source)
XLA Modules:
  0.0 43.6 jit_solution(4455847831684477446)
XLA Ops:
  0.0 0.1 collective-permute-start
  0.1 0.1 collective-permute-start.6
  0.8 14.0 %collective-permute-done.far = bf16[512,256]{1,0:T(8,128)(2,1)S(1)} collective-permute-done((bf16[512,256]{1,0:T(8,128)(2,1)}, bf16[512,256]{1,0:T(8,128)(2,1)S(1)}, u32[]{:S(2)}, u32[]{:S(2)}) %collective-permute-start) | collective-permute-done | bytes 262176 | tf_op jit(solution)/shard_map/ppermute | solution.py:195
  14.8 0.0 collective-permute-start.1
  14.8 0.2 add_sine_fusion.enc
  15.0 0.0 copy-start.2
  15.1 0.9 %copy-done.2 = bf16[1,32,16,256]{3,2,1,0:T(8,128)(2,1)S(1)} copy-done((bf16[1,32,16,256]{3,2,1,0:T(8,128)(2,1)S(1)}, bf16[1,32,16,256]{3,2,1,0:T(8,128)(2,1)}, u32[]{:S(2)}) %copy-start.2) | copy-done | bytes 262168
  16.0 0.1 shard_map.46
  16.1 3.5 %collective-permute-start.2 = (bf16[32,256]{1,0:T(8,128)(2,1)S(1)}, bf16[32,256]{1,0:T(8,128)(2,1)S(1)}, u32[]{:S(2)}, u32[]{:S(2)}) collective-permute-start(bf16[32,256]{1,0:T(8,128)(2,1)S(1)} %get-tuple-element.10), channel_id=1, source_target_pairs={{0,2},{2,4},{4,6},{1,3},{3,5},{5,7},{8,10},{10,12},{12,14},{9,11},... | collective-permute-start | bytes 49160 | tf_op jit(solution)/shard_map/ppermute | solution.py:211
  19.6 1.9 %collective-permute-start.3 = (bf16[32,256]{1,0:T(8,128)(2,1)S(1)}, bf16[32,256]{1,0:T(8,128)(2,1)S(1)}, u32[]{:S(2)}, u32[]{:S(2)}) collective-permute-start(bf16[32,256]{1,0:T(8,128)(2,1)S(1)} %get-tuple-element.11), channel_id=1, source_target_pairs={{2,0},{4,2},{6,4},{3,1},{5,3},{7,5},{10,8},{12,10},{14,12},{11,9},... | collective-permute-start | bytes 49160 | tf_op jit(solution)/shard_map/ppermute | solution.py:212
  21.5 0.0 collective-permute-done.2.left.refs_0_
  21.5 3.1 %collective-permute-done.3.right.refs_1_ = bf16[32,256]{1,0:T(8,128)(2,1)S(1)} collective-permute-done((bf16[32,256]{1,0:T(8,128)(2,1)S(1)}, bf16[32,256]{1,0:T(8,128)(2,1)S(1)}, u32[]{:S(2)}, u32[]{:S(2)}) %collective-permute-start.3) | collective-permute-done | bytes 16416 | tf_op jit(solution)/shard_map/ppermute | solution.py:212
  24.7 1.3 %collective-permute-start.4 = (bf16[32,256]{1,0:T(8,128)(2,1)S(1)}, bf16[32,256]{1,0:T(8,128)(2,1)S(1)}, u32[]{:S(2)}, u32[]{:S(2)}) collective-permute-start(bf16[32,256]{1,0:T(8,128)(2,1)S(1)} %shard_map.47), channel_id=1, source_target_pairs={{0,1},{1,0},{2,3},{3,2},{4,5},{5,4},{6,7},{7,6},{8,9},{9,8},{10,11... | collective-permute-start | bytes 49160 | tf_op jit(solution)/shard_map/ppermute | solution.py:221
  26.0 1.3 %fusion.7 = (s32[1,1]{1,0:T(1,128)}, s32[1,1]{1,0:T(1,128)}) fusion(s32[1,2]{1,0:T(1,128)} %param.5), kind=kLoop, calls=%fused_computation.15 | loop fusion | bytes 16 | tf_op jit(solution)/shard_map/slice | solution.py:28
  28.6 0.0 collective-permute-done.4.refs_2_
  28.6 1.8 %collective-permute-start.7 = (bf16[96,256]{1,0:T(8,128)(2,1)S(1)}, bf16[96,256]{1,0:T(8,128)(2,1)S(1)}, u32[]{:S(2)}, u32[]{:S(2)}) collective-permute-start(bf16[96,256]{1,0:T(8,128)(2,1)S(1)} %shard_map.48.strip0), channel_id=1, source_target_pairs={{0,8},{8,0},{16,24},{24,16},{1,9},{9,1},{17,25},{25,17},{2,10},{10... | collective-permute-start | bytes 147464 | tf_op jit(solution)/shard_map/ppermute | solution.py:195
  30.4 0.0 collective-permute-start.8
  30.4 2.2 %collective-permute-start.5 = (bf16[96,256]{1,0:T(8,128)(2,1)S(1)}, bf16[96,256]{1,0:T(8,128)(2,1)S(1)}, u32[]{:S(2)}, u32[]{:S(2)}) collective-permute-start(bf16[96,256]{1,0:T(8,128)(2,1)S(1)} %shard_map.48.strip0), channel_id=1, source_target_pairs={{0,24},{8,16},{16,8},{24,0},{1,25},{9,17},{17,9},{25,1},{2,26},{10... | collective-permute-start | bytes 147464 | tf_op jit(solution)/shard_map/ppermute | solution.py:195
  32.6 0.1 maximum_bitcast_fusion.mixing
  32.6 0.0 collective-permute-done.7.strip1
  32.6 3.3 %collective-permute-done.8.strip2 = bf16[96,256]{1,0:T(8,128)(2,1)S(1)} collective-permute-done((bf16[96,256]{1,0:T(8,128)(2,1)S(1)}, bf16[96,256]{1,0:T(8,128)(2,1)S(1)}, u32[]{:S(2)}, u32[]{:S(2)}) %collective-permute-start.8) | collective-permute-done | bytes 49184 | tf_op jit(solution)/shard_map/ppermute | solution.py:195
  36.0 0.0 collective-permute-done.6.near
  36.0 0.0 copy-start
  36.0 1.7 %copy-done = bf16[1,2,9,512,128]{4,3,2,1,0:T(8,128)(2,1)S(1)} copy-done((bf16[1,2,9,512,128]{4,3,2,1,0:T(8,128)(2,1)S(1)}, bf16[1,2,9,512,128]{4,3,2,1,0:T(8,128)(2,1)}, u32[]{:S(2)}) %copy-start) | copy-done | bytes 2359320
  37.6 0.0 copy-start.3
  37.6 0.9 %copy-done.3 = bf16[1,32,16,256]{3,2,1,0:T(8,128)(2,1)S(1)} copy-done((bf16[1,32,16,256]{3,2,1,0:T(8,128)(2,1)S(1)}, bf16[1,32,16,256]{3,2,1,0:T(8,128)(2,1)}, u32[]{:S(2)}) %copy-start.3) | copy-done | bytes 262168
  38.6 0.0 copy-start.1
  38.6 2.8 %shard_map.49 = (f32[512,256]{1,0:T(8,128)S(1)}, f32[512,128]{1,0:T(8,128)S(1)}) custom-call(f32[4]{0:T(128)S(1)} %maximum_bitcast_fusion.mixing, bf16[512,256]{1,0:T(8,128)(2,1)S(1)} %bitcast.17, bf16[512,256]{1,0:T(8,128)(2,1)S(1)} %collective-permute-done.6.near, bf16[512,256]{1,0:T(8,128)(2,1)S(1)} %collective-permute-done.far, ...), custom_call_target="tpu_custom_call" | custom-call | tf_op jit(solution)/shard_map/pallas_call | solution.py:177
  41.4 0.0 collective-permute-done.5.strip
  41.4 0.0 collective-permute-done.1.last
  41.4 0.0 copy-done.1
  41.4 2.2 %shard_map.50 = bf16[512,256]{1,0:T(8,128)(2,1)} custom-call(f32[4]{0:T(128)S(1)} %maximum_bitcast_fusion.mixing, bf16[512,256]{1,0:T(8,128)(2,1)S(1)} %collective-permute-done.1.last, f32[32,256]{1,0:T(8,128)S(1)} %add_sine_fusion.enc, bf16[96,256]{1,0:T(8,128)(2,1)S(1)} %collective-permute-done.5.strip, bf16[2,9,512,128]{3,2,1,0:T(8,128)(2,1)S(1)} %bitcast.13, ...), custom_call_target="tpu_custom_call" | custom-call | tf_op jit(solution)/shard_map/pallas_call | solution.py:177
  (4 shorter events, 0.0 us)
Async XLA Ops:
  0.0 14.8 %collective-permute-start = (bf16[512,256]{1,0:T(8,128)(2,1)}, bf16[512,256]{1,0:T(8,128)(2,1)S(1)}, u32[]{:S(2)}, u32[]{:S(2)}) collective-permute-start(bf16[512,256]{1,0:T(8,128)(2,1)} %bitcast.14), channel_id=1, source_target_pairs={{0,16},{8,24},{16,0},{24,8},{1,17},{9,25},{17,1},{25,9},{2,18},{10... | collective-permute-start | bytes 786440 | tf_op jit(solution)/shard_map/ppermute | solution.py:195
  0.1 35.9 %collective-permute-start.6 = (bf16[512,256]{1,0:T(8,128)(2,1)}, bf16[512,256]{1,0:T(8,128)(2,1)S(1)}, u32[]{:S(2)}, u32[]{:S(2)}) collective-permute-start(bf16[512,256]{1,0:T(8,128)(2,1)} %bitcast.15), channel_id=1, source_target_pairs={{0,8},{8,0},{16,24},{24,16},{1,9},{9,1},{17,25},{25,17},{2,10},{10... | collective-permute-start | bytes 786440 | tf_op jit(solution)/shard_map/ppermute | solution.py:195
  14.8 26.6 %collective-permute-start.1 = (bf16[512,256]{1,0:T(8,128)(2,1)S(1)}, bf16[512,256]{1,0:T(8,128)(2,1)S(1)}, u32[]{:S(2)}, u32[]{:S(2)}) collective-permute-start(bf16[512,256]{1,0:T(8,128)(2,1)S(1)} %collective-permute-done.far), channel_id=1, source_target_pairs={{0,8},{8,0},{16,24},{24,16},{1,9},{9,1},{17,25},{25,17},{2,10},{10... | collective-permute-start | bytes 786440 | tf_op jit(solution)/shard_map/ppermute | solution.py:195
  15.0 1.0 %copy-start.2 = (bf16[1,32,16,256]{3,2,1,0:T(8,128)(2,1)S(1)}, bf16[1,32,16,256]{3,2,1,0:T(8,128)(2,1)}, u32[]{:S(2)}) copy-start(bf16[1,32,16,256]{3,2,1,0:T(8,128)(2,1)} %param.4) | copy-start | bytes 786436
  16.1 5.5 %collective-permute-start.2 = (bf16[32,256]{1,0:T(8,128)(2,1)S(1)}, bf16[32,256]{1,0:T(8,128)(2,1)S(1)}, u32[]{:S(2)}, u32[]{:S(2)}) collective-permute-start(bf16[32,256]{1,0:T(8,128)(2,1)S(1)} %get-tuple-element.10), channel_id=1, source_target_pairs={{0,2},{2,4},{4,6},{1,3},{3,5},{5,7},{8,10},{10,12},{12,14},{9,11},... | collective-permute-start | bytes 49160 | tf_op jit(solution)/shard_map/ppermute | solution.py:211
  19.6 5.1 %collective-permute-start.3 = (bf16[32,256]{1,0:T(8,128)(2,1)S(1)}, bf16[32,256]{1,0:T(8,128)(2,1)S(1)}, u32[]{:S(2)}, u32[]{:S(2)}) collective-permute-start(bf16[32,256]{1,0:T(8,128)(2,1)S(1)} %get-tuple-element.11), channel_id=1, source_target_pairs={{2,0},{4,2},{6,4},{3,1},{5,3},{7,5},{10,8},{12,10},{14,12},{11,9},... | collective-permute-start | bytes 49160 | tf_op jit(solution)/shard_map/ppermute | solution.py:212
  24.7 3.9 %collective-permute-start.4 = (bf16[32,256]{1,0:T(8,128)(2,1)S(1)}, bf16[32,256]{1,0:T(8,128)(2,1)S(1)}, u32[]{:S(2)}, u32[]{:S(2)}) collective-permute-start(bf16[32,256]{1,0:T(8,128)(2,1)S(1)} %shard_map.47), channel_id=1, source_target_pairs={{0,1},{1,0},{2,3},{3,2},{4,5},{5,4},{6,7},{7,6},{8,9},{9,8},{10,11... | collective-permute-start | bytes 49160 | tf_op jit(solution)/shard_map/ppermute | solution.py:221
  28.6 4.0 %collective-permute-start.7 = (bf16[96,256]{1,0:T(8,128)(2,1)S(1)}, bf16[96,256]{1,0:T(8,128)(2,1)S(1)}, u32[]{:S(2)}, u32[]{:S(2)}) collective-permute-start(bf16[96,256]{1,0:T(8,128)(2,1)S(1)} %shard_map.48.strip0), channel_id=1, source_target_pairs={{0,8},{8,0},{16,24},{24,16},{1,9},{9,1},{17,25},{25,17},{2,10},{10... | collective-permute-start | bytes 147464 | tf_op jit(solution)/shard_map/ppermute | solution.py:195
  30.4 5.6 %collective-permute-start.8 = (bf16[96,256]{1,0:T(8,128)(2,1)S(1)}, bf16[96,256]{1,0:T(8,128)(2,1)S(1)}, u32[]{:S(2)}, u32[]{:S(2)}) collective-permute-start(bf16[96,256]{1,0:T(8,128)(2,1)S(1)} %shard_map.48.strip0), channel_id=1, source_target_pairs={{0,16},{8,24},{16,0},{24,8},{1,17},{9,25},{17,1},{25,9},{2,18},{10... | collective-permute-start | bytes 147464 | tf_op jit(solution)/shard_map/ppermute | solution.py:195
  30.4 11.0 %collective-permute-start.5 = (bf16[96,256]{1,0:T(8,128)(2,1)S(1)}, bf16[96,256]{1,0:T(8,128)(2,1)S(1)}, u32[]{:S(2)}, u32[]{:S(2)}) collective-permute-start(bf16[96,256]{1,0:T(8,128)(2,1)S(1)} %shard_map.48.strip0), channel_id=1, source_target_pairs={{0,24},{8,16},{16,8},{24,0},{1,25},{9,17},{17,9},{25,1},{2,26},{10... | collective-permute-start | bytes 147464 | tf_op jit(solution)/shard_map/ppermute | solution.py:195
  36.0 1.7 %copy-start = (bf16[1,2,9,512,128]{4,3,2,1,0:T(8,128)(2,1)S(1)}, bf16[1,2,9,512,128]{4,3,2,1,0:T(8,128)(2,1)}, u32[]{:S(2)}) copy-start(bf16[1,2,9,512,128]{4,3,2,1,0:T(8,128)(2,1)} %param.7) | copy-start | bytes 7077892
  37.6 0.9 %copy-start.3 = (bf16[1,32,16,256]{3,2,1,0:T(8,128)(2,1)S(1)}, bf16[1,32,16,256]{3,2,1,0:T(8,128)(2,1)}, u32[]{:S(2)}) copy-start(bf16[1,32,16,256]{3,2,1,0:T(8,128)(2,1)} %param.4) | copy-start | bytes 786436
  38.6 2.9 %copy-start.1 = (bf16[1,2,9,512,128]{4,3,2,1,0:T(8,128)(2,1)S(1)}, bf16[1,2,9,512,128]{4,3,2,1,0:T(8,128)(2,1)}, u32[]{:S(2)}) copy-start(bf16[1,2,9,512,128]{4,3,2,1,0:T(8,128)(2,1)} %param.7) | copy-start | bytes 7077892

commit v2 on v1

--- a/solution.py
+++ b/solution.py
@@ -23,25 +23,19 @@
     return jnp.sin(rowpos.astype(F32)[:, None] * frequency[None, :] + phases[None, :])
 
 
-def blend_weights(coords):
-    vertical = coords[:, 0].astype(F32) / 6.0
-    across = coords[:, 1].astype(F32) / 6.0
-    return jnp.stack(
-        [
-            (1.0 - vertical) * (1.0 - across),
-            (1.0 - vertical) * across,
-            vertical * (1.0 - across),
-            vertical * across,
-        ],
-        axis=1,
-    )
+def blend_weight(coords, view_index):
+    vertical = coords[0, 0].astype(F32) / 6.0
+    across = coords[0, 1].astype(F32) / 6.0
+    low, left = lax.div(view_index, 2) == 0, lax.rem(view_index, 2) == 0
+    return jnp.where(low, 1.0 - vertical, vertical) * jnp.where(left, 1.0 - across, across)
 
 
 def tiles(chan):
     return [(c, slice(c * LANES, (c + 1) * LANES)) for c in range(chan // LANES)]
 
 
-def borders_kernel(rows, cols, view, enc, first_col, last_col, edge_rows, wide):
+def borders_kernel(rows, cols, view, enc, col_a, col_b, edge_rows, wide):
+    even = lax.rem(lax.axis_index("shard"), 2) == 0
     for h in range(rows):
         block = view[h * cols : (h + 1) * cols, :].astype(F32) + enc[h : h + 1, :]
         for c, lanes in tiles(view.shape[1]):
@@ -51,37 +45,50 @@
         if h == rows - 1:
             edge_rows[cols : 2 * cols, :] = block.astype(BF16)
     for c, lanes in tiles(view.shape[1]):
-        first_col[:, lanes] = wide[c, pl.ds(0, rows, stride=cols), :].astype(BF16)
-        last_col[:, lanes] = wide[c, pl.ds(cols - 1, rows, stride=cols), :].astype(BF16)
+        first = wide[c, pl.ds(0, rows, stride=cols), :]
+        last = wide[c, pl.ds(cols - 1, rows, stride=cols), :]
+        col_a[:, lanes] = jnp.where(even, last, first).astype(BF16)
+        col_b[:, lanes] = jnp.where(even, first, last).astype(BF16)
+
+
+def sides(got_a, got_b):
+    even = lax.rem(lax.axis_index("shard"), 2) == 0
+    a, b = got_a[...].astype(F32), got_b[...].astype(F32)
+    return jnp.where(even, b, a), jnp.where(even, a, b)
 
 
 def corners(left, right, at):
-    picked = [left[at : at + 1, :].astype(F32), right[at : at + 1, :].astype(F32)]
     fill = jnp.zeros((14, left.shape[1]), F32)
-    return jnp.concatenate(picked + [fill], axis=0).astype(BF16)
-
-
-def edges_kernel(rows, cols, pick, edge_rows, left, right, *outs):
+    return jnp.concatenate([left[at : at + 1], right[at : at + 1], fill], axis=0)
+
+
+def edges_kernel(rows, cols, pick, edge_rows, got_a, got_b, *outs):
+    left, right = sides(got_a, got_b)
+    top = jnp.concatenate([edge_rows[0:cols, :].astype(F32), corners(left, right, 0)], axis=0)
+    bottom = jnp.concatenate(
+        [edge_rows[cols : 2 * cols, :].astype(F32), corners(left, right, rows - 1)], axis=0
+    )
     if pick:
-        first = lax.axis_index(pick) == 0
-        out = outs[0]
-        out[0:cols, :] = jnp.where(first, edge_rows[cols : 2 * cols, :], edge_rows[0:cols, :])
-        out[cols : cols + 16, :] = jnp.where(
-            first, corners(left, right, rows - 1), corners(left, right, 0)
-        )
+        outs[0][...] = jnp.where(lax.axis_index(pick) == 0, bottom, top).astype(BF16)
     else:
-        top, bottom = outs
-        top[0:cols, :] = edge_rows[0:cols, :]
-        top[cols : cols + 16, :] = corners(left, right, 0)
-        bottom[0:cols, :] = edge_rows[cols : 2 * cols, :]
-        bottom[cols : cols + 16, :] = corners(left, right, rows - 1)
-
-
-def strip_kernel(*refs):
-    out, at = refs[-1], 0
+        outs[0][...] = top.astype(BF16)
+        outs[1][...] = bottom.astype(BF16)
+
+
+def strip_kernel(rows, got_a, got_b, *refs):
+    out = refs[-1]
+    left, right = sides(got_a, got_b)
+    out[0:rows, :] = left.astype(BF16)
+    out[rows : 2 * rows, :] = right.astype(BF16)
+    at = 2 * rows
     for ref in refs[:-1]:
         out[at : at + ref.shape[0], :] = ref[...]
         at += ref.shape[0]
+
+
+def join_kernel(panel, strip, out):
+    out[0 : panel.shape[0], :] = panel[...]
+    out[panel.shape[0] :, :] = strip[...]
 
 
 def unfold(rows, cols, pick, view, enc, strip, wide, windows, base, weight, start):
@@ -140,29 +147,33 @@
     return x / (1.0 + jnp.exp(-x))
 
 
-def early_kernel(rows, cols, pick, mixing, own, near, far, enc, strip0, strip1, strip2, weights,
-                 base, joined, wide, windows):
+def early_kernel(rows, cols, pick, coords, own, near, far, enc, strip0, strip1, strip2, weights,
+                 base, joined, last_weight, wide, windows):
     me = lax.axis_index("src")
     pixels = rows * cols
     width = joined.shape[1]
     index = [me, jnp.bitwise_xor(me, 1), jnp.bitwise_xor(me, 2)]
     sums = []
     for i, (view, strip) in enumerate(((own, strip0), (near, strip1), (far, strip2))):
-        unfold(rows, cols, pick, view, enc, strip, wide, windows, base, mixing[index[i]], i == 0)
+        weight = blend_weight(coords, index[i])
+        unfold(rows, cols, pick, view, enc, strip, wide, windows, base, weight, i == 0)
         sums.append(convolve(pixels, cols, windows, weights, index[i]))
     joined[...] = sums[2]
     here = pl.ds(pl.multiple_of(lax.div(me, 2) * width, width), width)
     base[:, here] = base[:, here] + silu(sums[0] + sums[1])
-
-
-def late_kernel(rows, cols, pick, mixing, last, enc, strip, weights, base_in, joined, out,
+    weight = blend_weight(coords, jnp.bitwise_xor(me, 3))
+    last_weight[...] = jnp.full(last_weight.shape, weight, F32)
+
+
+def late_kernel(rows, cols, pick, last, enc, weights, base_in, joined, last_weight, out,
                 wide, windows, base):
     me = lax.axis_index("src")
     pixels = rows * cols
     width = joined.shape[1]
     index = jnp.bitwise_xor(me, 3)
     base[...] = base_in[...]
-    unfold(rows, cols, pick, last, enc, strip, wide, windows, base, mixing[index], False)
+    unfold(rows, cols, pick, last.at[0:pixels], enc, last.at[pixels:], wide, windows, base,
+           last_weight[0:1, :], False)
     total = joined[...] + convolve(pixels, cols, windows, weights, index)
     here = pl.ds(pl.multiple_of(lax.div(index, 2) * width, width), width)
     base[:, here] = base[:, here] + silu(total)
@@ -198,23 +209,26 @@
     near = across(own, 1)
     rowpos = offsets[0] + jnp.arange(rows, dtype=jnp.int32)
     enc = encoding(rowpos, chan)
-    mixing = blend_weights(coords).reshape(4)
-
-    first_col, last_col, edge_rows = call(
+
+    column = shape(rows, chan)
+    col_a, col_b, edge_rows = call(
         functools.partial(borders_kernel, rows, cols),
         [own, enc],
-        [shape(rows, chan), shape(rows, chan), shape(2 * cols, chan)],
+        [column, column, shape(2 * cols, chan)],
         [pltpu.VMEM((chan // LANES, pixels, LANES), F32)],
     )
     shards, slabs = lax.axis_size("shard"), lax.axis_size("slab")
-    up = [(i, i + 1) for i in range(shards - 1)]
-    left = lax.ppermute(last_col, "shard", up)
-    right = lax.ppermute(first_col, "shard", [(j, i) for i, j in up])
+
+    def swap(array, first):
+        pairs = [(i, i + 1) for i in range(first, shards - 1, 2)]
+        return lax.ppermute(array, "shard", pairs + [(j, i) for i, j in pairs])
+
+    got_b, got_a = swap(col_b, 1), swap(col_a, 0)
     pick = "slab" if slabs == 2 else None
     edge = shape(cols + 16, chan)
     edges = call(
         functools.partial(edges_kernel, rows, cols, pick),
-        [edge_rows, left, right],
+        [edge_rows, got_a, got_b],
         [edge] if pick else [edge, edge],
     )
     if pick:
@@ -226,27 +240,29 @@
             lax.ppermute(edges[0], "slab", [(j, i) for i, j in up]),
         ]
     strip_rows = 2 * rows + len(beyond) * (cols + 16)
-    strip = call(strip_kernel, [left, right, *beyond], [shape(strip_rows, chan)])[0]
-    strips = [strip] + [across(strip, k) for k in (1, 2, 3)]
-    last = across(far, 1)
+    strip = call(
+        functools.partial(strip_kernel, rows), [got_a, got_b, *beyond], [shape(strip_rows, chan)]
+    )[0]
+    strip_far, strip_near = across(strip, 2), across(strip, 1)
+    far, near, strip_far, strip_near = lax.optimization_barrier((far, near, strip_far, strip_near))
+    last = across(call(join_kernel, [far, strip_far], [shape(pixels + strip_rows, chan)])[0], 1)
 
     scratch = [
         pltpu.VMEM((chan // LANES, (rows + 2) * PITCH + 8, LANES), F32),
         pltpu.VMEM(((rows + 2) * cols, 3 * chan), BF16),
     ]
-    base, joined = call(
+    base, joined, last_weight = call(
         functools.partial(early_kernel, rows, cols, pick),
-        [mixing, own, near, far, enc, *strips[:3], weights[0]],
-        [shape(pixels, chan, F32), shape(pixels, width, F32)],
+        [coords, own, near, far, enc, strip, strip_near, strip_far, weights[0]],
+        [shape(pixels, chan, F32), shape(pixels, width, F32), shape(8, chan, F32)],
         scratch,
         smem=1,
     )
     out = call(
         functools.partial(late_kernel, rows, cols, pick),
-        [mixing, last, enc, strips[3], weights[0], base, joined],
+        [last, enc, weights[0], base, joined, last_weight],
         [shape(pixels, chan)],
         scratch + [pltpu.VMEM((pixels, chan), F32)],
-        smem=1,
     )[0]
     return out.reshape(1, rows, cols, chan)
 

time: 43.9 us -> 29.8 us (0.68)
  the two profiles are of different devices: /device:TPU:25 before, /device:TPU:1 now
where the time goes in v2:
time: 29.8 us; the launch traced here: 29.6 us
  starting transfers between devices  10.4 us (35%)
  waiting for transfers between devices  9.33 us (31%)
  Pallas kernels  4.63 us (16%)
  local copies, waits for them, and re-layouts  4.21 us (14%)
  between operations  0.74 us (2%)
    ppermute x5, waiting for transfers between devices, across(): return lax.ppermute(array, 'src', [(i, i ^ k) for i in range(4)])  5.38 us
    ppermute x5, starting transfers between devices, across(): return lax.ppermute(array, 'src', [(i, i ^ k) for i in range(4)])  4.82 us
    pallas_call x6, Pallas kernels, call(): pl.pallas_call(kernel, out_shape=outs, in_specs=[SMEM_SPEC] * smem + [VME...  4.63 us
    ppermute x2, starting transfers between devices, swap(): return lax.ppermute(array, 'shard', pairs + [(j, i) for i, j in pairs])  4.35 us
    unnamed x10, local copies, waits for them, and re-layouts  4.21 us
    ppermute x2, waiting for transfers between devices, swap(): return lax.ppermute(array, 'shard', pairs + [(j, i) for i, j in pairs])  2.28 us
    ppermute x1, waiting for transfers between devices, local(): beyond = [lax.ppermute(edges[0], 'slab', [(0, 1), (1, 0)])]  1.67 us
    ppermute x1, starting transfers between devices, local(): beyond = [lax.ppermute(edges[0], 'slab', [(0, 1), (1, 0)])]  1.28 us
  transfers between devices with their start and end apart: 8, of which 4 were waited for; matrix products, arithmetic and copies ran while one was open for 1% of the time, Pallas kernels for 10%

profile of v2, /device:TPU:1, one launch (start us, length us, event | category | flops | bytes accessed | tf_op | source)
XLA Modules:
  0.0 29.6 jit_solution(2569118634536757418)
XLA Ops:
  0.0 3.1 %collective-permute-start = (bf16[512,256]{1,0:T(8,128)(2,1)}, bf16[512,256]{1,0:T(8,128)(2,1)S(1)}, u32[]{:S(2)}, u32[]{:S(2)}) collective-permute-start(bf16[512,256]{1,0:T(8,128)(2,1)} %bitcast.7), channel_id=1, source_target_pairs={{0,16},{8,24},{16,0},{24,8},{1,17},{9,25},{17,1},{25,9},{2,18},{10... | collective-permute-start | bytes 786440 | tf_op jit(solution)/shard_map/ppermute | solution.py:206
  3.1 1.3 %collective-permute-start.1 = (bf16[512,256]{1,0:T(8,128)(2,1)}, bf16[512,256]{1,0:T(8,128)(2,1)S(1)}, u32[]{:S(2)}, u32[]{:S(2)}) collective-permute-start(bf16[512,256]{1,0:T(8,128)(2,1)} %bitcast.8), channel_id=1, source_target_pairs={{0,8},{8,0},{16,24},{24,16},{1,9},{9,1},{17,25},{25,17},{2,10},{10... | collective-permute-start | bytes 786440 | tf_op jit(solution)/shard_map/ppermute | solution.py:206
  5.1 0.2 add_sine_fusion.enc
  5.3 0.0 copy-start.2
  5.3 0.9 %copy-done.2 = bf16[1,32,16,256]{3,2,1,0:T(8,128)(2,1)S(1)} copy-done((bf16[1,32,16,256]{3,2,1,0:T(8,128)(2,1)S(1)}, bf16[1,32,16,256]{3,2,1,0:T(8,128)(2,1)}, u32[]{:S(2)}) %copy-start.2) | copy-done | bytes 262168
  6.3 0.1 shard_map.46
  6.3 1.3 %collective-permute-start.2 = (bf16[32,256]{1,0:T(8,128)(2,1)S(1)}, bf16[32,256]{1,0:T(8,128)(2,1)S(1)}, u32[]{:S(2)}, u32[]{:S(2)}) collective-permute-start(bf16[32,256]{1,0:T(8,128)(2,1)S(1)} %get-tuple-element.15), channel_id=1, source_target_pairs={{0,2},{4,6},{2,0},{6,4},{1,3},{5,7},{3,1},{7,5},{8,10},{12,14},{10... | collective-permute-start | bytes 49160 | tf_op jit(solution)/shard_map/ppermute | solution.py:224
  7.6 3.0 %collective-permute-start.3 = (bf16[32,256]{1,0:T(8,128)(2,1)S(1)}, bf16[32,256]{1,0:T(8,128)(2,1)S(1)}, u32[]{:S(2)}, u32[]{:S(2)}) collective-permute-start(bf16[32,256]{1,0:T(8,128)(2,1)S(1)} %get-tuple-element.16), channel_id=1, source_target_pairs={{2,4},{4,2},{3,5},{5,3},{10,12},{12,10},{11,13},{13,11},{18,20},{2... | collective-permute-start | bytes 49160 | tf_op jit(solution)/shard_map/ppermute | solution.py:224
  10.7 0.0 collective-permute-done.2.got_a
  10.7 2.3 %collective-permute-done.3.got_b = bf16[32,256]{1,0:T(8,128)(2,1)S(1)} collective-permute-done((bf16[32,256]{1,0:T(8,128)(2,1)S(1)}, bf16[32,256]{1,0:T(8,128)(2,1)S(1)}, u32[]{:S(2)}, u32[]{:S(2)}) %collective-permute-start.3) | collective-permute-done | bytes 16416 | tf_op jit(solution)/shard_map/ppermute | solution.py:224
  13.0 1.3 %collective-permute-start.4 = (bf16[32,256]{1,0:T(8,128)(2,1)S(1)}, bf16[32,256]{1,0:T(8,128)(2,1)S(1)}, u32[]{:S(2)}, u32[]{:S(2)}) collective-permute-start(bf16[32,256]{1,0:T(8,128)(2,1)S(1)} %shard_map.47), channel_id=1, source_target_pairs={{0,1},{1,0},{2,3},{3,2},{4,5},{5,4},{6,7},{7,6},{8,9},{9,8},{10,11... | collective-permute-start | bytes 49160 | tf_op jit(solution)/shard_map/ppermute | solution.py:235
  14.3 1.7 %collective-permute-done.4.refs_0_ = bf16[32,256]{1,0:T(8,128)(2,1)S(1)} collective-permute-done((bf16[32,256]{1,0:T(8,128)(2,1)S(1)}, bf16[32,256]{1,0:T(8,128)(2,1)S(1)}, u32[]{:S(2)}, u32[]{:S(2)}) %collective-permute-start.4) | collective-permute-done | bytes 16416 | tf_op jit(solution)/shard_map/ppermute | solution.py:235
  16.0 0.1 collective-permute-start.5
  16.1 0.2 collective-permute-start.6
  16.3 4.0 %collective-permute-done.5.strip.strip2 = bf16[96,256]{1,0:T(8,128)(2,1)S(1)} collective-permute-done((bf16[96,256]{1,0:T(8,128)(2,1)S(1)}, bf16[96,256]{1,0:T(8,128)(2,1)S(1)}, u32[]{:S(2)}, u32[]{:S(2)}) %collective-permute-start.5) | collective-permute-done | bytes 49184 | tf_op jit(solution)/shard_map/ppermute | solution.py:206
  20.3 0.0 collective-permute-done.6.strip1
  20.3 0.0 collective-permute-done.panel.far
  20.3 0.0 collective-permute-done.1.near
  20.3 0.1 collective-permute-start.7
  20.4 0.0 copy-start
  20.4 1.7 %copy-done = bf16[1,2,9,512,128]{4,3,2,1,0:T(8,128)(2,1)S(1)} copy-done((bf16[1,2,9,512,128]{4,3,2,1,0:T(8,128)(2,1)S(1)}, bf16[1,2,9,512,128]{4,3,2,1,0:T(8,128)(2,1)}, u32[]{:S(2)}) %copy-start) | copy-done | bytes 2359320
  22.1 0.0 copy-start.3
  22.1 0.9 %copy-done.3 = bf16[1,32,16,256]{3,2,1,0:T(8,128)(2,1)S(1)} copy-done((bf16[1,32,16,256]{3,2,1,0:T(8,128)(2,1)S(1)}, bf16[1,32,16,256]{3,2,1,0:T(8,128)(2,1)}, u32[]{:S(2)}) %copy-start.3) | copy-done | bytes 262168
  23.0 0.0 copy-start.4
  23.0 0.7 %copy-done.4 = s32[1,2]{1,0:T(1,128)S(1)} copy-done((s32[1,2]{1,0:T(1,128)S(1)}, s32[1,2]{1,0:T(1,128)}, u32[]{:S(2)}) %copy-start.4) | copy-done | bytes 32
  23.7 0.0 copy-start.1
  23.7 2.8 %shard_map.50 = (f32[512,256]{1,0:T(8,128)S(1)}, f32[512,128]{1,0:T(8,128)S(1)}, f32[8,256]{1,0:T(8,128)S(1)}) custom-call(s32[1,2]{1,0:T(1,128)S(1)} %copy-done.4, bf16[512,256]{1,0:T(8,128)(2,1)S(1)} %bitcast.10, bf16[512,256]{1,0:T(8,128)(2,1)S(1)} %collective-permute-done.1.near, bf16[512,256]{1,0:T(8,128)(2,1)S(1)} %collective-permute-done.panel.far, ...), custom_call_target="tpu_custom_call" | custom-call | tf_op jit(solution)/shard_map/pallas_call | solution.py:188
  26.5 1.4 %collective-permute-done.7.last = bf16[608,256]{1,0:T(8,128)(2,1)S(1)} collective-permute-done((bf16[608,256]{1,0:T(8,128)(2,1)S(1)}, bf16[608,256]{1,0:T(8,128)(2,1)S(1)}, u32[]{:S(2)}, u32[]{:S(2)}) %collective-permute-start.7) | collective-permute-done | bytes 311328 | tf_op jit(solution)/shard_map/ppermute | solution.py:206
  27.9 0.0 copy-done.1
  27.9 1.7 %shard_map.51 = bf16[512,256]{1,0:T(8,128)(2,1)} custom-call(bf16[608,256]{1,0:T(8,128)(2,1)S(1)} %collective-permute-done.7.last, f32[32,256]{1,0:T(8,128)S(1)} %add_sine_fusion.enc, bf16[2,9,512,128]{3,2,1,0:T(8,128)(2,1)S(1)} %bitcast.6, f32[512,256]{1,0:T(8,128)S(1)} %get-tuple-element.22.base_in, f32[512,128]{1,0:T(8,128)S(1)} %get-tuple-element.23.joined, ...), custom_call_target="tpu_custom_call" | custom-call | tf_op jit(solution)/shard_map/pallas_call | solution.py:188
  (5 shorter events, 0.1 us)
Async XLA Ops:
  0.0 20.3 %collective-permute-start = (bf16[512,256]{1,0:T(8,128)(2,1)}, bf16[512,256]{1,0:T(8,128)(2,1)S(1)}, u32[]{:S(2)}, u32[]{:S(2)}) collective-permute-start(bf16[512,256]{1,0:T(8,128)(2,1)} %bitcast.7), channel_id=1, source_target_pairs={{0,16},{8,24},{16,0},{24,8},{1,17},{9,25},{17,1},{25,9},{2,18},{10... | collective-permute-start | bytes 786440 | tf_op jit(solution)/shard_map/ppermute | solution.py:206
  3.1 17.2 %collective-permute-start.1 = (bf16[512,256]{1,0:T(8,128)(2,1)}, bf16[512,256]{1,0:T(8,128)(2,1)S(1)}, u32[]{:S(2)}, u32[]{:S(2)}) collective-permute-start(bf16[512,256]{1,0:T(8,128)(2,1)} %bitcast.8), channel_id=1, source_target_pairs={{0,8},{8,0},{16,24},{24,16},{1,9},{9,1},{17,25},{25,17},{2,10},{10... | collective-permute-start | bytes 786440 | tf_op jit(solution)/shard_map/ppermute | solution.py:206
  5.3 1.0 %copy-start.2 = (bf16[1,32,16,256]{3,2,1,0:T(8,128)(2,1)S(1)}, bf16[1,32,16,256]{3,2,1,0:T(8,128)(2,1)}, u32[]{:S(2)}) copy-start(bf16[1,32,16,256]{3,2,1,0:T(8,128)(2,1)} %param.4) | copy-start | bytes 786436
  6.3 4.4 %collective-permute-start.2 = (bf16[32,256]{1,0:T(8,128)(2,1)S(1)}, bf16[32,256]{1,0:T(8,128)(2,1)S(1)}, u32[]{:S(2)}, u32[]{:S(2)}) collective-permute-start(bf16[32,256]{1,0:T(8,128)(2,1)S(1)} %get-tuple-element.15), channel_id=1, source_target_pairs={{0,2},{4,6},{2,0},{6,4},{1,3},{5,7},{3,1},{7,5},{8,10},{12,14},{10... | collective-permute-start | bytes 49160 | tf_op jit(solution)/shard_map/ppermute | solution.py:224
  7.6 5.3 %collective-permute-start.3 = (bf16[32,256]{1,0:T(8,128)(2,1)S(1)}, bf16[32,256]{1,0:T(8,128)(2,1)S(1)}, u32[]{:S(2)}, u32[]{:S(2)}) collective-permute-start(bf16[32,256]{1,0:T(8,128)(2,1)S(1)} %get-tuple-element.16), channel_id=1, source_target_pairs={{2,4},{4,2},{3,5},{5,3},{10,12},{12,10},{11,13},{13,11},{18,20},{2... | collective-permute-start | bytes 49160 | tf_op jit(solution)/shard_map/ppermute | solution.py:224
  13.0 2.9 %collective-permute-start.4 = (bf16[32,256]{1,0:T(8,128)(2,1)S(1)}, bf16[32,256]{1,0:T(8,128)(2,1)S(1)}, u32[]{:S(2)}, u32[]{:S(2)}) collective-permute-start(bf16[32,256]{1,0:T(8,128)(2,1)S(1)} %shard_map.47), channel_id=1, source_target_pairs={{0,1},{1,0},{2,3},{3,2},{4,5},{5,4},{6,7},{7,6},{8,9},{9,8},{10,11... | collective-permute-start | bytes 49160 | tf_op jit(solution)/shard_map/ppermute | solution.py:235
  16.0 4.3 %collective-permute-start.5 = (bf16[96,256]{1,0:T(8,128)(2,1)S(1)}, bf16[96,256]{1,0:T(8,128)(2,1)S(1)}, u32[]{:S(2)}, u32[]{:S(2)}) collective-permute-start(bf16[96,256]{1,0:T(8,128)(2,1)S(1)} %shard_map.48.strip0), channel_id=1, source_target_pairs={{0,16},{8,24},{16,0},{24,8},{1,17},{9,25},{17,1},{25,9},{2,18},{10... | collective-permute-start | bytes 147464 | tf_op jit(solution)/shard_map/ppermute | solution.py:206
  16.1 4.2 %collective-permute-start.6 = (bf16[96,256]{1,0:T(8,128)(2,1)S(1)}, bf16[96,256]{1,0:T(8,128)(2,1)S(1)}, u32[]{:S(2)}, u32[]{:S(2)}) collective-permute-start(bf16[96,256]{1,0:T(8,128)(2,1)S(1)} %shard_map.48.strip0), channel_id=1, source_target_pairs={{0,8},{8,0},{16,24},{24,16},{1,9},{9,1},{17,25},{25,17},{2,10},{10... | collective-permute-start | bytes 147464 | tf_op jit(solution)/shard_map/ppermute | solution.py:206
  20.3 7.6 %collective-permute-start.7 = (bf16[608,256]{1,0:T(8,128)(2,1)S(1)}, bf16[608,256]{1,0:T(8,128)(2,1)S(1)}, u32[]{:S(2)}, u32[]{:S(2)}) collective-permute-start(bf16[608,256]{1,0:T(8,128)(2,1)S(1)} %shard_map.49), channel_id=1, source_target_pairs={{0,8},{8,0},{16,24},{24,16},{1,9},{9,1},{17,25},{25,17},{2,10},{10... | collective-permute-start | bytes 933896 | tf_op jit(solution)/shard_map/ppermute | solution.py:206
  20.4 1.7 %copy-start = (bf16[1,2,9,512,128]{4,3,2,1,0:T(8,128)(2,1)S(1)}, bf16[1,2,9,512,128]{4,3,2,1,0:T(8,128)(2,1)}, u32[]{:S(2)}) copy-start(bf16[1,2,9,512,128]{4,3,2,1,0:T(8,128)(2,1)} %param.7) | copy-start | bytes 7077892
  22.1 0.9 %copy-start.3 = (bf16[1,32,16,256]{3,2,1,0:T(8,128)(2,1)S(1)}, bf16[1,32,16,256]{3,2,1,0:T(8,128)(2,1)}, u32[]{:S(2)}) copy-start(bf16[1,32,16,256]{3,2,1,0:T(8,128)(2,1)} %param.4) | copy-start | bytes 786436
  23.0 0.7 %copy-start.4 = (s32[1,2]{1,0:T(1,128)S(1)}, s32[1,2]{1,0:T(1,128)}, u32[]{:S(2)}) copy-start(s32[1,2]{1,0:T(1,128)} %coords.1) | copy-start | bytes 28
  23.7 4.2 %copy-start.1 = (bf16[1,2,9,512,128]{4,3,2,1,0:T(8,128)(2,1)S(1)}, bf16[1,2,9,512,128]{4,3,2,1,0:T(8,128)(2,1)}, u32[]{:S(2)}) copy-start(bf16[1,2,9,512,128]{4,3,2,1,0:T(8,128)(2,1)} %param.7) | copy-start | bytes 7077892

commit v3 on v2

--- a/solution.py
+++ b/solution.py
@@ -10,7 +10,6 @@
 
 BF16, F32 = jnp.bfloat16, jnp.float32
 VMEM_SPEC = pl.BlockSpec(memory_space=pltpu.VMEM)
-SMEM_SPEC = pl.BlockSpec(memory_space=pltpu.SMEM)
 LANES = 128
 PITCH = 24
 
@@ -24,8 +23,7 @@
 
 
 def blend_weight(coords, view_index):
-    vertical = coords[0, 0].astype(F32) / 6.0
-    across = coords[0, 1].astype(F32) / 6.0
+    vertical, across = coords[0:1, :] / 6.0, coords[1:2, :] / 6.0
     low, left = lax.div(view_index, 2) == 0, lax.rem(view_index, 2) == 0
     return jnp.where(low, 1.0 - vertical, vertical) * jnp.where(left, 1.0 - across, across)
 
@@ -34,27 +32,26 @@
     return [(c, slice(c * LANES, (c + 1) * LANES)) for c in range(chan // LANES)]
 
 
-def borders_kernel(rows, cols, view, enc, col_a, col_b, edge_rows, wide):
+def columns_kernel(rows, cols, view, col_a, col_b, edge_rows, panel, wide):
     even = lax.rem(lax.axis_index("shard"), 2) == 0
-    for h in range(rows):
-        block = view[h * cols : (h + 1) * cols, :].astype(F32) + enc[h : h + 1, :]
-        for c, lanes in tiles(view.shape[1]):
-            wide[c, h * cols : (h + 1) * cols, :] = block[:, lanes]
-        if h == 0:
-            edge_rows[0:cols, :] = block.astype(BF16)
-        if h == rows - 1:
-            edge_rows[cols : 2 * cols, :] = block.astype(BF16)
     for c, lanes in tiles(view.shape[1]):
+        wide[c] = view[:, lanes].astype(F32)
         first = wide[c, pl.ds(0, rows, stride=cols), :]
         last = wide[c, pl.ds(cols - 1, rows, stride=cols), :]
         col_a[:, lanes] = jnp.where(even, last, first).astype(BF16)
         col_b[:, lanes] = jnp.where(even, first, last).astype(BF16)
-
-
-def sides(got_a, got_b):
-    even = lax.rem(lax.axis_index("shard"), 2) == 0
-    a, b = got_a[...].astype(F32), got_b[...].astype(F32)
-    return jnp.where(even, b, a), jnp.where(even, a, b)
+    edge_rows[0:cols, :] = view[0:cols, :]
+    edge_rows[cols : 2 * cols, :] = view[(rows - 1) * cols :, :]
+    panel[...] = view[...]
+
+
+def sides(shards, got_a, got_b, enc):
+    me = lax.axis_index("shard")
+    even = lax.rem(me, 2) == 0
+    a, b = got_a[...].astype(F32) + enc[...], got_b[...].astype(F32) + enc[...]
+    left = jnp.where(me > 0, jnp.where(even, b, a), 0.0)
+    right = jnp.where(me < shards - 1, jnp.where(even, a, b), 0.0)
+    return left, right
 
 
 def corners(left, right, at):
@@ -62,33 +59,28 @@
     return jnp.concatenate([left[at : at + 1], right[at : at + 1], fill], axis=0)
 
 
-def edges_kernel(rows, cols, pick, edge_rows, got_a, got_b, *outs):
-    left, right = sides(got_a, got_b)
-    top = jnp.concatenate([edge_rows[0:cols, :].astype(F32), corners(left, right, 0)], axis=0)
-    bottom = jnp.concatenate(
-        [edge_rows[cols : 2 * cols, :].astype(F32), corners(left, right, rows - 1)], axis=0
-    )
+def edges_kernel(rows, cols, shards, pick, edge_rows, got_a, got_b, enc, *outs):
+    left, right = sides(shards, got_a, got_b, enc)
+    lines = []
+    for i, h in ((0, 0), (1, rows - 1)):
+        row = edge_rows[i * cols : (i + 1) * cols, :].astype(F32) + enc[h : h + 1, :]
+        lines.append(jnp.concatenate([row, corners(left, right, h)], axis=0))
     if pick:
-        outs[0][...] = jnp.where(lax.axis_index(pick) == 0, bottom, top).astype(BF16)
+        outs[0][...] = jnp.where(lax.axis_index(pick) == 0, lines[1], lines[0]).astype(BF16)
     else:
-        outs[0][...] = top.astype(BF16)
-        outs[1][...] = bottom.astype(BF16)
-
-
-def strip_kernel(rows, got_a, got_b, *refs):
+        outs[0][...] = lines[0].astype(BF16)
+        outs[1][...] = lines[1].astype(BF16)
+
+
+def strip_kernel(rows, shards, got_a, got_b, enc, *refs):
     out = refs[-1]
-    left, right = sides(got_a, got_b)
+    left, right = sides(shards, got_a, got_b, enc)
     out[0:rows, :] = left.astype(BF16)
     out[rows : 2 * rows, :] = right.astype(BF16)
     at = 2 * rows
     for ref in refs[:-1]:
         out[at : at + ref.shape[0], :] = ref[...]
         at += ref.shape[0]
-
-
-def join_kernel(panel, strip, out):
-    out[0 : panel.shape[0], :] = panel[...]
-    out[panel.shape[0] :, :] = strip[...]
 
 
 def unfold(rows, cols, pick, view, enc, strip, wide, windows, base, weight, start):
@@ -147,33 +139,38 @@
     return x / (1.0 + jnp.exp(-x))
 
 
-def early_kernel(rows, cols, pick, coords, own, near, far, enc, strip0, strip1, strip2, weights,
-                 base, joined, last_weight, wide, windows):
+def own_kernel(rows, cols, pick, coords, own, enc, strip, weights, base, joined, wide, windows):
+    me = lax.axis_index("src")
+    unfold(rows, cols, pick, own, enc, strip, wide, windows, base, blend_weight(coords, me), True)
+    joined[...] = convolve(rows * cols, cols, windows, weights, me)
+
+
+def middle_kernel(rows, cols, pick, coords, near, far, enc, strip1, strip2, weights, base_in,
+                  joined_in, base, joined, wide, windows):
     me = lax.axis_index("src")
     pixels = rows * cols
     width = joined.shape[1]
-    index = [me, jnp.bitwise_xor(me, 1), jnp.bitwise_xor(me, 2)]
+    base[...] = base_in[...]
     sums = []
-    for i, (view, strip) in enumerate(((own, strip0), (near, strip1), (far, strip2))):
-        weight = blend_weight(coords, index[i])
-        unfold(rows, cols, pick, view, enc, strip, wide, windows, base, weight, i == 0)
-        sums.append(convolve(pixels, cols, windows, weights, index[i]))
-    joined[...] = sums[2]
+    for k, view, strip in ((1, near, strip1), (2, far, strip2)):
+        index = jnp.bitwise_xor(me, k)
+        weight = blend_weight(coords, index)
+        unfold(rows, cols, pick, view, enc, strip, wide, windows, base, weight, False)
+        sums.append(convolve(pixels, cols, windows, weights, index))
+    joined[...] = sums[1]
     here = pl.ds(pl.multiple_of(lax.div(me, 2) * width, width), width)
-    base[:, here] = base[:, here] + silu(sums[0] + sums[1])
-    weight = blend_weight(coords, jnp.bitwise_xor(me, 3))
-    last_weight[...] = jnp.full(last_weight.shape, weight, F32)
-
-
-def late_kernel(rows, cols, pick, last, enc, weights, base_in, joined, last_weight, out,
+    base[:, here] = base[:, here] + silu(joined_in[...] + sums[0])
+
+
+def late_kernel(rows, cols, pick, coords, last, enc, strip, weights, base_in, joined, out,
                 wide, windows, base):
     me = lax.axis_index("src")
     pixels = rows * cols
     width = joined.shape[1]
     index = jnp.bitwise_xor(me, 3)
     base[...] = base_in[...]
-    unfold(rows, cols, pick, last.at[0:pixels], enc, last.at[pixels:], wide, windows, base,
-           last_weight[0:1, :], False)
+    weight = blend_weight(coords, index)
+    unfold(rows, cols, pick, last, enc, strip, wide, windows, base, weight, False)
     total = joined[...] + convolve(pixels, cols, windows, weights, index)
     here = pl.ds(pl.multiple_of(lax.div(index, 2) * width, width), width)
     base[:, here] = base[:, here] + silu(total)
@@ -184,11 +181,11 @@
     return jax.ShapeDtypeStruct((rows, chan), dtype)
 
 
-def call(kernel, ins, outs, scratch=(), smem=0, cost=None):
+def call(kernel, ins, outs, scratch=(), cost=None):
     return pl.pallas_call(
         kernel,
         out_shape=outs,
-        in_specs=[SMEM_SPEC] * smem + [VMEM_SPEC] * (len(ins) - smem),
+        in_specs=[VMEM_SPEC] * len(ins),
         out_specs=jax.tree.map(lambda _: VMEM_SPEC, outs),
         scratch_shapes=list(scratch),
         compiler_params=pltpu.CompilerParams(vmem_limit_bytes=32 * 1024 * 1024),
@@ -211,12 +208,13 @@
     enc = encoding(rowpos, chan)
 
     column = shape(rows, chan)
-    col_a, col_b, edge_rows = call(
-        functools.partial(borders_kernel, rows, cols),
-        [own, enc],
-        [column, column, shape(2 * cols, chan)],
+    col_a, col_b, edge_rows, panel = call(
+        functools.partial(columns_kernel, rows, cols),
+        [own],
+        [column, column, shape(2 * cols, chan), shape(pixels, chan)],
         [pltpu.VMEM((chan // LANES, pixels, LANES), F32)],
     )
+    place = jnp.broadcast_to(coords.astype(F32).reshape(2, 1), (2, chan))
     shards, slabs = lax.axis_size("shard"), lax.axis_size("slab")
 
     def swap(array, first):
@@ -227,8 +225,8 @@
     pick = "slab" if slabs == 2 else None
     edge = shape(cols + 16, chan)
     edges = call(
-        functools.partial(edges_kernel, rows, cols, pick),
-        [edge_rows, got_a, got_b],
+        functools.partial(edges_kernel, rows, cols, shards, pick),
+        [edge_rows, got_a, got_b, enc],
         [edge] if pick else [edge, edge],
     )
     if pick:
@@ -241,26 +239,39 @@
         ]
     strip_rows = 2 * rows + len(beyond) * (cols + 16)
     strip = call(
-        functools.partial(strip_kernel, rows), [got_a, got_b, *beyond], [shape(strip_rows, chan)]
+        functools.partial(strip_kernel, rows, shards),
+        [got_a, got_b, enc, *beyond],
+        [shape(strip_rows, chan)],
     )[0]
-    strip_far, strip_near = across(strip, 2), across(strip, 1)
-    far, near, strip_far, strip_near = lax.optimization_barrier((far, near, strip_far, strip_near))
-    last = across(call(join_kernel, [far, strip_far], [shape(pixels + strip_rows, chan)])[0], 1)
+    strip_near, strip_far = across(strip, 1), across(strip, 2)
+    far, panel = lax.optimization_barrier((far, panel))
+    last = across(far, 1)
 
     scratch = [
         pltpu.VMEM((chan // LANES, (rows + 2) * PITCH + 8, LANES), F32),
         pltpu.VMEM(((rows + 2) * cols, 3 * chan), BF16),
     ]
-    base, joined, last_weight = call(
-        functools.partial(early_kernel, rows, cols, pick),
-        [coords, own, near, far, enc, strip, strip_near, strip_far, weights[0]],
-        [shape(pixels, chan, F32), shape(pixels, width, F32), shape(8, chan, F32)],
+    sums = [shape(pixels, chan, F32), shape(pixels, width, F32)]
+    cost = pl.CostEstimate(flops=5_000_000_000, bytes_accessed=4_000_000, transcendentals=0)
+    base, joined = call(
+        functools.partial(own_kernel, rows, cols, pick),
+        [place, panel, enc, strip, weights[0]],
+        sums,
         scratch,
-        smem=1,
+        cost=cost,
+    )
+    strip_far, base = lax.optimization_barrier((strip_far, base))
+    strip_last = across(strip_far, 1)
+    base, joined = call(
+        functools.partial(middle_kernel, rows, cols, pick),
+        [place, near, far, enc, strip_near, strip_far, weights[0], base, joined],
+        sums,
+        scratch,
+        cost=pl.CostEstimate(flops=0, bytes_accessed=0, transcendentals=0),
     )
     out = call(
         functools.partial(late_kernel, rows, cols, pick),
-        [last, enc, weights[0], base, joined, last_weight],
+        [place, last, enc, strip_last, weights[0], base, joined],
         [shape(pixels, chan)],
         scratch + [pltpu.VMEM((pixels, chan), F32)],
     )[0]

time: 29.8 us -> 27.9 us (0.936)
  the two profiles are of different devices: /device:TPU:1 before, /device:TPU:0 now
where the time goes in v3:
time: 27.9 us; the launch traced here: 27.7 us
  starting transfers between devices  10.6 us (38%)
  waiting for transfers between devices  8.39 us (30%)
  Pallas kernels  4.42 us (16%)
  local copies, waits for them, and re-layouts  2.72 us (10%)
  other arithmetic  0.86 us (3%)
  between operations  0.75 us (3%)
    ppermute x6, starting transfers between devices, across(): return lax.ppermute(array, 'src', [(i, i ^ k) for i in range(4)])  8.3 us
    ppermute x6, waiting for transfers between devices, across(): return lax.ppermute(array, 'src', [(i, i ^ k) for i in range(4)])  6.79 us
    pallas_call x6, Pallas kernels, call(): pl.pallas_call(kernel, out_shape=outs, in_specs=[VMEM_SPEC] * len(ins), o...  4.42 us
    unnamed x6, local copies, waits for them, and re-layouts  2.65 us
    ppermute x1, waiting for transfers between devices, local(): beyond = [lax.ppermute(edges[0], 'slab', [(0, 1), (1, 0)])]  1.59 us
    ppermute x1, starting transfers between devices, local(): beyond = [lax.ppermute(edges[0], 'slab', [(0, 1), (1, 0)])]  1.56 us
    ppermute x2, starting transfers between devices, swap(): return lax.ppermute(array, 'shard', pairs + [(j, i) for i, j in pairs])  0.73 us
    broadcast_in_dim x1, other arithmetic, local(): place = jnp.broadcast_to(coords.astype(F32).reshape(2, 1), (2, chan))  0.66 us
  transfers between devices with their start and end apart: 9, of which 3 were waited for; matrix products, arithmetic and copies ran while one was open for 3% of the time, Pallas kernels for 10%

profile of v3, /device:TPU:0, one launch (start us, length us, event | category | flops | bytes accessed | tf_op | source)
XLA Modules:
  0.0 27.7 jit_solution(12164318772624101861)
XLA Ops:
  0.0 4.0 %collective-permute-start = (bf16[512,256]{1,0:T(8,128)(2,1)}, bf16[512,256]{1,0:T(8,128)(2,1)S(1)}, u32[]{:S(2)}, u32[]{:S(2)}) collective-permute-start(bf16[512,256]{1,0:T(8,128)(2,1)} %bitcast.10), channel_id=1, source_target_pairs={{0,16},{8,24},{16,0},{24,8},{1,17},{9,25},{17,1},{25,9},{2,18},{10... | collective-permute-start | bytes 786440 | tf_op jit(solution)/shard_map/ppermute | solution.py:203
  4.0 1.6 %collective-permute-start.7 = (bf16[512,256]{1,0:T(8,128)(2,1)}, bf16[512,256]{1,0:T(8,128)(2,1)S(1)}, u32[]{:S(2)}, u32[]{:S(2)}) collective-permute-start(bf16[512,256]{1,0:T(8,128)(2,1)} %bitcast.11), channel_id=1, source_target_pairs={{0,8},{8,0},{16,24},{24,16},{1,9},{9,1},{17,25},{25,17},{2,10},{10... | collective-permute-start | bytes 786440 | tf_op jit(solution)/shard_map/ppermute | solution.py:203
  5.6 0.0 copy-start.2
  5.6 1.0 %copy-done.2 = bf16[1,32,16,256]{3,2,1,0:T(8,128)(2,1)S(1)} copy-done((bf16[1,32,16,256]{3,2,1,0:T(8,128)(2,1)S(1)}, bf16[1,32,16,256]{3,2,1,0:T(8,128)(2,1)}, u32[]{:S(2)}) %copy-start.2) | copy-done | bytes 262168
  6.6 0.1 shard_map.46
  6.7 0.1 collective-permute-start.2
  6.8 0.7 %collective-permute-start.3 = (bf16[32,256]{1,0:T(8,128)(2,1)S(1)}, bf16[32,256]{1,0:T(8,128)(2,1)S(1)}, u32[]{:S(2)}, u32[]{:S(2)}) collective-permute-start(bf16[32,256]{1,0:T(8,128)(2,1)S(1)} %get-tuple-element.20), channel_id=1, source_target_pairs={{2,4},{4,2},{3,5},{5,3},{10,12},{12,10},{11,13},{13,11},{18,20},{2... | collective-permute-start | bytes 49160 | tf_op jit(solution)/shard_map/ppermute | solution.py:222
  8.1 0.2 add_sine_fusion.enc
  8.3 0.0 collective-permute-done.2.got_a
  8.3 0.0 collective-permute-done.3.got_b
  8.3 1.6 %collective-permute-start.4 = (bf16[32,256]{1,0:T(8,128)(2,1)S(1)}, bf16[32,256]{1,0:T(8,128)(2,1)S(1)}, u32[]{:S(2)}, u32[]{:S(2)}) collective-permute-start(bf16[32,256]{1,0:T(8,128)(2,1)S(1)} %shard_map.47), channel_id=1, source_target_pairs={{0,1},{1,0},{2,3},{3,2},{4,5},{5,4},{6,7},{7,6},{8,9},{9,8},{10,11... | collective-permute-start | bytes 49160 | tf_op jit(solution)/shard_map/ppermute | solution.py:233
  9.9 0.7 %convert_bitcast_fusion = f32[2]{0:T(128)S(1)} fusion(s32[1,2]{1,0:T(1,128)} %param.5), kind=kLoop, calls=%fused_computation.14 | loop fusion | flops 2 | bytes 16 | tf_op jit(solution)/shard_map/broadcast_in_dim | solution.py:217
  10.6 1.6 %collective-permute-done.4.refs_0_ = bf16[32,256]{1,0:T(8,128)(2,1)S(1)} collective-permute-done((bf16[32,256]{1,0:T(8,128)(2,1)S(1)}, bf16[32,256]{1,0:T(8,128)(2,1)S(1)}, u32[]{:S(2)}, u32[]{:S(2)}) %collective-permute-start.4) | collective-permute-done | bytes 16416 | tf_op jit(solution)/shard_map/ppermute | solution.py:233
  12.2 0.4 %collective-permute-start.5 = (bf16[96,256]{1,0:T(8,128)(2,1)S(1)}, bf16[96,256]{1,0:T(8,128)(2,1)S(1)}, u32[]{:S(2)}, u32[]{:S(2)}) collective-permute-start(bf16[96,256]{1,0:T(8,128)(2,1)S(1)} %shard_map.48.strip), channel_id=1, source_target_pairs={{0,16},{8,24},{16,0},{24,8},{1,17},{9,25},{17,1},{25,9},{2,18},{10... | collective-permute-start | bytes 147464 | tf_op jit(solution)/shard_map/ppermute | solution.py:203
  12.6 0.2 collective-permute-start.8
  12.8 3.5 %collective-permute-done.far = bf16[512,256]{1,0:T(8,128)(2,1)S(1)} collective-permute-done((bf16[512,256]{1,0:T(8,128)(2,1)}, bf16[512,256]{1,0:T(8,128)(2,1)S(1)}, u32[]{:S(2)}, u32[]{:S(2)}) %collective-permute-start) | collective-permute-done | bytes 262176 | tf_op jit(solution)/shard_map/ppermute | solution.py:203
  16.3 1.0 %collective-permute-start.1 = (bf16[512,256]{1,0:T(8,128)(2,1)S(1)}, bf16[512,256]{1,0:T(8,128)(2,1)S(1)}, u32[]{:S(2)}, u32[]{:S(2)}) collective-permute-start(bf16[512,256]{1,0:T(8,128)(2,1)S(1)} %collective-permute-done.far), channel_id=1, source_target_pairs={{0,8},{8,0},{16,24},{24,16},{1,9},{9,1},{17,25},{25,17},{2,10},{10... | collective-permute-start | bytes 786440 | tf_op jit(solution)/shard_map/ppermute | solution.py:203
  17.3 0.1 broadcast_in_dim.5.coords
  17.3 0.0 copy-start
  17.3 1.7 %copy-done = bf16[1,2,9,512,128]{4,3,2,1,0:T(8,128)(2,1)S(1)} copy-done((bf16[1,2,9,512,128]{4,3,2,1,0:T(8,128)(2,1)S(1)}, bf16[1,2,9,512,128]{4,3,2,1,0:T(8,128)(2,1)}, u32[]{:S(2)}) %copy-start) | copy-done | bytes 2359320
  19.0 0.0 copy-start.1
  19.0 0.9 %shard_map.49 = (f32[512,256]{1,0:T(8,128)S(1)}, f32[512,128]{1,0:T(8,128)S(1)}) custom-call(f32[2,256]{1,0:T(2,128)S(1)} %broadcast_in_dim.5.coords, bf16[512,256]{1,0:T(8,128)(2,1)S(1)} %get-tuple-element.22.own, f32[32,256]{1,0:T(8,128)S(1)} %add_sine_fusion.enc, bf16[96,256]{1,0:T(8,128)(2,1)S(1)} %shard_map.48.strip, bf16[2,9,512,128]{3,2,1,0:T(8,128)(2,1)S(1)} %bitcast.7), custom_call_target="tpu_custom_call" | custom-call | flops 5000000000 | bytes 4000000 | tf_op jit(solution)/shard_map/pallas_call | solution.py:185
  19.8 0.0 collective-permute-done.5.strip2
  19.9 1.1 %collective-permute-start.6 = (bf16[96,256]{1,0:T(8,128)(2,1)S(1)}, bf16[96,256]{1,0:T(8,128)(2,1)S(1)}, u32[]{:S(2)}, u32[]{:S(2)}) collective-permute-start(bf16[96,256]{1,0:T(8,128)(2,1)S(1)} %collective-permute-done.5.strip2), channel_id=1, source_target_pairs={{0,8},{8,0},{16,24},{24,16},{1,9},{9,1},{17,25},{25,17},{2,10},{10... | collective-permute-start | bytes 147464 | tf_op jit(solution)/shard_map/ppermute | solution.py:203
  21.0 0.0 collective-permute-done.8.strip1
  21.0 0.0 collective-permute-done.7.near
  21.0 0.0 copy-done.1
  21.0 1.8 %shard_map.50 = (f32[512,256]{1,0:T(8,128)S(1)}, f32[512,128]{1,0:T(8,128)S(1)}) custom-call(f32[2,256]{1,0:T(2,128)S(1)} %broadcast_in_dim.5.coords, bf16[512,256]{1,0:T(8,128)(2,1)S(1)} %collective-permute-done.7.near, bf16[512,256]{1,0:T(8,128)(2,1)S(1)} %collective-permute-done.far, f32[32,256]{1,0:T(8,128)S(1)} %add_sine_fusion.enc, ...), custom_call_target="tpu_custom_call" | custom-call | tf_op jit(solution)/shard_map/pallas_call | solution.py:185
  22.8 3.3 %collective-permute-done.6.strip = bf16[96,256]{1,0:T(8,128)(2,1)S(1)} collective-permute-done((bf16[96,256]{1,0:T(8,128)(2,1)S(1)}, bf16[96,256]{1,0:T(8,128)(2,1)S(1)}, u32[]{:S(2)}, u32[]{:S(2)}) %collective-permute-start.6) | collective-permute-done | bytes 49184 | tf_op jit(solution)/shard_map/ppermute | solution.py:203
  26.0 0.0 collective-permute-done.1.last
  26.1 1.7 %shard_map.51 = bf16[512,256]{1,0:T(8,128)(2,1)} custom-call(f32[2,256]{1,0:T(2,128)S(1)} %broadcast_in_dim.5.coords, bf16[512,256]{1,0:T(8,128)(2,1)S(1)} %collective-permute-done.1.last, f32[32,256]{1,0:T(8,128)S(1)} %add_sine_fusion.enc, bf16[96,256]{1,0:T(8,128)(2,1)S(1)} %collective-permute-done.6.strip, bf16[2,9,512,128]{3,2,1,0:T(8,128)(2,1)S(1)} %bitcast.9, ...), custom_call_target="tpu_custom_call" | custom-call | tf_op jit(solution)/shard_map/pallas_call | solution.py:185
  (4 shorter events, 0.1 us)
Async XLA Ops:
  0.0 16.3 %collective-permute-start = (bf16[512,256]{1,0:T(8,128)(2,1)}, bf16[512,256]{1,0:T(8,128)(2,1)S(1)}, u32[]{:S(2)}, u32[]{:S(2)}) collective-permute-start(bf16[512,256]{1,0:T(8,128)(2,1)} %bitcast.10), channel_id=1, source_target_pairs={{0,16},{8,24},{16,0},{24,8},{1,17},{9,25},{17,1},{25,9},{2,18},{10... | collective-permute-start | bytes 786440 | tf_op jit(solution)/shard_map/ppermute | solution.py:203
  4.0 16.9 %collective-permute-start.7 = (bf16[512,256]{1,0:T(8,128)(2,1)}, bf16[512,256]{1,0:T(8,128)(2,1)S(1)}, u32[]{:S(2)}, u32[]{:S(2)}) collective-permute-start(bf16[512,256]{1,0:T(8,128)(2,1)} %bitcast.11), channel_id=1, source_target_pairs={{0,8},{8,0},{16,24},{24,16},{1,9},{9,1},{17,25},{25,17},{2,10},{10... | collective-permute-start | bytes 786440 | tf_op jit(solution)/shard_map/ppermute | solution.py:203
  5.6 1.0 %copy-start.2 = (bf16[1,32,16,256]{3,2,1,0:T(8,128)(2,1)S(1)}, bf16[1,32,16,256]{3,2,1,0:T(8,128)(2,1)}, u32[]{:S(2)}) copy-start(bf16[1,32,16,256]{3,2,1,0:T(8,128)(2,1)} %param.4) | copy-start | bytes 786436
  6.7 1.6 %collective-permute-start.2 = (bf16[32,256]{1,0:T(8,128)(2,1)S(1)}, bf16[32,256]{1,0:T(8,128)(2,1)S(1)}, u32[]{:S(2)}, u32[]{:S(2)}) collective-permute-start(bf16[32,256]{1,0:T(8,128)(2,1)S(1)} %get-tuple-element.19), channel_id=1, source_target_pairs={{0,2},{4,6},{2,0},{6,4},{1,3},{5,7},{3,1},{7,5},{8,10},{12,14},{10... | collective-permute-start | bytes 49160 | tf_op jit(solution)/shard_map/ppermute | solution.py:222
  6.8 1.6 %collective-permute-start.3 = (bf16[32,256]{1,0:T(8,128)(2,1)S(1)}, bf16[32,256]{1,0:T(8,128)(2,1)S(1)}, u32[]{:S(2)}, u32[]{:S(2)}) collective-permute-start(bf16[32,256]{1,0:T(8,128)(2,1)S(1)} %get-tuple-element.20), channel_id=1, source_target_pairs={{2,4},{4,2},{3,5},{5,3},{10,12},{12,10},{11,13},{13,11},{18,20},{2... | collective-permute-start | bytes 49160 | tf_op jit(solution)/shard_map/ppermute | solution.py:222
  8.3 3.8 %collective-permute-start.4 = (bf16[32,256]{1,0:T(8,128)(2,1)S(1)}, bf16[32,256]{1,0:T(8,128)(2,1)S(1)}, u32[]{:S(2)}, u32[]{:S(2)}) collective-permute-start(bf16[32,256]{1,0:T(8,128)(2,1)S(1)} %shard_map.47), channel_id=1, source_target_pairs={{0,1},{1,0},{2,3},{3,2},{4,5},{5,4},{6,7},{7,6},{8,9},{9,8},{10,11... | collective-permute-start | bytes 49160 | tf_op jit(solution)/shard_map/ppermute | solution.py:233
  12.2 7.7 %collective-permute-start.5 = (bf16[96,256]{1,0:T(8,128)(2,1)S(1)}, bf16[96,256]{1,0:T(8,128)(2,1)S(1)}, u32[]{:S(2)}, u32[]{:S(2)}) collective-permute-start(bf16[96,256]{1,0:T(8,128)(2,1)S(1)} %shard_map.48.strip), channel_id=1, source_target_pairs={{0,16},{8,24},{16,0},{24,8},{1,17},{9,25},{17,1},{25,9},{2,18},{10... | collective-permute-start | bytes 147464 | tf_op jit(solution)/shard_map/ppermute | solution.py:203
  12.6 8.4 %collective-permute-start.8 = (bf16[96,256]{1,0:T(8,128)(2,1)S(1)}, bf16[96,256]{1,0:T(8,128)(2,1)S(1)}, u32[]{:S(2)}, u32[]{:S(2)}) collective-permute-start(bf16[96,256]{1,0:T(8,128)(2,1)S(1)} %shard_map.48.strip), channel_id=1, source_target_pairs={{0,8},{8,0},{16,24},{24,16},{1,9},{9,1},{17,25},{25,17},{2,10},{10... | collective-permute-start | bytes 147464 | tf_op jit(solution)/shard_map/ppermute | solution.py:203
  16.3 9.8 %collective-permute-start.1 = (bf16[512,256]{1,0:T(8,128)(2,1)S(1)}, bf16[512,256]{1,0:T(8,128)(2,1)S(1)}, u32[]{:S(2)}, u32[]{:S(2)}) collective-permute-start(bf16[512,256]{1,0:T(8,128)(2,1)S(1)} %collective-permute-done.far), channel_id=1, source_target_pairs={{0,8},{8,0},{16,24},{24,16},{1,9},{9,1},{17,25},{25,17},{2,10},{10... | collective-permute-start | bytes 786440 | tf_op jit(solution)/shard_map/ppermute | solution.py:203
  17.3 1.7 %copy-start = (bf16[1,2,9,512,128]{4,3,2,1,0:T(8,128)(2,1)S(1)}, bf16[1,2,9,512,128]{4,3,2,1,0:T(8,128)(2,1)}, u32[]{:S(2)}) copy-start(bf16[1,2,9,512,128]{4,3,2,1,0:T(8,128)(2,1)} %param.7) | copy-start | bytes 7077892
  19.0 2.0 %copy-start.1 = (bf16[1,2,9,512,128]{4,3,2,1,0:T(8,128)(2,1)S(1)}, bf16[1,2,9,512,128]{4,3,2,1,0:T(8,128)(2,1)}, u32[]{:S(2)}) copy-start(bf16[1,2,9,512,128]{4,3,2,1,0:T(8,128)(2,1)} %param.7) | copy-start | bytes 7077892
  19.9 6.2 %collective-permute-start.6 = (bf16[96,256]{1,0:T(8,128)(2,1)S(1)}, bf16[96,256]{1,0:T(8,128)(2,1)S(1)}, u32[]{:S(2)}, u32[]{:S(2)}) collective-permute-start(bf16[96,256]{1,0:T(8,128)(2,1)S(1)} %collective-permute-done.5.strip2), channel_id=1, source_target_pairs={{0,8},{8,0},{16,24},{24,16},{1,9},{9,1},{17,25},{25,17},{2,10},{10... | collective-permute-start | bytes 147464 | tf_op jit(solution)/shard_map/ppermute | solution.py:203

commit v4 on v3

--- a/solution.py
+++ b/solution.py
@@ -32,26 +32,41 @@
     return [(c, slice(c * LANES, (c + 1) * LANES)) for c in range(chan // LANES)]
 
 
-def columns_kernel(rows, cols, view, col_a, col_b, edge_rows, panel, wide):
-    even = lax.rem(lax.axis_index("shard"), 2) == 0
+def column(rows, cols, view, wide, pick_last):
     for c, lanes in tiles(view.shape[1]):
         wide[c] = view[:, lanes].astype(F32)
         first = wide[c, pl.ds(0, rows, stride=cols), :]
         last = wide[c, pl.ds(cols - 1, rows, stride=cols), :]
-        col_a[:, lanes] = jnp.where(even, last, first).astype(BF16)
-        col_b[:, lanes] = jnp.where(even, first, last).astype(BF16)
+        yield lanes, jnp.where(pick_last, last, first), jnp.where(pick_last, first, last)
+
+
+def columns_kernel(rows, cols, view, col_a, col_b, edge_rows, panel, wide):
+    even = lax.rem(lax.axis_index("shard"), 2) == 0
+    for lanes, a, b in column(rows, cols, view, wide, even):
+        col_a[:, lanes] = a.astype(BF16)
+        col_b[:, lanes] = b.astype(BF16)
     edge_rows[0:cols, :] = view[0:cols, :]
     edge_rows[cols : 2 * cols, :] = view[(rows - 1) * cols :, :]
     panel[...] = view[...]
 
 
-def sides(shards, got_a, got_b, enc):
+def inner_kernel(rows, cols, near, far, cols_a, wide):
+    even = lax.rem(lax.axis_index("shard"), 2) == 0
+    for i, view in enumerate((near, far)):
+        for lanes, a, _ in column(rows, cols, view, wide, even):
+            cols_a[i * rows : (i + 1) * rows, lanes] = a.astype(BF16)
+
+
+def pose(shards, raw, enc, is_a):
     me = lax.axis_index("shard")
-    even = lax.rem(me, 2) == 0
-    a, b = got_a[...].astype(F32) + enc[...], got_b[...].astype(F32) + enc[...]
-    left = jnp.where(me > 0, jnp.where(even, b, a), 0.0)
-    right = jnp.where(me < shards - 1, jnp.where(even, a, b), 0.0)
-    return left, right
+    is_left = (lax.rem(me, 2) == 0) != is_a
+    inside = jnp.where(is_left, me > 0, me < shards - 1)
+    return jnp.where(inside, raw[...].astype(F32) + enc[...], 0.0)
+
+
+def sides(a, b):
+    even = lax.rem(lax.axis_index("shard"), 2) == 0
+    return jnp.where(even, b, a), jnp.where(even, a, b)
 
 
 def corners(left, right, at):
@@ -60,7 +75,7 @@
 
 
 def edges_kernel(rows, cols, shards, pick, edge_rows, got_a, got_b, enc, *outs):
-    left, right = sides(shards, got_a, got_b, enc)
+    left, right = sides(pose(shards, got_a, enc, True), pose(shards, got_b, enc, False))
     lines = []
     for i, h in ((0, 0), (1, rows - 1)):
         row = edge_rows[i * cols : (i + 1) * cols, :].astype(F32) + enc[h : h + 1, :]
@@ -73,35 +88,40 @@
 
 
 def strip_kernel(rows, shards, got_a, got_b, enc, *refs):
-    out = refs[-1]
-    left, right = sides(shards, got_a, got_b, enc)
-    out[0:rows, :] = left.astype(BF16)
-    out[rows : 2 * rows, :] = right.astype(BF16)
-    at = 2 * rows
+    out, at = refs[-1], rows
+    out[0:rows, :] = pose(shards, got_b, enc, False).astype(BF16)
     for ref in refs[:-1]:
         out[at : at + ref.shape[0], :] = ref[...]
         at += ref.shape[0]
 
 
-def unfold(rows, cols, pick, view, enc, strip, wide, windows, base, weight, start):
+def relay_kernel(rows, strip, cols_a, out):
+    size = strip.shape[0]
+    out[0:size, :] = strip[...]
+    out[size:, :] = cols_a[rows:, :]
+
+
+def unfold(rows, cols, shards, pick, view, enc, strip, raw_a, wide, windows, base, weight, start):
     chan = view.shape[1]
     extra = cols + 16
-    before = strip[2 * rows : 2 * rows + extra, :].astype(F32)
+    size = extra if pick else 2 * extra
+    lines = strip[rows : rows + size, :].astype(F32)
     if pick:
         first = lax.axis_index(pick) == 0
-        zero = jnp.zeros_like(before)
-        before, after = jnp.where(first, zero, before), jnp.where(first, before, zero)
+        zero = jnp.zeros_like(lines)
+        before, after = jnp.where(first, zero, lines), jnp.where(first, lines, zero)
     else:
-        after = strip[2 * rows + extra : 2 * rows + 2 * extra, :].astype(F32)
+        before, after = lines[0:extra], lines[extra:]
+    posed_a = pose(shards, raw_a, enc, True).astype(BF16).astype(F32)
+    left_col, right_col = sides(posed_a, strip[0:rows, :].astype(F32))
     for c, lanes in tiles(chan):
         for h, edge in ((0, before), (rows + 1, after)):
             at = h * PITCH + 8
             wide[c, at : at + cols, :] = edge[0:cols, lanes]
             wide[c, at - 1 : at, :] = edge[cols : cols + 1, lanes]
             wide[c, at + cols : at + cols + 1, :] = edge[cols + 1 : cols + 2, lanes]
-        left, right = strip[0:rows, lanes].astype(F32), strip[rows : 2 * rows, lanes].astype(F32)
-        wide[c, pl.ds(PITCH + 7, rows, stride=PITCH), :] = left
-        wide[c, pl.ds(PITCH + 8 + cols, rows, stride=PITCH), :] = right
+        wide[c, pl.ds(PITCH + 7, rows, stride=PITCH), :] = left_col[:, lanes]
+        wide[c, pl.ds(PITCH + 8 + cols, rows, stride=PITCH), :] = right_col[:, lanes]
     for h in range(rows):
         here = slice(h * cols, (h + 1) * cols)
         posed = (view[here, :].astype(F32) + enc[h : h + 1, :]).astype(BF16).astype(F32)
@@ -123,54 +143,68 @@
     chan = windows.shape[1] // 3
     group = lax.div(view_index, 2)
     at = pl.multiple_of(lax.rem(view_index, 2) * chan, chan)
-    total = None
-    for a in range(3):
-        kernel = jnp.concatenate(
-            [weights[group, 3 * a + b, pl.ds(at, chan), :] for b in range(3)], axis=0
-        )
-        part = jnp.dot(
-            windows[a * cols : a * cols + pixels, :], kernel, preferred_element_type=F32
-        )
-        total = part if total is None else total + part
-    return total
+    width = weights.shape[3]
+    kernel = jnp.concatenate(
+        [
+            jnp.concatenate(
+                [weights[group, 3 * a + b, pl.ds(at, chan), :] for b in range(3)], axis=0
+            )
+            for a in range(3)
+        ],
+        axis=1,
+    )
+    taps = jnp.dot(windows[...], kernel, preferred_element_type=F32)
+    return (
+        taps[0:pixels, 0:width]
+        + taps[cols : cols + pixels, width : 2 * width]
+        + taps[2 * cols : 2 * cols + pixels, 2 * width :]
+    )
 
 
 def silu(x):
     return x / (1.0 + jnp.exp(-x))
 
 
-def own_kernel(rows, cols, pick, coords, own, enc, strip, weights, base, joined, wide, windows):
+def own_kernel(rows, cols, shards, pick, coords, own, enc, strip, got_a, weights, base, joined, wide,
+               windows):
     me = lax.axis_index("src")
-    unfold(rows, cols, pick, own, enc, strip, wide, windows, base, blend_weight(coords, me), True)
+    weight = blend_weight(coords, me)
+    unfold(rows, cols, shards, pick, own, enc, strip, got_a, wide, windows, base, weight, True)
     joined[...] = convolve(rows * cols, cols, windows, weights, me)
 
 
-def middle_kernel(rows, cols, pick, coords, near, far, enc, strip1, strip2, weights, base_in,
-                  joined_in, base, joined, wide, windows):
+def middle_kernel(rows, cols, shards, pick, coords, near, far, enc, near_strip, far_strip, cols_a,
+                  weights, base_in, joined_in, base, joined, wide, windows):
     me = lax.axis_index("src")
     pixels = rows * cols
     width = joined.shape[1]
     base[...] = base_in[...]
     sums = []
-    for k, view, strip in ((1, near, strip1), (2, far, strip2)):
+    views = (
+        (1, near, near_strip, cols_a.at[0:rows]),
+        (2, far, far_strip, cols_a.at[rows : 2 * rows]),
+    )
+    for k, view, strip, raw_a in views:
         index = jnp.bitwise_xor(me, k)
         weight = blend_weight(coords, index)
-        unfold(rows, cols, pick, view, enc, strip, wide, windows, base, weight, False)
+        unfold(rows, cols, shards, pick, view, enc, strip, raw_a, wide, windows, base, weight, False)
         sums.append(convolve(pixels, cols, windows, weights, index))
     joined[...] = sums[1]
     here = pl.ds(pl.multiple_of(lax.div(me, 2) * width, width), width)
     base[:, here] = base[:, here] + silu(joined_in[...] + sums[0])
 
 
-def late_kernel(rows, cols, pick, coords, last, enc, strip, weights, base_in, joined, out,
-                wide, windows, base):
+def late_kernel(rows, cols, shards, pick, coords, last, enc, strip, weights, base_in, joined, out, wide,
+                windows, base):
     me = lax.axis_index("src")
     pixels = rows * cols
     width = joined.shape[1]
     index = jnp.bitwise_xor(me, 3)
     base[...] = base_in[...]
     weight = blend_weight(coords, index)
-    unfold(rows, cols, pick, last, enc, strip, wide, windows, base, weight, False)
+    size = strip.shape[0] - rows
+    raw_a = strip.at[size:]
+    unfold(rows, cols, shards, pick, last, enc, strip.at[0:size], raw_a, wide, windows, base, weight, False)
     total = joined[...] + convolve(pixels, cols, windows, weights, index)
     here = pl.ds(pl.multiple_of(lax.div(index, 2) * width, width), width)
     base[:, here] = base[:, here] + silu(total)
@@ -207,11 +241,11 @@
     rowpos = offsets[0] + jnp.arange(rows, dtype=jnp.int32)
     enc = encoding(rowpos, chan)
 
-    column = shape(rows, chan)
+    line = shape(rows, chan)
     col_a, col_b, edge_rows, panel = call(
         functools.partial(columns_kernel, rows, cols),
         [own],
-        [column, column, shape(2 * cols, chan), shape(pixels, chan)],
+        [line, line, shape(2 * cols, chan), shape(pixels, chan)],
         [pltpu.VMEM((chan // LANES, pixels, LANES), F32)],
     )
     place = jnp.broadcast_to(coords.astype(F32).reshape(2, 1), (2, chan))
@@ -237,13 +271,12 @@
             lax.ppermute(edges[1], "slab", up),
             lax.ppermute(edges[0], "slab", [(j, i) for i, j in up]),
         ]
-    strip_rows = 2 * rows + len(beyond) * (cols + 16)
     strip = call(
         functools.partial(strip_kernel, rows, shards),
         [got_a, got_b, enc, *beyond],
-        [shape(strip_rows, chan)],
+        [shape(rows + len(beyond) * (cols + 16), chan)],
     )[0]
-    strip_near, strip_far = across(strip, 1), across(strip, 2)
+    near_strip, far_strip = across(strip, 1), across(strip, 2)
     far, panel = lax.optimization_barrier((far, panel))
     last = across(far, 1)
 
@@ -254,24 +287,36 @@
     sums = [shape(pixels, chan, F32), shape(pixels, width, F32)]
     cost = pl.CostEstimate(flops=5_000_000_000, bytes_accessed=4_000_000, transcendentals=0)
     base, joined = call(
-        functools.partial(own_kernel, rows, cols, pick),
-        [place, panel, enc, strip, weights[0]],
+        functools.partial(own_kernel, rows, cols, shards, pick),
+        [place, panel, enc, strip, got_a, weights[0]],
         sums,
         scratch,
         cost=cost,
     )
-    strip_far, base = lax.optimization_barrier((strip_far, base))
-    strip_last = across(strip_far, 1)
+    near, far, base, near_strip = lax.optimization_barrier((near, far, base, near_strip))
+    cols_a = call(
+        functools.partial(inner_kernel, rows, cols),
+        [near, far],
+        [shape(2 * rows, chan)],
+        [pltpu.VMEM((chan // LANES, pixels, LANES), F32)],
+    )[0]
+    cols_a = swap(cols_a, 0)
+    relayed = call(
+        functools.partial(relay_kernel, rows),
+        [far_strip, cols_a],
+        [shape(strip.shape[0] + rows, chan)],
+    )[0]
+    last_strip = across(relayed, 1)
     base, joined = call(
-        functools.partial(middle_kernel, rows, cols, pick),
-        [place, near, far, enc, strip_near, strip_far, weights[0], base, joined],
+        functools.partial(middle_kernel, rows, cols, shards, pick),
+        [place, near, far, enc, near_strip, far_strip, cols_a, weights[0], base, joined],
         sums,
         scratch,
         cost=pl.CostEstimate(flops=0, bytes_accessed=0, transcendentals=0),
     )
     out = call(
-        functools.partial(late_kernel, rows, cols, pick),
-        [place, last, enc, strip_last, weights[0], base, joined],
+        functools.partial(late_kernel, rows, cols, shards, pick),
+        [place, last, enc, last_strip, weights[0], base, joined],
         [shape(pixels, chan)],
         scratch + [pltpu.VMEM((pixels, chan), F32)],
     )[0]

time: 27.9 us -> 27.3 us (0.978)
  Pallas kernels: 4.42 us -> 3.82 us
    ppermute x6, waiting for transfers between devices: 6.79 us -> 5.59 us  [across(): return lax.ppermute(array, 'src', [(i, i ^ k) for i in range(4)])]
    ppermute x2 -> x3, waiting for transfers between devices: 0.01 us -> 1.06 us  [swap(): return lax.ppermute(array, 'shard', pairs + [(j, i) for i, j in pairs])]
    pallas_call x6 -> x8, Pallas kernels: 4.42 us -> 3.82 us  [call(): pl.pallas_call(kernel, out_shape=outs, in_specs=[VMEM_SPEC] * len(ins), o...]
    ppermute x2 -> x3, starting transfers between devices: 0.73 us -> 0.95 us  [swap(): return lax.ppermute(array, 'shard', pairs + [(j, i) for i, j in pairs])]
  transfers between devices with their start and end apart: 9 -> 10, of which waited for: 3 -> 4; matrix products, arithmetic and copies ran while one was open for 3% -> 3% of each run, Pallas kernels for 10% -> 9%
where the time goes in v4:
time: 27.3 us; the launch traced here: 27.1 us
  starting transfers between devices  10.7 us (39%)
  waiting for transfers between devices  8.25 us (30%)
  Pallas kernels  3.82 us (14%)
  local copies, waits for them, and re-layouts  2.72 us (10%)
  other arithmetic  0.86 us (3%)
  between operations  0.76 us (3%)
    ppermute x6, starting transfers between devices, across(): return lax.ppermute(array, 'src', [(i, i ^ k) for i in range(4)])  8.15 us
    ppermute x6, waiting for transfers between devices, across(): return lax.ppermute(array, 'src', [(i, i ^ k) for i in range(4)])  5.59 us
    pallas_call x8, Pallas kernels, call(): pl.pallas_call(kernel, out_shape=outs, in_specs=[VMEM_SPEC] * len(ins), o...  3.82 us
    unnamed x6, local copies, waits for them, and re-layouts  2.65 us
    ppermute x1, waiting for transfers between devices, local(): beyond = [lax.ppermute(edges[0], 'slab', [(0, 1), (1, 0)])]  1.59 us
    ppermute x1, starting transfers between devices, local(): beyond = [lax.ppermute(edges[0], 'slab', [(0, 1), (1, 0)])]  1.56 us
    ppermute x3, waiting for transfers between devices, swap(): return lax.ppermute(array, 'shard', pairs + [(j, i) for i, j in pairs])  1.06 us
    ppermute x3, starting transfers between devices, swap(): return lax.ppermute(array, 'shard', pairs + [(j, i) for i, j in pairs])  0.95 us
  transfers between devices with their start and end apart: 10, of which 4 were waited for; matrix products, arithmetic and copies ran while one was open for 3% of the time, Pallas kernels for 9%

profile of v4, /device:TPU:0, one launch (start us, length us, event | category | flops | bytes accessed | tf_op | source)
XLA Modules:
  0.0 27.1 jit_solution(3830508598065411259)
XLA Ops:
  0.0 4.0 %collective-permute-start = (bf16[512,256]{1,0:T(8,128)(2,1)}, bf16[512,256]{1,0:T(8,128)(2,1)S(1)}, u32[]{:S(2)}, u32[]{:S(2)}) collective-permute-start(bf16[512,256]{1,0:T(8,128)(2,1)} %bitcast.10), channel_id=1, source_target_pairs={{0,16},{8,24},{16,0},{24,8},{1,17},{9,25},{17,1},{25,9},{2,18},{10... | collective-permute-start | bytes 786440 | tf_op jit(solution)/shard_map/ppermute | solution.py:237
  4.0 1.6 %collective-permute-start.6 = (bf16[512,256]{1,0:T(8,128)(2,1)}, bf16[512,256]{1,0:T(8,128)(2,1)S(1)}, u32[]{:S(2)}, u32[]{:S(2)}) collective-permute-start(bf16[512,256]{1,0:T(8,128)(2,1)} %bitcast.11), channel_id=1, source_target_pairs={{0,8},{8,0},{16,24},{24,16},{1,9},{9,1},{17,25},{25,17},{2,10},{10... | collective-permute-start | bytes 786440 | tf_op jit(solution)/shard_map/ppermute | solution.py:237
  5.6 0.0 copy-start.2
  5.6 1.0 %copy-done.2 = bf16[1,32,16,256]{3,2,1,0:T(8,128)(2,1)S(1)} copy-done((bf16[1,32,16,256]{3,2,1,0:T(8,128)(2,1)S(1)}, bf16[1,32,16,256]{3,2,1,0:T(8,128)(2,1)}, u32[]{:S(2)}) %copy-start.2) | copy-done | bytes 262168
  6.6 0.1 shard_map.46
  6.7 0.1 collective-permute-start.2
  6.8 0.7 %collective-permute-start.3 = (bf16[32,256]{1,0:T(8,128)(2,1)S(1)}, bf16[32,256]{1,0:T(8,128)(2,1)S(1)}, u32[]{:S(2)}, u32[]{:S(2)}) collective-permute-start(bf16[32,256]{1,0:T(8,128)(2,1)S(1)} %get-tuple-element.22), channel_id=1, source_target_pairs={{2,4},{4,2},{3,5},{5,3},{10,12},{12,10},{11,13},{13,11},{18,20},{2... | collective-permute-start | bytes 49160 | tf_op jit(solution)/shard_map/ppermute | solution.py:256
  8.1 0.2 add_sine_fusion.enc
  8.3 0.0 collective-permute-done.2.got_a
  8.3 0.0 collective-permute-done.3.got_b
  8.4 1.6 %collective-permute-start.4 = (bf16[32,256]{1,0:T(8,128)(2,1)S(1)}, bf16[32,256]{1,0:T(8,128)(2,1)S(1)}, u32[]{:S(2)}, u32[]{:S(2)}) collective-permute-start(bf16[32,256]{1,0:T(8,128)(2,1)S(1)} %shard_map.47), channel_id=1, source_target_pairs={{0,1},{1,0},{2,3},{3,2},{4,5},{5,4},{6,7},{7,6},{8,9},{9,8},{10,11... | collective-permute-start | bytes 49160 | tf_op jit(solution)/shard_map/ppermute | solution.py:267
  9.9 0.7 %convert_bitcast_fusion = f32[2]{0:T(128)S(1)} fusion(s32[1,2]{1,0:T(1,128)} %param.5), kind=kLoop, calls=%fused_computation.14 | loop fusion | flops 2 | bytes 16 | tf_op jit(solution)/shard_map/broadcast_in_dim | solution.py:251
  10.6 1.6 %collective-permute-done.4.refs_0_ = bf16[32,256]{1,0:T(8,128)(2,1)S(1)} collective-permute-done((bf16[32,256]{1,0:T(8,128)(2,1)S(1)}, bf16[32,256]{1,0:T(8,128)(2,1)S(1)}, u32[]{:S(2)}, u32[]{:S(2)}) %collective-permute-start.4) | collective-permute-done | bytes 16416 | tf_op jit(solution)/shard_map/ppermute | solution.py:267
  12.2 0.5 %collective-permute-start.7 = (bf16[64,256]{1,0:T(8,128)(2,1)S(1)}, bf16[64,256]{1,0:T(8,128)(2,1)S(1)}, u32[]{:S(2)}, u32[]{:S(2)}) collective-permute-start(bf16[64,256]{1,0:T(8,128)(2,1)S(1)} %shard_map.48.strip), channel_id=1, source_target_pairs={{0,8},{8,0},{16,24},{24,16},{1,9},{9,1},{17,25},{25,17},{2,10},{10... | collective-permute-start | bytes 98312 | tf_op jit(solution)/shard_map/ppermute | solution.py:237
  12.7 0.0 collective-permute-start.5
  12.7 3.6 %collective-permute-done.far = bf16[512,256]{1,0:T(8,128)(2,1)S(1)} collective-permute-done((bf16[512,256]{1,0:T(8,128)(2,1)}, bf16[512,256]{1,0:T(8,128)(2,1)S(1)}, u32[]{:S(2)}, u32[]{:S(2)}) %collective-permute-start) | collective-permute-done | bytes 262176 | tf_op jit(solution)/shard_map/ppermute | solution.py:237
  16.3 0.8 %collective-permute-start.1 = (bf16[512,256]{1,0:T(8,128)(2,1)S(1)}, bf16[512,256]{1,0:T(8,128)(2,1)S(1)}, u32[]{:S(2)}, u32[]{:S(2)}) collective-permute-start(bf16[512,256]{1,0:T(8,128)(2,1)S(1)} %collective-permute-done.far), channel_id=1, source_target_pairs={{0,8},{8,0},{16,24},{24,16},{1,9},{9,1},{17,25},{25,17},{2,10},{10... | collective-permute-start | bytes 786440 | tf_op jit(solution)/shard_map/ppermute | solution.py:237
  17.0 0.1 broadcast_in_dim.5.coords
  17.1 0.0 copy-start
  17.1 1.7 %copy-done = bf16[1,2,9,512,128]{4,3,2,1,0:T(8,128)(2,1)S(1)} copy-done((bf16[1,2,9,512,128]{4,3,2,1,0:T(8,128)(2,1)S(1)}, bf16[1,2,9,512,128]{4,3,2,1,0:T(8,128)(2,1)}, u32[]{:S(2)}) %copy-start) | copy-done | bytes 2359320
  18.8 0.0 copy-start.1
  18.8 0.7 %shard_map.49 = (f32[512,256]{1,0:T(8,128)S(1)}, f32[512,128]{1,0:T(8,128)S(1)}) custom-call(f32[2,256]{1,0:T(2,128)S(1)} %broadcast_in_dim.5.coords, bf16[512,256]{1,0:T(8,128)(2,1)S(1)} %get-tuple-element.24.own, f32[32,256]{1,0:T(8,128)S(1)} %add_sine_fusion.enc, bf16[64,256]{1,0:T(8,128)(2,1)S(1)} %shard_map.48.strip, ...), custom_call_target="tpu_custom_call" | custom-call | flops 5000000000 | bytes 4000000 | tf_op jit(solution)/shard_map/pallas_call | solution.py:219
  19.5 0.0 collective-permute-done.7.near_strip
  19.5 0.0 collective-permute-done.6.near
  19.5 0.1 shard_map.50
  19.6 0.2 collective-permute-start.8
  19.8 0.0 collective-permute-done.5.strip.far_strip
  19.8 1.1 %collective-permute-done.8.cols_a = bf16[64,256]{1,0:T(8,128)(2,1)S(1)} collective-permute-done((bf16[64,256]{1,0:T(8,128)(2,1)S(1)}, bf16[64,256]{1,0:T(8,128)(2,1)S(1)}, u32[]{:S(2)}, u32[]{:S(2)}) %collective-permute-start.8) | collective-permute-done | bytes 32800 | tf_op jit(solution)/shard_map/ppermute | solution.py:256
  20.9 1.3 %collective-permute-start.9 = (bf16[96,256]{1,0:T(8,128)(2,1)S(1)}, bf16[96,256]{1,0:T(8,128)(2,1)S(1)}, u32[]{:S(2)}, u32[]{:S(2)}) collective-permute-start(bf16[96,256]{1,0:T(8,128)(2,1)S(1)} %shard_map.51), channel_id=1, source_target_pairs={{0,8},{8,0},{16,24},{24,16},{1,9},{9,1},{17,25},{25,17},{2,10},{10... | collective-permute-start | bytes 147464 | tf_op jit(solution)/shard_map/ppermute | solution.py:237
  22.1 0.0 copy-done.1
  22.1 1.5 %shard_map.52 = (f32[512,256]{1,0:T(8,128)S(1)}, f32[512,128]{1,0:T(8,128)S(1)}) custom-call(f32[2,256]{1,0:T(2,128)S(1)} %broadcast_in_dim.5.coords, bf16[512,256]{1,0:T(8,128)(2,1)S(1)} %collective-permute-done.6.near, bf16[512,256]{1,0:T(8,128)(2,1)S(1)} %collective-permute-done.far, f32[32,256]{1,0:T(8,128)S(1)} %add_sine_fusion.enc, ...), custom_call_target="tpu_custom_call" | custom-call | tf_op jit(solution)/shard_map/pallas_call | solution.py:219
  23.6 2.0 %collective-permute-done.9.strip = bf16[96,256]{1,0:T(8,128)(2,1)S(1)} collective-permute-done((bf16[96,256]{1,0:T(8,128)(2,1)S(1)}, bf16[96,256]{1,0:T(8,128)(2,1)S(1)}, u32[]{:S(2)}, u32[]{:S(2)}) %collective-permute-start.9) | collective-permute-done | bytes 49184 | tf_op jit(solution)/shard_map/ppermute | solution.py:237
  25.6 0.0 collective-permute-done.1.last
  25.6 1.4 %shard_map.53 = bf16[512,256]{1,0:T(8,128)(2,1)} custom-call(f32[2,256]{1,0:T(2,128)S(1)} %broadcast_in_dim.5.coords, bf16[512,256]{1,0:T(8,128)(2,1)S(1)} %collective-permute-done.1.last, f32[32,256]{1,0:T(8,128)S(1)} %add_sine_fusion.enc, bf16[96,256]{1,0:T(8,128)(2,1)S(1)} %collective-permute-done.9.strip, bf16[2,9,512,128]{3,2,1,0:T(8,128)(2,1)S(1)} %bitcast.9, ...), custom_call_target="tpu_custom_call" | custom-call | tf_op jit(solution)/shard_map/pallas_call | solution.py:219
  (5 shorter events, 0.1 us)
Async XLA Ops:
  0.0 16.3 %collective-permute-start = (bf16[512,256]{1,0:T(8,128)(2,1)}, bf16[512,256]{1,0:T(8,128)(2,1)S(1)}, u32[]{:S(2)}, u32[]{:S(2)}) collective-permute-start(bf16[512,256]{1,0:T(8,128)(2,1)} %bitcast.10), channel_id=1, source_target_pairs={{0,16},{8,24},{16,0},{24,8},{1,17},{9,25},{17,1},{25,9},{2,18},{10... | collective-permute-start | bytes 786440 | tf_op jit(solution)/shard_map/ppermute | solution.py:237
  4.0 15.4 %collective-permute-start.6 = (bf16[512,256]{1,0:T(8,128)(2,1)}, bf16[512,256]{1,0:T(8,128)(2,1)S(1)}, u32[]{:S(2)}, u32[]{:S(2)}) collective-permute-start(bf16[512,256]{1,0:T(8,128)(2,1)} %bitcast.11), channel_id=1, source_target_pairs={{0,8},{8,0},{16,24},{24,16},{1,9},{9,1},{17,25},{25,17},{2,10},{10... | collective-permute-start | bytes 786440 | tf_op jit(solution)/shard_map/ppermute | solution.py:237
  5.6 1.0 %copy-start.2 = (bf16[1,32,16,256]{3,2,1,0:T(8,128)(2,1)S(1)}, bf16[1,32,16,256]{3,2,1,0:T(8,128)(2,1)}, u32[]{:S(2)}) copy-start(bf16[1,32,16,256]{3,2,1,0:T(8,128)(2,1)} %param.4) | copy-start | bytes 786436
  6.7 1.6 %collective-permute-start.2 = (bf16[32,256]{1,0:T(8,128)(2,1)S(1)}, bf16[32,256]{1,0:T(8,128)(2,1)S(1)}, u32[]{:S(2)}, u32[]{:S(2)}) collective-permute-start(bf16[32,256]{1,0:T(8,128)(2,1)S(1)} %get-tuple-element.21), channel_id=1, source_target_pairs={{0,2},{4,6},{2,0},{6,4},{1,3},{5,7},{3,1},{7,5},{8,10},{12,14},{10... | collective-permute-start | bytes 49160 | tf_op jit(solution)/shard_map/ppermute | solution.py:256
  6.8 1.6 %collective-permute-start.3 = (bf16[32,256]{1,0:T(8,128)(2,1)S(1)}, bf16[32,256]{1,0:T(8,128)(2,1)S(1)}, u32[]{:S(2)}, u32[]{:S(2)}) collective-permute-start(bf16[32,256]{1,0:T(8,128)(2,1)S(1)} %get-tuple-element.22), channel_id=1, source_target_pairs={{2,4},{4,2},{3,5},{5,3},{10,12},{12,10},{11,13},{13,11},{18,20},{2... | collective-permute-start | bytes 49160 | tf_op jit(solution)/shard_map/ppermute | solution.py:256
  8.4 3.8 %collective-permute-start.4 = (bf16[32,256]{1,0:T(8,128)(2,1)S(1)}, bf16[32,256]{1,0:T(8,128)(2,1)S(1)}, u32[]{:S(2)}, u32[]{:S(2)}) collective-permute-start(bf16[32,256]{1,0:T(8,128)(2,1)S(1)} %shard_map.47), channel_id=1, source_target_pairs={{0,1},{1,0},{2,3},{3,2},{4,5},{5,4},{6,7},{7,6},{8,9},{9,8},{10,11... | collective-permute-start | bytes 49160 | tf_op jit(solution)/shard_map/ppermute | solution.py:267
  12.2 7.3 %collective-permute-start.7 = (bf16[64,256]{1,0:T(8,128)(2,1)S(1)}, bf16[64,256]{1,0:T(8,128)(2,1)S(1)}, u32[]{:S(2)}, u32[]{:S(2)}) collective-permute-start(bf16[64,256]{1,0:T(8,128)(2,1)S(1)} %shard_map.48.strip), channel_id=1, source_target_pairs={{0,8},{8,0},{16,24},{24,16},{1,9},{9,1},{17,25},{25,17},{2,10},{10... | collective-permute-start | bytes 98312 | tf_op jit(solution)/shard_map/ppermute | solution.py:237
  12.7 7.1 %collective-permute-start.5 = (bf16[64,256]{1,0:T(8,128)(2,1)S(1)}, bf16[64,256]{1,0:T(8,128)(2,1)S(1)}, u32[]{:S(2)}, u32[]{:S(2)}) collective-permute-start(bf16[64,256]{1,0:T(8,128)(2,1)S(1)} %shard_map.48.strip), channel_id=1, source_target_pairs={{0,16},{8,24},{16,0},{24,8},{1,17},{9,25},{17,1},{25,9},{2,18},{10... | collective-permute-start | bytes 98312 | tf_op jit(solution)/shard_map/ppermute | solution.py:237
  16.3 9.3 %collective-permute-start.1 = (bf16[512,256]{1,0:T(8,128)(2,1)S(1)}, bf16[512,256]{1,0:T(8,128)(2,1)S(1)}, u32[]{:S(2)}, u32[]{:S(2)}) collective-permute-start(bf16[512,256]{1,0:T(8,128)(2,1)S(1)} %collective-permute-done.far), channel_id=1, source_target_pairs={{0,8},{8,0},{16,24},{24,16},{1,9},{9,1},{17,25},{25,17},{2,10},{10... | collective-permute-start | bytes 786440 | tf_op jit(solution)/shard_map/ppermute | solution.py:237
  17.1 1.7 %copy-start = (bf16[1,2,9,512,128]{4,3,2,1,0:T(8,128)(2,1)S(1)}, bf16[1,2,9,512,128]{4,3,2,1,0:T(8,128)(2,1)}, u32[]{:S(2)}) copy-start(bf16[1,2,9,512,128]{4,3,2,1,0:T(8,128)(2,1)} %param.7) | copy-start | bytes 7077892
  18.8 3.4 %copy-start.1 = (bf16[1,2,9,512,128]{4,3,2,1,0:T(8,128)(2,1)S(1)}, bf16[1,2,9,512,128]{4,3,2,1,0:T(8,128)(2,1)}, u32[]{:S(2)}) copy-start(bf16[1,2,9,512,128]{4,3,2,1,0:T(8,128)(2,1)} %param.7) | copy-start | bytes 7077892
  19.6 1.3 %collective-permute-start.8 = (bf16[64,256]{1,0:T(8,128)(2,1)S(1)}, bf16[64,256]{1,0:T(8,128)(2,1)S(1)}, u32[]{:S(2)}, u32[]{:S(2)}) collective-permute-start(bf16[64,256]{1,0:T(8,128)(2,1)S(1)} %shard_map.50), channel_id=1, source_target_pairs={{0,2},{4,6},{2,0},{6,4},{1,3},{5,7},{3,1},{7,5},{8,10},{12,14},{10... | collective-permute-start | bytes 98312 | tf_op jit(solution)/shard_map/ppermute | solution.py:256
  20.9 4.7 %collective-permute-start.9 = (bf16[96,256]{1,0:T(8,128)(2,1)S(1)}, bf16[96,256]{1,0:T(8,128)(2,1)S(1)}, u32[]{:S(2)}, u32[]{:S(2)}) collective-permute-start(bf16[96,256]{1,0:T(8,128)(2,1)S(1)} %shard_map.51), channel_id=1, source_target_pairs={{0,8},{8,0},{16,24},{24,16},{1,9},{9,1},{17,25},{25,17},{2,10},{10... | collective-permute-start | bytes 147464 | tf_op jit(solution)/shard_map/ppermute | solution.py:237

commit v5 on v4

--- a/solution.py
+++ b/solution.py
@@ -101,8 +101,7 @@
     out[size:, :] = cols_a[rows:, :]
 
 
-def unfold(rows, cols, shards, pick, view, enc, strip, raw_a, wide, windows, base, weight, start):
-    chan = view.shape[1]
+def halo(rows, cols, shards, pick, enc, strip, raw_a):
     extra = cols + 16
     size = extra if pick else 2 * extra
     lines = strip[rows : rows + size, :].astype(F32)
@@ -113,15 +112,21 @@
     else:
         before, after = lines[0:extra], lines[extra:]
     posed_a = pose(shards, raw_a, enc, True).astype(BF16).astype(F32)
-    left_col, right_col = sides(posed_a, strip[0:rows, :].astype(F32))
+    left, right = sides(posed_a, strip[0:rows, :].astype(F32))
+    return left, right, before, after
+
+
+def unfold(rows, cols, view, enc, edges, wide, windows, base, weight, start):
+    chan = view.shape[1]
+    left, right, before, after = edges
     for c, lanes in tiles(chan):
         for h, edge in ((0, before), (rows + 1, after)):
             at = h * PITCH + 8
             wide[c, at : at + cols, :] = edge[0:cols, lanes]
             wide[c, at - 1 : at, :] = edge[cols : cols + 1, lanes]
             wide[c, at + cols : at + cols + 1, :] = edge[cols + 1 : cols + 2, lanes]
-        wide[c, pl.ds(PITCH + 7, rows, stride=PITCH), :] = left_col[:, lanes]
-        wide[c, pl.ds(PITCH + 8 + cols, rows, stride=PITCH), :] = right_col[:, lanes]
+        wide[c, pl.ds(PITCH + 7, rows, stride=PITCH), :] = left[:, lanes]
+        wide[c, pl.ds(PITCH + 8 + cols, rows, stride=PITCH), :] = right[:, lanes]
     for h in range(rows):
         here = slice(h * cols, (h + 1) * cols)
         posed = (view[here, :].astype(F32) + enc[h : h + 1, :]).astype(BF16).astype(F32)
@@ -129,7 +134,7 @@
         for c, lanes in tiles(chan):
             wide[c, at : at + cols, :] = posed[:, lanes]
         part = weight * posed
-        base[here, :] = part if start else base[here, :] + part
+        base[here, :] = part if start is True else (base if start is None else start)[here, :] + part
     for h in range(rows + 2):
         at = h * PITCH + 7
         here = slice(h * cols, (h + 1) * cols)
@@ -139,12 +144,8 @@
                 windows[here, to : to + LANES] = wide[c, at + b : at + b + cols, :].astype(BF16)
 
 
-def convolve(pixels, cols, windows, weights, view_index):
-    chan = windows.shape[1] // 3
-    group = lax.div(view_index, 2)
-    at = pl.multiple_of(lax.rem(view_index, 2) * chan, chan)
-    width = weights.shape[3]
-    kernel = jnp.concatenate(
+def kernel_of(weights, group, at, chan):
+    return jnp.concatenate(
         [
             jnp.concatenate(
                 [weights[group, 3 * a + b, pl.ds(at, chan), :] for b in range(3)], axis=0
@@ -153,7 +154,16 @@
         ],
         axis=1,
     )
-    taps = jnp.dot(windows[...], kernel, preferred_element_type=F32)
+
+
+def convolve(pixels, cols, windows, weights, view_index):
+    chan = windows.shape[1] // 3
+    group = lax.div(view_index, 2)
+    at = pl.multiple_of(lax.rem(view_index, 2) * chan, chan)
+    width = weights.shape[3]
+    taps = jnp.dot(
+        windows[...], kernel_of(weights, group, at, chan), preferred_element_type=F32
+    )
     return (
         taps[0:pixels, 0:width]
         + taps[cols : cols + pixels, width : 2 * width]
@@ -168,47 +178,110 @@
 def own_kernel(rows, cols, shards, pick, coords, own, enc, strip, got_a, weights, base, joined, wide,
                windows):
     me = lax.axis_index("src")
-    weight = blend_weight(coords, me)
-    unfold(rows, cols, shards, pick, own, enc, strip, got_a, wide, windows, base, weight, True)
+    edges = halo(rows, cols, shards, pick, enc, strip, got_a)
+    unfold(rows, cols, own, enc, edges, wide, windows, base, blend_weight(coords, me), True)
     joined[...] = convolve(rows * cols, cols, windows, weights, me)
 
 
 def middle_kernel(rows, cols, shards, pick, coords, near, far, enc, near_strip, far_strip, cols_a,
                   weights, base_in, joined_in, base, joined, wide, windows):
     me = lax.axis_index("src")
-    pixels = rows * cols
     width = joined.shape[1]
-    base[...] = base_in[...]
     sums = []
     views = (
-        (1, near, near_strip, cols_a.at[0:rows]),
-        (2, far, far_strip, cols_a.at[rows : 2 * rows]),
-    )
-    for k, view, strip, raw_a in views:
+        (1, near, near_strip, cols_a.at[0:rows], base_in),
+        (2, far, far_strip, cols_a.at[rows : 2 * rows], None),
+    )
+    for k, view, strip, raw_a, start in views:
         index = jnp.bitwise_xor(me, k)
+        edges = halo(rows, cols, shards, pick, enc, strip, raw_a)
         weight = blend_weight(coords, index)
-        unfold(rows, cols, shards, pick, view, enc, strip, raw_a, wide, windows, base, weight, False)
-        sums.append(convolve(pixels, cols, windows, weights, index))
+        unfold(rows, cols, view, enc, edges, wide, windows, base, weight, start)
+        sums.append(convolve(rows * cols, cols, windows, weights, index))
     joined[...] = sums[1]
     here = pl.ds(pl.multiple_of(lax.div(me, 2) * width, width), width)
     base[:, here] = base[:, here] + silu(joined_in[...] + sums[0])
 
 
-def late_kernel(rows, cols, shards, pick, coords, last, enc, strip, weights, base_in, joined, out, wide,
-                windows, base):
-    me = lax.axis_index("src")
-    pixels = rows * cols
-    width = joined.shape[1]
-    index = jnp.bitwise_xor(me, 3)
-    base[...] = base_in[...]
+def inside_kernel(rows, cols, top, coords, part, enc, weights, base_in, joined_in, base, joined, wide,
+                  windows):
+    index = jnp.bitwise_xor(lax.axis_index("src"), 3)
     weight = blend_weight(coords, index)
+    chan, width = base.shape[1], joined.shape[1]
+    count = part.shape[0] // cols
+    column = jnp.zeros((count, LANES), F32)
+    for c in range(chan // LANES):
+        wide[c, pl.ds(PITCH + 7, count, stride=PITCH), :] = column
+        wide[c, pl.ds(PITCH + 8 + cols, count, stride=PITCH), :] = column
+    for h in range(count):
+        here = slice(h * cols, (h + 1) * cols)
+        line = enc[top + h : top + h + 1, :]
+        posed = (part[here, :].astype(F32) + line).astype(BF16).astype(F32)
+        at = (h + 1) * PITCH + 8
+        for c, lanes in tiles(chan):
+            wide[c, at : at + cols, :] = posed[:, lanes]
+        base[here, :] = base_in[(top + h) * cols : (top + h + 1) * cols, :] + weight * posed
+        for b in range(3):
+            for c in range(chan // LANES):
+                to = b * chan + c * LANES
+                windows[here, to : to + LANES] = wide[c, at - 1 + b : at - 1 + b + cols, :].astype(BF16)
+    group = lax.div(index, 2)
+    at = pl.multiple_of(lax.rem(index, 2) * chan, chan)
+    taps = jnp.dot(
+        windows[0 : count * cols, :], kernel_of(weights, group, at, chan), preferred_element_type=F32
+    )
+    joined[...] = joined_in[...]
+    for a in range(3):
+        first, last = max(top + 1 - a, 0), min(top + 1 - a + count, rows)
+        skip = (first - (top + 1 - a)) * cols
+        size = (last - first) * cols
+        joined[first * cols : last * cols, :] += taps[
+            skip : skip + size, a * width : (a + 1) * width
+        ]
+
+
+def rim_kernel(rows, cols, shards, pick, enc, strip, weights, joined_in, *refs):
+    index = jnp.bitwise_xor(lax.axis_index("src"), 3)
+    *bases, out, joined = refs
+    chan, width = out.shape[1], joined.shape[1]
+    group = lax.div(index, 2)
+    at = pl.multiple_of(lax.rem(index, 2) * chan, chan)
+
+    def taps(pairs):
+        return jnp.concatenate([weights[group, 3 * a + b, pl.ds(at, chan), :] for a, b in pairs], axis=0)
+
+    joined[...] = joined_in[...]
     size = strip.shape[0] - rows
-    raw_a = strip.at[size:]
-    unfold(rows, cols, shards, pick, last, enc, strip.at[0:size], raw_a, wide, windows, base, weight, False)
-    total = joined[...] + convolve(pixels, cols, windows, weights, index)
-    here = pl.ds(pl.multiple_of(lax.div(index, 2) * width, width), width)
-    base[:, here] = base[:, here] + silu(total)
-    out[...] = base[...].astype(BF16)
+    left, right, before, after = halo(
+        rows, cols, shards, pick, enc, strip.at[0:size], strip.at[size:]
+    )
+    for column, corner, b in ((left, 0, 0), (right, 1, 2)):
+        above, below = (line[cols + corner : cols + corner + 1] for line in (before, after))
+        tall = jnp.concatenate([above, column, below], axis=0)
+        wide = jnp.concatenate([tall[a : a + rows] for a in range(3)], axis=1).astype(BF16)
+        kernel = taps([(a, b) for a in range(3)])
+        where = pl.ds(b // 2 * (cols - 1), rows, stride=cols)
+        joined[where, :] += jnp.dot(wide, kernel, preferred_element_type=F32)
+    if pick:
+        first = lax.axis_index(pick) == 0
+        lines = [(before + after, jnp.where(first, rows - 1, 0), jnp.where(first, 2, 0))]
+    else:
+        lines = [(before, 0, 0), (after, rows - 1, 2)]
+    for line, h, a in lines:
+        zero = jnp.zeros((1, chan), F32)
+        tall = jnp.concatenate([zero, line[0:cols], zero], axis=0)
+        wide = jnp.concatenate([tall[b : b + cols] for b in range(3)], axis=1).astype(BF16)
+        where = pl.ds(pl.multiple_of(h * cols, cols), cols)
+        kernel = taps([(a, b) for b in range(3)])
+        joined[where, :] += jnp.dot(wide, kernel, preferred_element_type=F32)
+    added, at = silu(joined[...]), 0
+    for base in bases:
+        size = base.shape[0]
+        for c, lanes in tiles(chan):
+            here = group == c * LANES // width
+            more = jnp.where(here, added[at : at + size], 0.0)
+            out[at : at + size, lanes] = (base[:, lanes] + more).astype(BF16)
+        at += size
 
 
 def shape(rows, chan, dtype=BF16):
@@ -278,7 +351,7 @@
     )[0]
     near_strip, far_strip = across(strip, 1), across(strip, 2)
     far, panel = lax.optimization_barrier((far, panel))
-    last = across(far, 1)
+    parts = [(0, across(far, 1))]
 
     scratch = [
         pltpu.VMEM((chan // LANES, (rows + 2) * PITCH + 8, LANES), F32),
@@ -314,11 +387,21 @@
         scratch,
         cost=pl.CostEstimate(flops=0, bytes_accessed=0, transcendentals=0),
     )
+    bases = []
+    for top, part in parts:
+        done, joined = call(
+            functools.partial(inside_kernel, rows, cols, top),
+            [place, part, enc, weights[0], base, joined],
+            [shape(part.shape[0], chan, F32), shape(pixels, width, F32)],
+            scratch,
+            cost=pl.CostEstimate(flops=0, bytes_accessed=0, transcendentals=0),
+        )
+        bases.append(done)
     out = call(
-        functools.partial(late_kernel, rows, cols, shards, pick),
-        [place, last, enc, last_strip, weights[0], base, joined],
+        functools.partial(rim_kernel, rows, cols, shards, pick),
+        [enc, last_strip, weights[0], joined, *bases],
         [shape(pixels, chan)],
-        scratch + [pltpu.VMEM((pixels, chan), F32)],
+        [pltpu.VMEM((pixels, width), F32)],
     )[0]
     return out.reshape(1, rows, cols, chan)
 

time: 27.3 us -> 27 us (0.989)
  waiting for transfers between devices: 8.25 us -> 7.75 us
    ppermute x6, waiting for transfers between devices: 5.59 us -> 5.1 us  [across(): return lax.ppermute(array, 'src', [(i, i ^ k) for i in range(4)])]
    pallas_call x8 -> x9, Pallas kernels: 3.82 us -> 4.02 us  [call(): pl.pallas_call(kernel, out_shape=outs, in_specs=[VMEM_SPEC] * len(ins), o...]
  transfers between devices with their start and end apart: 10 -> 10, of which waited for: 4 -> 4; matrix products, arithmetic and copies ran while one was open for 3% -> 3% of each run, Pallas kernels for 9% -> 11%
where the time goes in v5:
time: 27 us; the launch traced here: 26.8 us
  starting transfers between devices  10.7 us (40%)
  waiting for transfers between devices  7.75 us (29%)
  Pallas kernels  4.02 us (15%)
  local copies, waits for them, and re-layouts  2.72 us (10%)
  other arithmetic  0.86 us (3%)
  between operations  0.77 us (3%)
    ppermute x6, starting transfers between devices, across(): return lax.ppermute(array, 'src', [(i, i ^ k) for i in range(4)])  8.16 us
    ppermute x6, waiting for transfers between devices, across(): return lax.ppermute(array, 'src', [(i, i ^ k) for i in range(4)])  5.1 us
    pallas_call x9, Pallas kernels, call(): pl.pallas_call(kernel, out_shape=outs, in_specs=[VMEM_SPEC] * len(ins), o...  4.02 us
    unnamed x6, local copies, waits for them, and re-layouts  2.65 us
    ppermute x1, waiting for transfers between devices, local(): beyond = [lax.ppermute(edges[0], 'slab', [(0, 1), (1, 0)])]  1.59 us
    ppermute x1, starting transfers between devices, local(): beyond = [lax.ppermute(edges[0], 'slab', [(0, 1), (1, 0)])]  1.56 us
    ppermute x3, waiting for transfers between devices, swap(): return lax.ppermute(array, 'shard', pairs + [(j, i) for i, j in pairs])  1.06 us
    ppermute x3, starting transfers between devices, swap(): return lax.ppermute(array, 'shard', pairs + [(j, i) for i, j in pairs])  0.95 us
  transfers between devices with their start and end apart: 10, of which 4 were waited for; matrix products, arithmetic and copies ran while one was open for 3% of the time, Pallas kernels for 11%

profile of v5, /device:TPU:0, one launch (start us, length us, event | category | flops | bytes accessed | tf_op | source)
XLA Modules:
  0.0 26.8 jit_solution(9455194180534479164)
XLA Ops:
  0.0 4.0 %collective-permute-start.5 = (bf16[512,256]{1,0:T(8,128)(2,1)}, bf16[512,256]{1,0:T(8,128)(2,1)S(1)}, u32[]{:S(2)}, u32[]{:S(2)}) collective-permute-start(bf16[512,256]{1,0:T(8,128)(2,1)} %bitcast.11), channel_id=1, source_target_pairs={{0,16},{8,24},{16,0},{24,8},{1,17},{9,25},{17,1},{25,9},{2,18},{10... | collective-permute-start | bytes 786440 | tf_op jit(solution)/shard_map/ppermute | solution.py:310
  4.0 1.6 %collective-permute-start.4 = (bf16[512,256]{1,0:T(8,128)(2,1)}, bf16[512,256]{1,0:T(8,128)(2,1)S(1)}, u32[]{:S(2)}, u32[]{:S(2)}) collective-permute-start(bf16[512,256]{1,0:T(8,128)(2,1)} %bitcast.12), channel_id=1, source_target_pairs={{0,8},{8,0},{16,24},{24,16},{1,9},{9,1},{17,25},{25,17},{2,10},{10... | collective-permute-start | bytes 786440 | tf_op jit(solution)/shard_map/ppermute | solution.py:310
  5.6 0.0 copy-start.2
  5.6 1.0 %copy-done.2 = bf16[1,32,16,256]{3,2,1,0:T(8,128)(2,1)S(1)} copy-done((bf16[1,32,16,256]{3,2,1,0:T(8,128)(2,1)S(1)}, bf16[1,32,16,256]{3,2,1,0:T(8,128)(2,1)}, u32[]{:S(2)}) %copy-start.2) | copy-done | bytes 262168
  6.6 0.1 shard_map.46
  6.7 0.1 collective-permute-start
  6.8 0.7 %collective-permute-start.1 = (bf16[32,256]{1,0:T(8,128)(2,1)S(1)}, bf16[32,256]{1,0:T(8,128)(2,1)S(1)}, u32[]{:S(2)}, u32[]{:S(2)}) collective-permute-start(bf16[32,256]{1,0:T(8,128)(2,1)S(1)} %get-tuple-element.22), channel_id=1, source_target_pairs={{2,4},{4,2},{3,5},{5,3},{10,12},{12,10},{11,13},{13,11},{18,20},{2... | collective-permute-start | bytes 49160 | tf_op jit(solution)/shard_map/ppermute | solution.py:329
  8.1 0.2 add_sine_fusion.enc
  8.3 0.0 collective-permute-done.got_a
  8.3 0.0 collective-permute-done.1.got_b
  8.4 1.6 %collective-permute-start.2 = (bf16[32,256]{1,0:T(8,128)(2,1)S(1)}, bf16[32,256]{1,0:T(8,128)(2,1)S(1)}, u32[]{:S(2)}, u32[]{:S(2)}) collective-permute-start(bf16[32,256]{1,0:T(8,128)(2,1)S(1)} %shard_map.47), channel_id=1, source_target_pairs={{0,1},{1,0},{2,3},{3,2},{4,5},{5,4},{6,7},{7,6},{8,9},{9,8},{10,11... | collective-permute-start | bytes 49160 | tf_op jit(solution)/shard_map/ppermute | solution.py:340
  9.9 0.7 %convert_bitcast_fusion = f32[2]{0:T(128)S(1)} fusion(s32[1,2]{1,0:T(1,128)} %param.5), kind=kLoop, calls=%fused_computation.13 | loop fusion | flops 2 | bytes 16 | tf_op jit(solution)/shard_map/broadcast_in_dim | solution.py:324
  10.6 1.6 %collective-permute-done.2.refs_0_ = bf16[32,256]{1,0:T(8,128)(2,1)S(1)} collective-permute-done((bf16[32,256]{1,0:T(8,128)(2,1)S(1)}, bf16[32,256]{1,0:T(8,128)(2,1)S(1)}, u32[]{:S(2)}, u32[]{:S(2)}) %collective-permute-start.2) | collective-permute-done | bytes 16416 | tf_op jit(solution)/shard_map/ppermute | solution.py:340
  12.2 0.5 %collective-permute-start.6 = (bf16[64,256]{1,0:T(8,128)(2,1)S(1)}, bf16[64,256]{1,0:T(8,128)(2,1)S(1)}, u32[]{:S(2)}, u32[]{:S(2)}) collective-permute-start(bf16[64,256]{1,0:T(8,128)(2,1)S(1)} %shard_map.48.strip), channel_id=1, source_target_pairs={{0,8},{8,0},{16,24},{24,16},{1,9},{9,1},{17,25},{25,17},{2,10},{10... | collective-permute-start | bytes 98312 | tf_op jit(solution)/shard_map/ppermute | solution.py:310
  12.7 0.0 collective-permute-start.3
  12.7 3.6 %collective-permute-done.5.far = bf16[512,256]{1,0:T(8,128)(2,1)S(1)} collective-permute-done((bf16[512,256]{1,0:T(8,128)(2,1)}, bf16[512,256]{1,0:T(8,128)(2,1)S(1)}, u32[]{:S(2)}, u32[]{:S(2)}) %collective-permute-start.5) | collective-permute-done | bytes 262176 | tf_op jit(solution)/shard_map/ppermute | solution.py:310
  16.3 0.8 %collective-permute-start.9 = (bf16[512,256]{1,0:T(8,128)(2,1)S(1)}, bf16[512,256]{1,0:T(8,128)(2,1)S(1)}, u32[]{:S(2)}, u32[]{:S(2)}) collective-permute-start(bf16[512,256]{1,0:T(8,128)(2,1)S(1)} %collective-permute-done.5.far), channel_id=1, source_target_pairs={{0,8},{8,0},{16,24},{24,16},{1,9},{9,1},{17,25},{25,17},{2,10},{10... | collective-permute-start | bytes 786440 | tf_op jit(solution)/shard_map/ppermute | solution.py:310
  17.0 0.1 broadcast_in_dim.5.coords
  17.1 0.0 copy-start
  17.1 1.7 %copy-done = bf16[1,2,9,512,128]{4,3,2,1,0:T(8,128)(2,1)S(1)} copy-done((bf16[1,2,9,512,128]{4,3,2,1,0:T(8,128)(2,1)S(1)}, bf16[1,2,9,512,128]{4,3,2,1,0:T(8,128)(2,1)}, u32[]{:S(2)}) %copy-start) | copy-done | bytes 2359320
  18.8 0.0 copy-start.1
  18.8 0.7 %shard_map.49 = (f32[512,256]{1,0:T(8,128)S(1)}, f32[512,128]{1,0:T(8,128)S(1)}) custom-call(f32[2,256]{1,0:T(2,128)S(1)} %broadcast_in_dim.5.coords, bf16[512,256]{1,0:T(8,128)(2,1)S(1)} %get-tuple-element.26.own, f32[32,256]{1,0:T(8,128)S(1)} %add_sine_fusion.enc, bf16[64,256]{1,0:T(8,128)(2,1)S(1)} %shard_map.48.strip, ...), custom_call_target="tpu_custom_call" | custom-call | flops 5000000000 | bytes 4000000 | tf_op jit(solution)/shard_map/pallas_call | solution.py:292
  19.5 0.0 collective-permute-done.6.near_strip
  19.5 0.0 collective-permute-done.4.near
  19.5 0.1 shard_map.50
  19.6 0.2 collective-permute-start.7
  19.8 0.0 collective-permute-done.3.strip.far_strip
  19.8 1.1 %collective-permute-done.7.cols_a = bf16[64,256]{1,0:T(8,128)(2,1)S(1)} collective-permute-done((bf16[64,256]{1,0:T(8,128)(2,1)S(1)}, bf16[64,256]{1,0:T(8,128)(2,1)S(1)}, u32[]{:S(2)}, u32[]{:S(2)}) %collective-permute-start.7) | collective-permute-done | bytes 32800 | tf_op jit(solution)/shard_map/ppermute | solution.py:329
  20.9 1.3 %collective-permute-start.8 = (bf16[96,256]{1,0:T(8,128)(2,1)S(1)}, bf16[96,256]{1,0:T(8,128)(2,1)S(1)}, u32[]{:S(2)}, u32[]{:S(2)}) collective-permute-start(bf16[96,256]{1,0:T(8,128)(2,1)S(1)} %shard_map.51), channel_id=1, source_target_pairs={{0,8},{8,0},{16,24},{24,16},{1,9},{9,1},{17,25},{25,17},{2,10},{10... | collective-permute-start | bytes 147464 | tf_op jit(solution)/shard_map/ppermute | solution.py:310
  22.1 0.0 copy-done.1
  22.1 1.5 %shard_map.52 = (f32[512,256]{1,0:T(8,128)S(1)}, f32[512,128]{1,0:T(8,128)S(1)}) custom-call(f32[2,256]{1,0:T(2,128)S(1)} %broadcast_in_dim.5.coords, bf16[512,256]{1,0:T(8,128)(2,1)S(1)} %collective-permute-done.4.near, bf16[512,256]{1,0:T(8,128)(2,1)S(1)} %collective-permute-done.5.far, f32[32,256]{1,0:T(8,128)S(1)} %add_sine_fusion.enc, ...), custom_call_target="tpu_custom_call" | custom-call | tf_op jit(solution)/shard_map/pallas_call | solution.py:292
  23.6 1.5 %collective-permute-done.9.part = bf16[512,256]{1,0:T(8,128)(2,1)S(1)} collective-permute-done((bf16[512,256]{1,0:T(8,128)(2,1)S(1)}, bf16[512,256]{1,0:T(8,128)(2,1)S(1)}, u32[]{:S(2)}, u32[]{:S(2)}) %collective-permute-start.9) | collective-permute-done | bytes 262176 | tf_op jit(solution)/shard_map/ppermute | solution.py:310
  25.1 0.7 %shard_map.53 = (f32[512,256]{1,0:T(8,128)S(1)}, f32[512,128]{1,0:T(8,128)S(1)}) custom-call(f32[2,256]{1,0:T(2,128)S(1)} %broadcast_in_dim.5.coords, bf16[512,256]{1,0:T(8,128)(2,1)S(1)} %collective-permute-done.9.part, f32[32,256]{1,0:T(8,128)S(1)} %add_sine_fusion.enc, bf16[2,9,512,128]{3,2,1,0:T(8,128)(2,1)S(1)} %bitcast.9, ...), custom_call_target="tpu_custom_call" | custom-call | tf_op jit(solution)/shard_map/pallas_call | solution.py:292
  25.7 0.0 collective-permute-done.8.strip
  25.8 1.0 %shard_map.54 = bf16[512,256]{1,0:T(8,128)(2,1)} custom-call(f32[32,256]{1,0:T(8,128)S(1)} %add_sine_fusion.enc, bf16[96,256]{1,0:T(8,128)(2,1)S(1)} %collective-permute-done.8.strip, bf16[2,9,512,128]{3,2,1,0:T(8,128)(2,1)S(1)} %bitcast.10, f32[512,128]{1,0:T(8,128)S(1)} %get-tuple-element.35.joined_in, f32[512,256]{1,0:T(8,128)S(1)} %get-tuple-element.36.refs_0_), custom_call_target="tpu_custom_call" | custom-call | tf_op jit(solution)/shard_map/pallas_call | solution.py:292
  (5 shorter events, 0.1 us)
Async XLA Ops:
  0.0 16.3 %collective-permute-start.5 = (bf16[512,256]{1,0:T(8,128)(2,1)}, bf16[512,256]{1,0:T(8,128)(2,1)S(1)}, u32[]{:S(2)}, u32[]{:S(2)}) collective-permute-start(bf16[512,256]{1,0:T(8,128)(2,1)} %bitcast.11), channel_id=1, source_target_pairs={{0,16},{8,24},{16,0},{24,8},{1,17},{9,25},{17,1},{25,9},{2,18},{10... | collective-permute-start | bytes 786440 | tf_op jit(solution)/shard_map/ppermute | solution.py:310
  4.0 15.4 %collective-permute-start.4 = (bf16[512,256]{1,0:T(8,128)(2,1)}, bf16[512,256]{1,0:T(8,128)(2,1)S(1)}, u32[]{:S(2)}, u32[]{:S(2)}) collective-permute-start(bf16[512,256]{1,0:T(8,128)(2,1)} %bitcast.12), channel_id=1, source_target_pairs={{0,8},{8,0},{16,24},{24,16},{1,9},{9,1},{17,25},{25,17},{2,10},{10... | collective-permute-start | bytes 786440 | tf_op jit(solution)/shard_map/ppermute | solution.py:310
  5.6 1.0 %copy-start.2 = (bf16[1,32,16,256]{3,2,1,0:T(8,128)(2,1)S(1)}, bf16[1,32,16,256]{3,2,1,0:T(8,128)(2,1)}, u32[]{:S(2)}) copy-start(bf16[1,32,16,256]{3,2,1,0:T(8,128)(2,1)} %param.4) | copy-start | bytes 786436
  6.7 1.6 %collective-permute-start = (bf16[32,256]{1,0:T(8,128)(2,1)S(1)}, bf16[32,256]{1,0:T(8,128)(2,1)S(1)}, u32[]{:S(2)}, u32[]{:S(2)}) collective-permute-start(bf16[32,256]{1,0:T(8,128)(2,1)S(1)} %get-tuple-element.21), channel_id=1, source_target_pairs={{0,2},{4,6},{2,0},{6,4},{1,3},{5,7},{3,1},{7,5},{8,10},{12,14},{10... | collective-permute-start | bytes 49160 | tf_op jit(solution)/shard_map/ppermute | solution.py:329
  6.8 1.6 %collective-permute-start.1 = (bf16[32,256]{1,0:T(8,128)(2,1)S(1)}, bf16[32,256]{1,0:T(8,128)(2,1)S(1)}, u32[]{:S(2)}, u32[]{:S(2)}) collective-permute-start(bf16[32,256]{1,0:T(8,128)(2,1)S(1)} %get-tuple-element.22), channel_id=1, source_target_pairs={{2,4},{4,2},{3,5},{5,3},{10,12},{12,10},{11,13},{13,11},{18,20},{2... | collective-permute-start | bytes 49160 | tf_op jit(solution)/shard_map/ppermute | solution.py:329
  8.4 3.8 %collective-permute-start.2 = (bf16[32,256]{1,0:T(8,128)(2,1)S(1)}, bf16[32,256]{1,0:T(8,128)(2,1)S(1)}, u32[]{:S(2)}, u32[]{:S(2)}) collective-permute-start(bf16[32,256]{1,0:T(8,128)(2,1)S(1)} %shard_map.47), channel_id=1, source_target_pairs={{0,1},{1,0},{2,3},{3,2},{4,5},{5,4},{6,7},{7,6},{8,9},{9,8},{10,11... | collective-permute-start | bytes 49160 | tf_op jit(solution)/shard_map/ppermute | solution.py:340
  12.2 7.3 %collective-permute-start.6 = (bf16[64,256]{1,0:T(8,128)(2,1)S(1)}, bf16[64,256]{1,0:T(8,128)(2,1)S(1)}, u32[]{:S(2)}, u32[]{:S(2)}) collective-permute-start(bf16[64,256]{1,0:T(8,128)(2,1)S(1)} %shard_map.48.strip), channel_id=1, source_target_pairs={{0,8},{8,0},{16,24},{24,16},{1,9},{9,1},{17,25},{25,17},{2,10},{10... | collective-permute-start | bytes 98312 | tf_op jit(solution)/shard_map/ppermute | solution.py:310
  12.7 7.1 %collective-permute-start.3 = (bf16[64,256]{1,0:T(8,128)(2,1)S(1)}, bf16[64,256]{1,0:T(8,128)(2,1)S(1)}, u32[]{:S(2)}, u32[]{:S(2)}) collective-permute-start(bf16[64,256]{1,0:T(8,128)(2,1)S(1)} %shard_map.48.strip), channel_id=1, source_target_pairs={{0,16},{8,24},{16,0},{24,8},{1,17},{9,25},{17,1},{25,9},{2,18},{10... | collective-permute-start | bytes 98312 | tf_op jit(solution)/shard_map/ppermute | solution.py:310
  16.3 8.8 %collective-permute-start.9 = (bf16[512,256]{1,0:T(8,128)(2,1)S(1)}, bf16[512,256]{1,0:T(8,128)(2,1)S(1)}, u32[]{:S(2)}, u32[]{:S(2)}) collective-permute-start(bf16[512,256]{1,0:T(8,128)(2,1)S(1)} %collective-permute-done.5.far), channel_id=1, source_target_pairs={{0,8},{8,0},{16,24},{24,16},{1,9},{9,1},{17,25},{25,17},{2,10},{10... | collective-permute-start | bytes 786440 | tf_op jit(solution)/shard_map/ppermute | solution.py:310
  17.1 1.7 %copy-start = (bf16[1,2,9,512,128]{4,3,2,1,0:T(8,128)(2,1)S(1)}, bf16[1,2,9,512,128]{4,3,2,1,0:T(8,128)(2,1)}, u32[]{:S(2)}) copy-start(bf16[1,2,9,512,128]{4,3,2,1,0:T(8,128)(2,1)} %param.7) | copy-start | bytes 7077892
  18.8 3.3 %copy-start.1 = (bf16[1,2,9,512,128]{4,3,2,1,0:T(8,128)(2,1)S(1)}, bf16[1,2,9,512,128]{4,3,2,1,0:T(8,128)(2,1)}, u32[]{:S(2)}) copy-start(bf16[1,2,9,512,128]{4,3,2,1,0:T(8,128)(2,1)} %param.7) | copy-start | bytes 7077892
  19.6 1.3 %collective-permute-start.7 = (bf16[64,256]{1,0:T(8,128)(2,1)S(1)}, bf16[64,256]{1,0:T(8,128)(2,1)S(1)}, u32[]{:S(2)}, u32[]{:S(2)}) collective-permute-start(bf16[64,256]{1,0:T(8,128)(2,1)S(1)} %shard_map.50), channel_id=1, source_target_pairs={{0,2},{4,6},{2,0},{6,4},{1,3},{5,7},{3,1},{7,5},{8,10},{12,14},{10... | collective-permute-start | bytes 98312 | tf_op jit(solution)/shard_map/ppermute | solution.py:329
  20.9 4.9 %collective-permute-start.8 = (bf16[96,256]{1,0:T(8,128)(2,1)S(1)}, bf16[96,256]{1,0:T(8,128)(2,1)S(1)}, u32[]{:S(2)}, u32[]{:S(2)}) collective-permute-start(bf16[96,256]{1,0:T(8,128)(2,1)S(1)} %shard_map.51), channel_id=1, source_target_pairs={{0,8},{8,0},{16,24},{24,16},{1,9},{9,1},{17,25},{25,17},{2,10},{10... | collective-permute-start | bytes 147464 | tf_op jit(solution)/shard_map/ppermute | solution.py:310

commit v6 on v5

--- a/solution.py
+++ b/solution.py
@@ -183,44 +183,36 @@
     joined[...] = convolve(rows * cols, cols, windows, weights, me)
 
 
-def middle_kernel(rows, cols, shards, pick, coords, near, far, enc, near_strip, far_strip, cols_a,
-                  weights, base_in, joined_in, base, joined, wide, windows):
+def middle_kernel(rows, cols, shards, pick, coords, near, far, enc, near_strip, cols_a, weights,
+                  base_in, joined_in, base, joined, wide, windows):
     me = lax.axis_index("src")
     width = joined.shape[1]
-    sums = []
-    views = (
-        (1, near, near_strip, cols_a.at[0:rows], base_in),
-        (2, far, far_strip, cols_a.at[rows : 2 * rows], None),
-    )
-    for k, view, strip, raw_a, start in views:
-        index = jnp.bitwise_xor(me, k)
-        edges = halo(rows, cols, shards, pick, enc, strip, raw_a)
-        weight = blend_weight(coords, index)
-        unfold(rows, cols, view, enc, edges, wide, windows, base, weight, start)
-        sums.append(convolve(rows * cols, cols, windows, weights, index))
-    joined[...] = sums[1]
+    index = jnp.bitwise_xor(me, 1)
+    edges = halo(rows, cols, shards, pick, enc, near_strip, cols_a.at[0:rows])
+    weight = blend_weight(coords, index)
+    unfold(rows, cols, near, enc, edges, wide, windows, base, weight, base_in)
+    done = joined_in[...] + convolve(rows * cols, cols, windows, weights, index)
     here = pl.ds(pl.multiple_of(lax.div(me, 2) * width, width), width)
-    base[:, here] = base[:, here] + silu(joined_in[...] + sums[0])
-
-
-def inside_kernel(rows, cols, top, coords, part, enc, weights, base_in, joined_in, base, joined, wide,
-                  windows):
-    index = jnp.bitwise_xor(lax.axis_index("src"), 3)
+    base[:, here] = base[:, here] + silu(done)
+    joined[...] = jnp.zeros_like(joined)
+    inside(rows, cols, 3, coords, far, enc, weights, base, base, joined, wide, windows)
+
+
+def inside(rows, cols, k, coords, view, enc, weights, base_in, base, joined, wide, windows):
+    index = jnp.bitwise_xor(lax.axis_index("src"), k)
     weight = blend_weight(coords, index)
     chan, width = base.shape[1], joined.shape[1]
-    count = part.shape[0] // cols
-    column = jnp.zeros((count, LANES), F32)
+    column = jnp.zeros((rows, LANES), F32)
     for c in range(chan // LANES):
-        wide[c, pl.ds(PITCH + 7, count, stride=PITCH), :] = column
-        wide[c, pl.ds(PITCH + 8 + cols, count, stride=PITCH), :] = column
-    for h in range(count):
+        wide[c, pl.ds(PITCH + 7, rows, stride=PITCH), :] = column
+        wide[c, pl.ds(PITCH + 8 + cols, rows, stride=PITCH), :] = column
+    for h in range(rows):
         here = slice(h * cols, (h + 1) * cols)
-        line = enc[top + h : top + h + 1, :]
-        posed = (part[here, :].astype(F32) + line).astype(BF16).astype(F32)
+        posed = (view[here, :].astype(F32) + enc[h : h + 1, :]).astype(BF16).astype(F32)
         at = (h + 1) * PITCH + 8
         for c, lanes in tiles(chan):
             wide[c, at : at + cols, :] = posed[:, lanes]
-        base[here, :] = base_in[(top + h) * cols : (top + h + 1) * cols, :] + weight * posed
+        base[here, :] = base_in[here, :] + weight * posed
         for b in range(3):
             for c in range(chan // LANES):
                 to = b * chan + c * LANES
@@ -228,60 +220,68 @@
     group = lax.div(index, 2)
     at = pl.multiple_of(lax.rem(index, 2) * chan, chan)
     taps = jnp.dot(
-        windows[0 : count * cols, :], kernel_of(weights, group, at, chan), preferred_element_type=F32
-    )
-    joined[...] = joined_in[...]
+        windows[0 : rows * cols, :], kernel_of(weights, group, at, chan), preferred_element_type=F32
+    )
     for a in range(3):
-        first, last = max(top + 1 - a, 0), min(top + 1 - a + count, rows)
-        skip = (first - (top + 1 - a)) * cols
-        size = (last - first) * cols
+        first, last = max(1 - a, 0), min(1 - a + rows, rows)
+        skip, size = (first - (1 - a)) * cols, (last - first) * cols
         joined[first * cols : last * cols, :] += taps[
             skip : skip + size, a * width : (a + 1) * width
         ]
 
 
-def rim_kernel(rows, cols, shards, pick, enc, strip, weights, joined_in, *refs):
-    index = jnp.bitwise_xor(lax.axis_index("src"), 3)
-    *bases, out, joined = refs
+def last_kernel(rows, cols, coords, last, enc, weights, base_in, joined_in, base, joined, wide,
+                windows):
+    joined[...] = joined_in[...]
+    inside(rows, cols, 2, coords, last, enc, weights, base_in, base, joined, wide, windows)
+
+
+def rim_kernel(rows, cols, shards, pick, enc, last_strip, relayed, cols_a, weights, base, joined_in,
+               out, joined):
+    me = lax.axis_index("src")
     chan, width = out.shape[1], joined.shape[1]
-    group = lax.div(index, 2)
-    at = pl.multiple_of(lax.rem(index, 2) * chan, chan)
-
-    def taps(pairs):
-        return jnp.concatenate([weights[group, 3 * a + b, pl.ds(at, chan), :] for a, b in pairs], axis=0)
+    group = lax.div(jnp.bitwise_xor(me, 2), 2)
+    size = last_strip.shape[0]
+    edges = [
+        (3, halo(rows, cols, shards, pick, enc, relayed.at[0:size], cols_a.at[rows : 2 * rows])),
+        (2, halo(rows, cols, shards, pick, enc, last_strip, relayed.at[size : size + rows])),
+    ]
+
+    def add(where, lines, pairs):
+        wide, kernel = [], []
+        for k, line in lines:
+            at = pl.multiple_of(lax.rem(jnp.bitwise_xor(me, k), 2) * chan, chan)
+            count = line.shape[0] - 2
+            wide += [line[i : i + count] for i in range(3)]
+            kernel += [weights[group, 3 * a + b, pl.ds(at, chan), :] for a, b in pairs]
+        joined[where, :] += jnp.dot(
+            jnp.concatenate(wide, axis=1).astype(BF16),
+            jnp.concatenate(kernel, axis=0),
+            preferred_element_type=F32,
+        )
 
     joined[...] = joined_in[...]
-    size = strip.shape[0] - rows
-    left, right, before, after = halo(
-        rows, cols, shards, pick, enc, strip.at[0:size], strip.at[size:]
-    )
-    for column, corner, b in ((left, 0, 0), (right, 1, 2)):
-        above, below = (line[cols + corner : cols + corner + 1] for line in (before, after))
-        tall = jnp.concatenate([above, column, below], axis=0)
-        wide = jnp.concatenate([tall[a : a + rows] for a in range(3)], axis=1).astype(BF16)
-        kernel = taps([(a, b) for a in range(3)])
-        where = pl.ds(b // 2 * (cols - 1), rows, stride=cols)
-        joined[where, :] += jnp.dot(wide, kernel, preferred_element_type=F32)
+    for side, b in ((0, 0), (1, 2)):
+        tall = []
+        for k, view in edges:
+            above, below = (line[cols + side : cols + side + 1] for line in view[2:])
+            tall.append((k, jnp.concatenate([above, view[side], below], axis=0)))
+        where = pl.ds(side * (cols - 1), rows, stride=cols)
+        add(where, tall, [(a, b) for a in range(3)])
+    zero = jnp.zeros((1, chan), F32)
     if pick:
         first = lax.axis_index(pick) == 0
-        lines = [(before + after, jnp.where(first, rows - 1, 0), jnp.where(first, 2, 0))]
+        places = [(jnp.where(first, rows - 1, 0), jnp.where(first, 2, 0), lambda view: view[2] + view[3])]
     else:
-        lines = [(before, 0, 0), (after, rows - 1, 2)]
-    for line, h, a in lines:
-        zero = jnp.zeros((1, chan), F32)
-        tall = jnp.concatenate([zero, line[0:cols], zero], axis=0)
-        wide = jnp.concatenate([tall[b : b + cols] for b in range(3)], axis=1).astype(BF16)
+        places = [(0, 0, lambda view: view[2]), (rows - 1, 2, lambda view: view[3])]
+    for h, a, line in places:
+        tall = [(k, jnp.concatenate([zero, line(view)[0:cols], zero], axis=0)) for k, view in edges]
         where = pl.ds(pl.multiple_of(h * cols, cols), cols)
-        kernel = taps([(a, b) for b in range(3)])
-        joined[where, :] += jnp.dot(wide, kernel, preferred_element_type=F32)
-    added, at = silu(joined[...]), 0
-    for base in bases:
-        size = base.shape[0]
-        for c, lanes in tiles(chan):
-            here = group == c * LANES // width
-            more = jnp.where(here, added[at : at + size], 0.0)
-            out[at : at + size, lanes] = (base[:, lanes] + more).astype(BF16)
-        at += size
+        add(where, tall, [(a, b) for b in range(3)])
+    added = silu(joined[...])
+    for c, lanes in tiles(chan):
+        here = group == c * LANES // width
+        out[:, lanes] = (base[:, lanes] + jnp.where(here, added, 0.0)).astype(BF16)
 
 
 def shape(rows, chan, dtype=BF16):
@@ -309,7 +309,7 @@
     def across(array, k):
         return lax.ppermute(array, "src", [(i, i ^ k) for i in range(4)])
 
-    far = across(own, 2)
+    far = across(own, 3)
     near = across(own, 1)
     rowpos = offsets[0] + jnp.arange(rows, dtype=jnp.int32)
     enc = encoding(rowpos, chan)
@@ -349,9 +349,9 @@
         [got_a, got_b, enc, *beyond],
         [shape(rows + len(beyond) * (cols + 16), chan)],
     )[0]
-    near_strip, far_strip = across(strip, 1), across(strip, 2)
+    near_strip, last_strip = across(strip, 1), across(strip, 2)
     far, panel = lax.optimization_barrier((far, panel))
-    parts = [(0, across(far, 1))]
+    last = across(far, 1)
 
     scratch = [
         pltpu.VMEM((chan // LANES, (rows + 2) * PITCH + 8, LANES), F32),
@@ -376,30 +376,27 @@
     cols_a = swap(cols_a, 0)
     relayed = call(
         functools.partial(relay_kernel, rows),
-        [far_strip, cols_a],
+        [last_strip, cols_a],
         [shape(strip.shape[0] + rows, chan)],
     )[0]
-    last_strip = across(relayed, 1)
+    relayed = across(relayed, 1)
     base, joined = call(
         functools.partial(middle_kernel, rows, cols, shards, pick),
-        [place, near, far, enc, near_strip, far_strip, cols_a, weights[0], base, joined],
+        [place, near, far, enc, near_strip, cols_a, weights[0], base, joined],
         sums,
         scratch,
         cost=pl.CostEstimate(flops=0, bytes_accessed=0, transcendentals=0),
     )
-    bases = []
-    for top, part in parts:
-        done, joined = call(
-            functools.partial(inside_kernel, rows, cols, top),
-            [place, part, enc, weights[0], base, joined],
-            [shape(part.shape[0], chan, F32), shape(pixels, width, F32)],
-            scratch,
-            cost=pl.CostEstimate(flops=0, bytes_accessed=0, transcendentals=0),
-        )
-        bases.append(done)
+    base, joined = call(
+        functools.partial(last_kernel, rows, cols),
+        [place, last, enc, weights[0], base, joined],
+        sums,
+        scratch,
+        cost=pl.CostEstimate(flops=0, bytes_accessed=0, transcendentals=0),
+    )
     out = call(
         functools.partial(rim_kernel, rows, cols, shards, pick),
-        [enc, last_strip, weights[0], joined, *bases],
+        [enc, last_strip, relayed, cols_a, weights[0], base, joined],
         [shape(pixels, chan)],
         [pltpu.VMEM((pixels, width), F32)],
     )[0]

time: 27 us -> 26.7 us (0.989)
  waiting for transfers between devices: 7.75 us -> 3.98 us
  starting transfers between devices: 10.7 us -> 14.1 us
    ppermute x6, waiting for transfers between devices: 5.1 us -> 1.26 us  [across(): return lax.ppermute(array, 'src', [(i, i ^ k) for i in range(4)])]
    ppermute x6, starting transfers between devices: 8.16 us -> 11.6 us  [across(): return lax.ppermute(array, 'src', [(i, i ^ k) for i in range(4)])]
  transfers between devices with their start and end apart: 10 -> 10, of which waited for: 4 -> 4; matrix products, arithmetic and copies ran while one was open for 3% -> 4% of each run, Pallas kernels for 11% -> 11%
where the time goes in v6:
time: 26.7 us; the launch traced here: 26.5 us
  starting transfers between devices  14.1 us (53%)
  Pallas kernels  4.03 us (15%)
  waiting for transfers between devices  3.98 us (15%)
  local copies, waits for them, and re-layouts  2.75 us (10%)
  other arithmetic  0.86 us (3%)
  between operations  0.77 us (3%)
    ppermute x6, starting transfers between devices, across(): return lax.ppermute(array, 'src', [(i, i ^ k) for i in range(4)])  11.6 us
    pallas_call x9, Pallas kernels, call(): pl.pallas_call(kernel, out_shape=outs, in_specs=[VMEM_SPEC] * len(ins), o...  4.03 us
    unnamed x6, local copies, waits for them, and re-layouts  2.68 us
    ppermute x1, waiting for transfers between devices, local(): beyond = [lax.ppermute(edges[0], 'slab', [(0, 1), (1, 0)])]  1.59 us
    ppermute x1, starting transfers between devices, local(): beyond = [lax.ppermute(edges[0], 'slab', [(0, 1), (1, 0)])]  1.56 us
    ppermute x6, waiting for transfers between devices, across(): return lax.ppermute(array, 'src', [(i, i ^ k) for i in range(4)])  1.26 us
    ppermute x3, waiting for transfers between devices, swap(): return lax.ppermute(array, 'shard', pairs + [(j, i) for i, j in pairs])  1.13 us
    ppermute x3, starting transfers between devices, swap(): return lax.ppermute(array, 'shard', pairs + [(j, i) for i, j in pairs])  0.88 us
  transfers between devices with their start and end apart: 10, of which 4 were waited for; matrix products, arithmetic and copies ran while one was open for 4% of the time, Pallas kernels for 11%

profile of v6, /device:TPU:0, one launch (start us, length us, event | category | flops | bytes accessed | tf_op | source)
XLA Modules:
  0.0 26.5 jit_solution(4891327476784334397)
XLA Ops:
  0.0 5.0 %collective-permute-start.5 = (bf16[512,256]{1,0:T(8,128)(2,1)}, bf16[512,256]{1,0:T(8,128)(2,1)S(1)}, u32[]{:S(2)}, u32[]{:S(2)}) collective-permute-start(bf16[512,256]{1,0:T(8,128)(2,1)} %bitcast.11), channel_id=1, source_target_pairs={{0,24},{8,16},{16,8},{24,0},{1,25},{9,17},{17,9},{25,1},{2,26},{10... | collective-permute-start | bytes 786440 | tf_op jit(solution)/shard_map/ppermute | solution.py:310
  5.0 0.0 collective-permute-start.4
  5.1 0.0 copy-start.2
  5.1 1.0 %copy-done.2 = bf16[1,32,16,256]{3,2,1,0:T(8,128)(2,1)S(1)} copy-done((bf16[1,32,16,256]{3,2,1,0:T(8,128)(2,1)S(1)}, bf16[1,32,16,256]{3,2,1,0:T(8,128)(2,1)}, u32[]{:S(2)}) %copy-start.2) | copy-done | bytes 262168
  6.1 0.1 shard_map.46
  6.1 0.1 collective-permute-start
  6.2 0.7 %collective-permute-start.1 = (bf16[32,256]{1,0:T(8,128)(2,1)S(1)}, bf16[32,256]{1,0:T(8,128)(2,1)S(1)}, u32[]{:S(2)}, u32[]{:S(2)}) collective-permute-start(bf16[32,256]{1,0:T(8,128)(2,1)S(1)} %get-tuple-element.22), channel_id=1, source_target_pairs={{2,4},{4,2},{3,5},{5,3},{10,12},{12,10},{11,13},{13,11},{18,20},{2... | collective-permute-start | bytes 49160 | tf_op jit(solution)/shard_map/ppermute | solution.py:329
  7.6 0.2 add_sine_fusion.enc
  7.8 0.0 collective-permute-done.got_a
  7.8 0.0 collective-permute-done.1.got_b
  7.8 1.6 %collective-permute-start.2 = (bf16[32,256]{1,0:T(8,128)(2,1)S(1)}, bf16[32,256]{1,0:T(8,128)(2,1)S(1)}, u32[]{:S(2)}, u32[]{:S(2)}) collective-permute-start(bf16[32,256]{1,0:T(8,128)(2,1)S(1)} %shard_map.47), channel_id=1, source_target_pairs={{0,1},{1,0},{2,3},{3,2},{4,5},{5,4},{6,7},{7,6},{8,9},{9,8},{10,11... | collective-permute-start | bytes 49160 | tf_op jit(solution)/shard_map/ppermute | solution.py:340
  9.4 0.7 %convert_bitcast_fusion = f32[2]{0:T(128)S(1)} fusion(s32[1,2]{1,0:T(1,128)} %param.5), kind=kLoop, calls=%fused_computation.13 | loop fusion | flops 2 | bytes 16 | tf_op jit(solution)/shard_map/broadcast_in_dim | solution.py:324
  10.0 1.6 %collective-permute-done.2.refs_0_ = bf16[32,256]{1,0:T(8,128)(2,1)S(1)} collective-permute-done((bf16[32,256]{1,0:T(8,128)(2,1)S(1)}, bf16[32,256]{1,0:T(8,128)(2,1)S(1)}, u32[]{:S(2)}, u32[]{:S(2)}) %collective-permute-start.2) | collective-permute-done | bytes 16416 | tf_op jit(solution)/shard_map/ppermute | solution.py:340
  11.6 2.1 %collective-permute-start.6 = (bf16[64,256]{1,0:T(8,128)(2,1)S(1)}, bf16[64,256]{1,0:T(8,128)(2,1)S(1)}, u32[]{:S(2)}, u32[]{:S(2)}) collective-permute-start(bf16[64,256]{1,0:T(8,128)(2,1)S(1)} %shard_map.48.strip), channel_id=1, source_target_pairs={{0,8},{8,0},{16,24},{24,16},{1,9},{9,1},{17,25},{25,17},{2,10},{10... | collective-permute-start | bytes 98312 | tf_op jit(solution)/shard_map/ppermute | solution.py:310
  13.7 0.0 collective-permute-start.3
  13.7 0.0 collective-permute-done.5.far
  13.7 3.2 %collective-permute-start.9 = (bf16[512,256]{1,0:T(8,128)(2,1)S(1)}, bf16[512,256]{1,0:T(8,128)(2,1)S(1)}, u32[]{:S(2)}, u32[]{:S(2)}) collective-permute-start(bf16[512,256]{1,0:T(8,128)(2,1)S(1)} %collective-permute-done.5.far), channel_id=1, source_target_pairs={{0,8},{8,0},{16,24},{24,16},{1,9},{9,1},{17,25},{25,17},{2,10},{10... | collective-permute-start | bytes 786440 | tf_op jit(solution)/shard_map/ppermute | solution.py:310
  16.9 0.1 broadcast_in_dim.5.coords
  17.0 0.0 copy-start
  17.0 1.7 %copy-done = bf16[1,2,9,512,128]{4,3,2,1,0:T(8,128)(2,1)S(1)} copy-done((bf16[1,2,9,512,128]{4,3,2,1,0:T(8,128)(2,1)S(1)}, bf16[1,2,9,512,128]{4,3,2,1,0:T(8,128)(2,1)}, u32[]{:S(2)}) %copy-start) | copy-done | bytes 2359320
  18.6 0.0 copy-start.1
  18.7 0.7 %shard_map.49 = (f32[512,256]{1,0:T(8,128)S(1)}, f32[512,128]{1,0:T(8,128)S(1)}) custom-call(f32[2,256]{1,0:T(2,128)S(1)} %broadcast_in_dim.5.coords, bf16[512,256]{1,0:T(8,128)(2,1)S(1)} %get-tuple-element.26.own, f32[32,256]{1,0:T(8,128)S(1)} %add_sine_fusion.enc, bf16[64,256]{1,0:T(8,128)(2,1)S(1)} %shard_map.48.strip, ...), custom_call_target="tpu_custom_call" | custom-call | flops 5000000000 | bytes 4000000 | tf_op jit(solution)/shard_map/pallas_call | solution.py:292
  19.3 0.0 collective-permute-done.6.near_strip
  19.3 0.0 collective-permute-done.4.near
  19.3 0.1 shard_map.50
  19.5 0.1 collective-permute-start.7
  19.6 0.0 collective-permute-done.3.strip.last_strip
  19.6 1.1 %collective-permute-done.7.cols_a = bf16[64,256]{1,0:T(8,128)(2,1)S(1)} collective-permute-done((bf16[64,256]{1,0:T(8,128)(2,1)S(1)}, bf16[64,256]{1,0:T(8,128)(2,1)S(1)}, u32[]{:S(2)}, u32[]{:S(2)}) %collective-permute-start.7) | collective-permute-done | bytes 32800 | tf_op jit(solution)/shard_map/ppermute | solution.py:329
  20.7 1.3 %collective-permute-start.8 = (bf16[96,256]{1,0:T(8,128)(2,1)S(1)}, bf16[96,256]{1,0:T(8,128)(2,1)S(1)}, u32[]{:S(2)}, u32[]{:S(2)}) collective-permute-start(bf16[96,256]{1,0:T(8,128)(2,1)S(1)} %shard_map.51), channel_id=1, source_target_pairs={{0,8},{8,0},{16,24},{24,16},{1,9},{9,1},{17,25},{25,17},{2,10},{10... | collective-permute-start | bytes 147464 | tf_op jit(solution)/shard_map/ppermute | solution.py:310
  22.1 0.0 copy-done.1
  22.1 1.4 %shard_map.52 = (f32[512,256]{1,0:T(8,128)S(1)}, f32[512,128]{1,0:T(8,128)S(1)}) custom-call(f32[2,256]{1,0:T(2,128)S(1)} %broadcast_in_dim.5.coords, bf16[512,256]{1,0:T(8,128)(2,1)S(1)} %collective-permute-done.4.near, bf16[512,256]{1,0:T(8,128)(2,1)S(1)} %collective-permute-done.5.far, f32[32,256]{1,0:T(8,128)S(1)} %add_sine_fusion.enc, ...), custom_call_target="tpu_custom_call" | custom-call | tf_op jit(solution)/shard_map/pallas_call | solution.py:292
  23.5 0.4 %collective-permute-done.9.last = bf16[512,256]{1,0:T(8,128)(2,1)S(1)} collective-permute-done((bf16[512,256]{1,0:T(8,128)(2,1)S(1)}, bf16[512,256]{1,0:T(8,128)(2,1)S(1)}, u32[]{:S(2)}, u32[]{:S(2)}) %collective-permute-start.9) | collective-permute-done | bytes 262176 | tf_op jit(solution)/shard_map/ppermute | solution.py:310
  23.9 0.7 %shard_map.53 = (f32[512,256]{1,0:T(8,128)S(1)}, f32[512,128]{1,0:T(8,128)S(1)}) custom-call(f32[2,256]{1,0:T(2,128)S(1)} %broadcast_in_dim.5.coords, bf16[512,256]{1,0:T(8,128)(2,1)S(1)} %collective-permute-done.9.last, f32[32,256]{1,0:T(8,128)S(1)} %add_sine_fusion.enc, bf16[2,9,512,128]{3,2,1,0:T(8,128)(2,1)S(1)} %bitcast.9, ...), custom_call_target="tpu_custom_call" | custom-call | tf_op jit(solution)/shard_map/pallas_call | solution.py:292
  24.5 0.9 %collective-permute-done.8.relayed = bf16[96,256]{1,0:T(8,128)(2,1)S(1)} collective-permute-done((bf16[96,256]{1,0:T(8,128)(2,1)S(1)}, bf16[96,256]{1,0:T(8,128)(2,1)S(1)}, u32[]{:S(2)}, u32[]{:S(2)}) %collective-permute-start.8) | collective-permute-done | bytes 49184 | tf_op jit(solution)/shard_map/ppermute | solution.py:310
  25.4 1.1 %shard_map.54 = bf16[512,256]{1,0:T(8,128)(2,1)} custom-call(f32[32,256]{1,0:T(8,128)S(1)} %add_sine_fusion.enc, bf16[64,256]{1,0:T(8,128)(2,1)S(1)} %collective-permute-done.3.strip.last_strip, bf16[96,256]{1,0:T(8,128)(2,1)S(1)} %collective-permute-done.8.relayed, bf16[64,256]{1,0:T(8,128)(2,1)S(1)} %collective-permute-done.7.cols_a, ...), custom_call_target="tpu_custom_call" | custom-call | tf_op jit(solution)/shard_map/pallas_call | solution.py:292
  (5 shorter events, 0.1 us)
Async XLA Ops:
  0.0 13.7 %collective-permute-start.5 = (bf16[512,256]{1,0:T(8,128)(2,1)}, bf16[512,256]{1,0:T(8,128)(2,1)S(1)}, u32[]{:S(2)}, u32[]{:S(2)}) collective-permute-start(bf16[512,256]{1,0:T(8,128)(2,1)} %bitcast.11), channel_id=1, source_target_pairs={{0,24},{8,16},{16,8},{24,0},{1,25},{9,17},{17,9},{25,1},{2,26},{10... | collective-permute-start | bytes 786440 | tf_op jit(solution)/shard_map/ppermute | solution.py:310
  5.0 14.3 %collective-permute-start.4 = (bf16[512,256]{1,0:T(8,128)(2,1)}, bf16[512,256]{1,0:T(8,128)(2,1)S(1)}, u32[]{:S(2)}, u32[]{:S(2)}) collective-permute-start(bf16[512,256]{1,0:T(8,128)(2,1)} %bitcast.12), channel_id=1, source_target_pairs={{0,8},{8,0},{16,24},{24,16},{1,9},{9,1},{17,25},{25,17},{2,10},{10... | collective-permute-start | bytes 786440 | tf_op jit(solution)/shard_map/ppermute | solution.py:310
  5.1 1.0 %copy-start.2 = (bf16[1,32,16,256]{3,2,1,0:T(8,128)(2,1)S(1)}, bf16[1,32,16,256]{3,2,1,0:T(8,128)(2,1)}, u32[]{:S(2)}) copy-start(bf16[1,32,16,256]{3,2,1,0:T(8,128)(2,1)} %param.4) | copy-start | bytes 786436
  6.1 1.6 %collective-permute-start = (bf16[32,256]{1,0:T(8,128)(2,1)S(1)}, bf16[32,256]{1,0:T(8,128)(2,1)S(1)}, u32[]{:S(2)}, u32[]{:S(2)}) collective-permute-start(bf16[32,256]{1,0:T(8,128)(2,1)S(1)} %get-tuple-element.21), channel_id=1, source_target_pairs={{0,2},{4,6},{2,0},{6,4},{1,3},{5,7},{3,1},{7,5},{8,10},{12,14},{10... | collective-permute-start | bytes 49160 | tf_op jit(solution)/shard_map/ppermute | solution.py:329
  6.2 1.6 %collective-permute-start.1 = (bf16[32,256]{1,0:T(8,128)(2,1)S(1)}, bf16[32,256]{1,0:T(8,128)(2,1)S(1)}, u32[]{:S(2)}, u32[]{:S(2)}) collective-permute-start(bf16[32,256]{1,0:T(8,128)(2,1)S(1)} %get-tuple-element.22), channel_id=1, source_target_pairs={{2,4},{4,2},{3,5},{5,3},{10,12},{12,10},{11,13},{13,11},{18,20},{2... | collective-permute-start | bytes 49160 | tf_op jit(solution)/shard_map/ppermute | solution.py:329
  7.8 3.8 %collective-permute-start.2 = (bf16[32,256]{1,0:T(8,128)(2,1)S(1)}, bf16[32,256]{1,0:T(8,128)(2,1)S(1)}, u32[]{:S(2)}, u32[]{:S(2)}) collective-permute-start(bf16[32,256]{1,0:T(8,128)(2,1)S(1)} %shard_map.47), channel_id=1, source_target_pairs={{0,1},{1,0},{2,3},{3,2},{4,5},{5,4},{6,7},{7,6},{8,9},{9,8},{10,11... | collective-permute-start | bytes 49160 | tf_op jit(solution)/shard_map/ppermute | solution.py:340
  11.6 7.7 %collective-permute-start.6 = (bf16[64,256]{1,0:T(8,128)(2,1)S(1)}, bf16[64,256]{1,0:T(8,128)(2,1)S(1)}, u32[]{:S(2)}, u32[]{:S(2)}) collective-permute-start(bf16[64,256]{1,0:T(8,128)(2,1)S(1)} %shard_map.48.strip), channel_id=1, source_target_pairs={{0,8},{8,0},{16,24},{24,16},{1,9},{9,1},{17,25},{25,17},{2,10},{10... | collective-permute-start | bytes 98312 | tf_op jit(solution)/shard_map/ppermute | solution.py:310
  13.7 5.9 %collective-permute-start.3 = (bf16[64,256]{1,0:T(8,128)(2,1)S(1)}, bf16[64,256]{1,0:T(8,128)(2,1)S(1)}, u32[]{:S(2)}, u32[]{:S(2)}) collective-permute-start(bf16[64,256]{1,0:T(8,128)(2,1)S(1)} %shard_map.48.strip), channel_id=1, source_target_pairs={{0,16},{8,24},{16,0},{24,8},{1,17},{9,25},{17,1},{25,9},{2,18},{10... | collective-permute-start | bytes 98312 | tf_op jit(solution)/shard_map/ppermute | solution.py:310
  13.7 10.2 %collective-permute-start.9 = (bf16[512,256]{1,0:T(8,128)(2,1)S(1)}, bf16[512,256]{1,0:T(8,128)(2,1)S(1)}, u32[]{:S(2)}, u32[]{:S(2)}) collective-permute-start(bf16[512,256]{1,0:T(8,128)(2,1)S(1)} %collective-permute-done.5.far), channel_id=1, source_target_pairs={{0,8},{8,0},{16,24},{24,16},{1,9},{9,1},{17,25},{25,17},{2,10},{10... | collective-permute-start | bytes 786440 | tf_op jit(solution)/shard_map/ppermute | solution.py:310
  17.0 1.7 %copy-start = (bf16[1,2,9,512,128]{4,3,2,1,0:T(8,128)(2,1)S(1)}, bf16[1,2,9,512,128]{4,3,2,1,0:T(8,128)(2,1)}, u32[]{:S(2)}) copy-start(bf16[1,2,9,512,128]{4,3,2,1,0:T(8,128)(2,1)} %param.7) | copy-start | bytes 7077892
  18.6 3.4 %copy-start.1 = (bf16[1,2,9,512,128]{4,3,2,1,0:T(8,128)(2,1)S(1)}, bf16[1,2,9,512,128]{4,3,2,1,0:T(8,128)(2,1)}, u32[]{:S(2)}) copy-start(bf16[1,2,9,512,128]{4,3,2,1,0:T(8,128)(2,1)} %param.7) | copy-start | bytes 7077892
  19.5 1.3 %collective-permute-start.7 = (bf16[64,256]{1,0:T(8,128)(2,1)S(1)}, bf16[64,256]{1,0:T(8,128)(2,1)S(1)}, u32[]{:S(2)}, u32[]{:S(2)}) collective-permute-start(bf16[64,256]{1,0:T(8,128)(2,1)S(1)} %shard_map.50), channel_id=1, source_target_pairs={{0,2},{4,6},{2,0},{6,4},{1,3},{5,7},{3,1},{7,5},{8,10},{12,14},{10... | collective-permute-start | bytes 98312 | tf_op jit(solution)/shard_map/ppermute | solution.py:329
  20.7 4.7 %collective-permute-start.8 = (bf16[96,256]{1,0:T(8,128)(2,1)S(1)}, bf16[96,256]{1,0:T(8,128)(2,1)S(1)}, u32[]{:S(2)}, u32[]{:S(2)}) collective-permute-start(bf16[96,256]{1,0:T(8,128)(2,1)S(1)} %shard_map.51), channel_id=1, source_target_pairs={{0,8},{8,0},{16,24},{24,16},{1,9},{9,1},{17,25},{25,17},{2,10},{10... | collective-permute-start | bytes 147464 | tf_op jit(solution)/shard_map/ppermute | solution.py:310

commit v7 on v4

v7 whole, which is shorter than its diff:
```python
import functools
import math

import jax
import jax.numpy as jnp
from jax import lax
from jax.experimental import pallas as pl
from jax.experimental.pallas import tpu as pltpu
from jax.sharding import PartitionSpec as P

BF16, F32 = jnp.bfloat16, jnp.float32
VMEM_SPEC = pl.BlockSpec(memory_space=pltpu.VMEM)
LANES = 128
BLOCKS = 4


def encoding(rowpos, chan_count):
    channel_idx = jnp.arange(chan_count, dtype=jnp.int32)
    halves = (channel_idx // 2).astype(F32)
    frequency = jnp.exp(-math.log(1000.0) * halves / (chan_count / 2))
    phases = (channel_idx % 2).astype(F32) * (math.pi / 2)
    return jnp.sin(rowpos.astype(F32)[:, None] * frequency[None, :] + phases[None, :])


def blend_weight(coords, view_index):
    vertical, across = coords[0:1, :] / 6.0, coords[1:2, :] / 6.0
    low, left = lax.div(view_index, 2) == 0, lax.rem(view_index, 2) == 0
    return jnp.where(low, 1.0 - vertical, vertical) * jnp.where(left, 1.0 - across, across)


def tiles(chan):
    return [(c, slice(c * LANES, (c + 1) * LANES)) for c in range(chan // LANES)]


def column(rows, cols, view, wide, pick_last):
    for c, lanes in tiles(view.shape[1]):
        wide[c] = view[:, lanes].astype(F32)
        first = wide[c, pl.ds(0, rows, stride=cols), :]
        last = wide[c, pl.ds(cols - 1, rows, stride=cols), :]
        yield lanes, jnp.where(pick_last, last, first), jnp.where(pick_last, first, last)


def columns_kernel(rows, cols, view, col_a, col_b, edge_rows, panel, wide):
    even = lax.rem(lax.axis_index("shard"), 2) == 0
    for lanes, a, b in column(rows, cols, view, wide, even):
        col_a[:, lanes] = a.astype(BF16)
        col_b[:, lanes] = b.astype(BF16)
    edge_rows[0:cols, :] = view[0:cols, :]
    edge_rows[cols : 2 * cols, :] = view[(rows - 1) * cols :, :]
    panel[...] = view[...]


def inner_kernel(rows, cols, view, out, wide):
    even = lax.rem(lax.axis_index("shard"), 2) == 0
    for lanes, a, _ in column(rows, cols, view, wide, even):
        out[:, lanes] = a.astype(BF16)


def pose(shards, raw, enc, is_a):
    me = lax.axis_index("shard")
    is_left = (lax.rem(me, 2) == 0) != is_a
    inside = jnp.where(is_left, me > 0, me < shards - 1)
    return jnp.where(inside, raw[...].astype(F32) + enc[...], 0.0)


def sides(a, b):
    even = lax.rem(lax.axis_index("shard"), 2) == 0
    return jnp.where(even, b, a), jnp.where(even, a, b)


def corners(left, right, at):
    fill = jnp.zeros((14, left.shape[1]), F32)
    return jnp.concatenate([left[at : at + 1], right[at : at + 1], fill], axis=0)


def edges_kernel(rows, cols, shards, pick, edge_rows, got_a, got_b, enc, *outs):
    left, right = sides(pose(shards, got_a, enc, True), pose(shards, got_b, enc, False))
    lines = []
    for i, h in ((0, 0), (1, rows - 1)):
        row = edge_rows[i * cols : (i + 1) * cols, :].astype(F32) + enc[h : h + 1, :]
        lines.append(jnp.concatenate([row, corners(left, right, h)], axis=0))
    if pick:
        outs[0][...] = jnp.where(lax.axis_index(pick) == 0, lines[1], lines[0]).astype(BF16)
    else:
        outs[0][...] = lines[0].astype(BF16)
        outs[1][...] = lines[1].astype(BF16)


def strip_kernel(rows, shards, got_a, got_b, enc, *refs):
    out, at = refs[-1], rows
    out[0:rows, :] = pose(shards, got_b, enc, False).astype(BF16)
    for ref in refs[:-1]:
        out[at : at + ref.shape[0], :] = ref[...]
        at += ref.shape[0]


def relay_kernel(strip, far_a, out):
    size = strip.shape[0]
    out[0:size, :] = strip[...]
    out[size:, :] = far_a[...]


def neighbours(rows, cols, shards, pick, enc, strip, raw_a):
    extra = cols + 16
    size = extra if pick else 2 * extra
    lines = strip[rows : rows + size, :].astype(F32)
    if pick:
        first = lax.axis_index(pick) == 0
        zero = jnp.zeros_like(lines)
        both = jnp.where(first, zero, lines), jnp.where(first, lines, zero)
    else:
        both = lines[0:extra], lines[extra:]
    before, after = (
        jnp.concatenate([x[cols : cols + 1], x[0:cols], x[cols + 1 : cols + 2]], axis=0) for x in both
    )
    posed_a = pose(shards, raw_a, enc, True).astype(BF16).astype(F32)
    return posed_a, strip[0:rows, :].astype(F32), before, after


def where_of(k, chan):
    index = jnp.bitwise_xor(lax.axis_index("src"), k)
    return lax.div(index, 2), pl.multiple_of(lax.rem(index, 2) * chan, chan)


def inside(rows, cols, k, coords, view, enc, weights, base_in, base, joined, panel):
    weight = blend_weight(coords, jnp.bitwise_xor(lax.axis_index("src"), k))
    chan, width = view.shape[1], joined.shape[1]
    pixels = rows * cols
    for h in range(rows):
        here = slice(h * cols, (h + 1) * cols)
        posed = (view[here, :].astype(F32) + enc[h : h + 1, :]).astype(BF16)
        part = weight * posed.astype(F32)
        base[here, :] = part if base_in is None else base_in[here, :] + part
        panel[here, :] = posed
    group, at = where_of(k, chan)
    kernel = jnp.concatenate(
        [weights[group, 3 * a + b, pl.ds(at, chan), :] for b in range(3) for a in range(3)], axis=1
    )
    size = pixels // BLOCKS
    taps = jnp.concatenate(
        [
            jnp.dot(panel[i * size : (i + 1) * size, :], kernel, preferred_element_type=F32)
            for i in range(BLOCKS)
        ],
        axis=0,
    )
    column = lax.rem(lax.broadcasted_iota(jnp.int32, (pixels, width), 0), cols)
    zero = jnp.zeros((cols, width), F32)
    total = joined[...]
    for b in (1, 0, 2):
        up, level, down = (taps[:, (3 * b + a) * width : (3 * b + a + 1) * width] for a in range(3))
        part = level + jnp.concatenate([zero, up[: pixels - cols]], axis=0)
        part = part + jnp.concatenate([down[cols:], zero], axis=0)
        if b == 0:
            part = jnp.where(column == 0, 0.0, pltpu.roll(part, 1, 0))
        if b == 2:
            part = jnp.where(column == cols - 1, 0.0, pltpu.roll(part, pixels - 1, 0))
        total = total + part
    joined[...] = total


def add_line(joined, where, line, weights, group, at, taps):
    chan, count = line.shape[1], line.shape[0] - 2
    wide = jnp.concatenate([line[i : i + count] for i in range(3)], axis=1).astype(BF16)
    kernel = jnp.concatenate([weights[group, tap, pl.ds(at, chan), :] for tap in taps], axis=0)
    joined[where, :] += jnp.dot(wide, kernel, preferred_element_type=F32)


def add_columns(rows, cols, joined, weights, a, a_view, b, b_view):
    even = lax.rem(lax.axis_index("shard"), 2) == 0
    chan = a.shape[1]
    group, at_a = where_of(a_view, chan)
    at_b = where_of(b_view, chan)[1]
    zero = jnp.zeros((1, chan), F32)
    left, right = sides(a, b)
    at_left = pl.multiple_of(jnp.where(even, at_b, at_a), chan)
    at_right = pl.multiple_of(jnp.where(even, at_a, at_b), chan)
    for side, tap, start, at in ((left, 0, 0, at_left), (right, 2, cols - 1, at_right)):
        line = jnp.concatenate([zero, side, zero], axis=0)
        where = pl.ds(start, rows, stride=cols)
        add_line(joined, where, line, weights, group, at, [3 * i + tap for i in range(3)])


def add_rows(rows, cols, pick, joined, weights, view, before, after):
    group, at = where_of(view, before.shape[1])
    if pick:
        first = lax.axis_index(pick) == 0
        places = [(before + after, jnp.where(first, rows - 1, 0), jnp.where(first, 6, 0))]
    else:
        places = [(before, 0, 0), (after, rows - 1, 6)]
    for line, h, tap in places:
        where = pl.ds(pl.multiple_of(h * cols, cols), cols)
        add_line(joined, where, line, weights, group, at, [tap + i for i in range(3)])


def silu(x):
    return x / (1.0 + jnp.exp(-x))


def own_kernel(rows, cols, shards, pick, coords, own, enc, strip, got_a, weights, base, joined, panel):
    a, b, before, after = neighbours(rows, cols, shards, pick, enc, strip, got_a)
    joined[...] = jnp.zeros_like(joined)
    inside(rows, cols, 0, coords, own, enc, weights, None, base, joined, panel)
    add_columns(rows, cols, joined, weights, a, 0, b, 0)
    add_rows(rows, cols, pick, joined, weights, 0, before, after)


def middle_kernel(rows, cols, shards, pick, coords, near, far, enc, near_strip, last_strip, near_a,
                  far_a, weights, base_in, joined_in, base, joined, panel):
    me = lax.axis_index("src")
    width = joined.shape[1]
    a, b, before, after = neighbours(rows, cols, shards, pick, enc, near_strip, near_a)
    joined[...] = joined_in[...]
    inside(rows, cols, 1, coords, near, enc, weights, base_in, base, joined, panel)
    add_columns(rows, cols, joined, weights, a, 1, b, 1)
    add_rows(rows, cols, pick, joined, weights, 1, before, after)
    here = pl.ds(pl.multiple_of(lax.div(me, 2) * width, width), width)
    base[:, here] = base[:, here] + silu(joined[...])
    a, b, before, after = neighbours(rows, cols, shards, pick, enc, last_strip, far_a)
    joined[...] = jnp.zeros_like(joined)
    inside(rows, cols, 3, coords, far, enc, weights, base, base, joined, panel)
    add_columns(rows, cols, joined, weights, a, 3, b, 2)
    add_rows(rows, cols, pick, joined, weights, 2, before, after)


def last_kernel(rows, cols, coords, last, enc, weights, base_in, joined_in, base, joined, panel):
    joined[...] = joined_in[...]
    inside(rows, cols, 2, coords, last, enc, weights, base_in, base, joined, panel)


def rim_kernel(rows, cols, shards, pick, enc, relayed, weights, base, joined_in, out, joined):
    chan, width = out.shape[1], joined.shape[1]
    size = relayed.shape[0] - rows
    last_a, b, before, after = neighbours(
        rows, cols, shards, pick, enc, relayed.at[0:size], relayed.at[size : size + rows]
    )
    joined[...] = joined_in[...]
    add_columns(rows, cols, joined, weights, last_a, 2, b, 3)
    add_rows(rows, cols, pick, joined, weights, 3, before, after)
    group = where_of(2, chan)[0]
    added = silu(joined[...])
    for c, lanes in tiles(chan):
        here = group == c * LANES // width
        out[:, lanes] = (base[:, lanes] + jnp.where(here, added, 0.0)).astype(BF16)


def shape(rows, chan, dtype=BF16):
    return jax.ShapeDtypeStruct((rows, chan), dtype)


def call(kernel, ins, outs, scratch=(), cost=None):
    return pl.pallas_call(
        kernel,
        out_shape=outs,
        in_specs=[VMEM_SPEC] * len(ins),
        out_specs=jax.tree.map(lambda _: VMEM_SPEC, outs),
        scratch_shapes=list(scratch),
        compiler_params=pltpu.CompilerParams(vmem_limit_bytes=32 * 1024 * 1024),
        cost_estimate=cost,
    )(*ins)


def local(src_feat, coords, offsets, weights):
    _, rows, cols, chan = src_feat.shape
    pixels = rows * cols
    width = weights.shape[4]
    own = src_feat.reshape(pixels, chan)

    def across(array, k):
        return lax.ppermute(array, "src", [(i, i ^ k) for i in range(4)])

    far = across(own, 3)
    near = across(own, 1)
    rowpos = offsets[0] + jnp.arange(rows, dtype=jnp.int32)
    enc = encoding(rowpos, chan)

    line = shape(rows, chan)
    col_a, col_b, edge_rows, panel = call(
        functools.partial(columns_kernel, rows, cols),
        [own],
        [line, line, shape(2 * cols, chan), shape(pixels, chan)],
        [pltpu.VMEM((chan // LANES, pixels, LANES), F32)],
    )
    place = jnp.broadcast_to(coords.astype(F32).reshape(2, 1), (2, chan))
    shards, slabs = lax.axis_size("shard"), lax.axis_size("slab")

    def swap(array, first):
        pairs = [(i, i + 1) for i in range(first, shards - 1, 2)]
        return lax.ppermute(array, "shard", pairs + [(j, i) for i, j in pairs])

    got_b, got_a = swap(col_b, 1), swap(col_a, 0)
    pick = "slab" if slabs == 2 else None
    edge = shape(cols + 16, chan)
    edges = call(
        functools.partial(edges_kernel, rows, cols, shards, pick),
        [edge_rows, got_a, got_b, enc],
        [edge] if pick else [edge, edge],
    )
    if pick:
        beyond = [lax.ppermute(edges[0], "slab", [(0, 1), (1, 0)])]
    else:
        up = [(i, i + 1) for i in range(slabs - 1)]
        beyond = [
            lax.ppermute(edges[1], "slab", up),
            lax.ppermute(edges[0], "slab", [(j, i) for i, j in up]),
        ]
    strip = call(
        functools.partial(strip_kernel, rows, shards),
        [got_a, got_b, enc, *beyond],
        [shape(rows + len(beyond) * (cols + 16), chan)],
    )[0]
    near_strip, last_strip = across(strip, 1), across(strip, 2)
    far, panel = lax.optimization_barrier((far, panel))
    last = across(far, 1)

    def beside(view):
        out = call(
            functools.partial(inner_kernel, rows, cols),
            [view],
            [line],
            [pltpu.VMEM((chan // LANES, pixels, LANES), F32)],
        )[0]
        return swap(out, 0)

    far_a = beside(far)

    scratch = [pltpu.VMEM((pixels, chan), BF16)]
    sums = [shape(pixels, chan, F32), shape(pixels, width, F32)]
    cost = pl.CostEstimate(flops=5_000_000_000, bytes_accessed=4_000_000, transcendentals=0)
    base, joined = call(
        functools.partial(own_kernel, rows, cols, shards, pick),
        [place, panel, enc, strip, got_a, weights[0]],
        sums,
        scratch,
        cost=cost,
    )
    last_strip, base = lax.optimization_barrier((last_strip, base))
    near, base, near_strip, far_a = lax.optimization_barrier((near, base, near_strip, far_a))
    relayed = call(
        relay_kernel, [last_strip, far_a], [shape(strip.shape[0] + rows, chan)]
    )[0]
    relayed = across(relayed, 1)
    near_a = beside(near)
    base, joined = call(
        functools.partial(middle_kernel, rows, cols, shards, pick),
        [place, near, far, enc, near_strip, last_strip, near_a, far_a, weights[0], base, joined],
        sums,
        scratch,
        cost=pl.CostEstimate(flops=0, bytes_accessed=0, transcendentals=0),
    )
    base, joined = call(
        functools.partial(last_kernel, rows, cols),
        [place, last, enc, weights[0], base, joined],
        sums,
        scratch,
        cost=pl.CostEstimate(flops=0, bytes_accessed=0, transcendentals=0),
    )
    out = call(
        functools.partial(rim_kernel, rows, cols, shards, pick),
        [enc, relayed, weights[0], base, joined],
        [shape(pixels, chan)],
        [pltpu.VMEM((pixels, width), F32)],
    )[0]
    return out.reshape(1, rows, cols, chan)


def solution(mesh):
    in_specs = (
        P("src", "slab", "shard", None),
        P("src", None),
        P("slab"),
        P("src", None, None, None, None),
    )
    out_specs = P("src", "slab", "shard", None)
    return jax.shard_map(local, mesh=mesh, in_specs=in_specs, out_specs=out_specs, check_vma=False)
```

time: 27.3 us -> 26.3 us (0.963)
  waiting for transfers between devices: 8.25 us -> 3.34 us
  starting transfers between devices: 10.7 us -> 14.6 us
    ppermute x6, waiting for transfers between devices: 5.59 us -> 0.58 us  [across(): return lax.ppermute(array, 'src', [(i, i ^ k) for i in range(4)])]
    ppermute x6, starting transfers between devices: 8.15 us -> 12.1 us  [across(): return lax.ppermute(array, 'src', [(i, i ^ k) for i in range(4)])]
    pallas_call x8 -> x10, Pallas kernels: 3.82 us -> 3.6 us  [call(): pl.pallas_call(kernel, out_shape=outs, in_specs=[VMEM_SPEC] * len(ins), o...]
    ppermute x3 -> x4, waiting for transfers between devices: 1.06 us -> 1.18 us  [swap(): return lax.ppermute(array, 'shard', pairs + [(j, i) for i, j in pairs])]
    ppermute x3 -> x4, starting transfers between devices: 0.95 us -> 0.89 us  [swap(): return lax.ppermute(array, 'shard', pairs + [(j, i) for i, j in pairs])]
  transfers between devices with their start and end apart: 10 -> 11, of which waited for: 4 -> 4; matrix products, arithmetic and copies ran while one was open for 3% -> 4% of each run, Pallas kernels for 9% -> 10%
where the time goes in v7:
time: 26.3 us; the launch traced here: 25.9 us
  starting transfers between devices  14.6 us (56%)
  Pallas kernels  3.6 us (14%)
  waiting for transfers between devices  3.34 us (13%)
  local copies, waits for them, and re-layouts  2.75 us (10%)
  other arithmetic  0.86 us (3%)
  between operations  0.78 us (3%)
    ppermute x6, starting transfers between devices, across(): return lax.ppermute(array, 'src', [(i, i ^ k) for i in range(4)])  12.1 us
    pallas_call x10, Pallas kernels, call(): pl.pallas_call(kernel, out_shape=outs, in_specs=[VMEM_SPEC] * len(ins), o...  3.6 us
    unnamed x6, local copies, waits for them, and re-layouts  2.68 us
    ppermute x1, waiting for transfers between devices, local(): beyond = [lax.ppermute(edges[0], 'slab', [(0, 1), (1, 0)])]  1.59 us
    ppermute x1, starting transfers between devices, local(): beyond = [lax.ppermute(edges[0], 'slab', [(0, 1), (1, 0)])]  1.56 us
    ppermute x4, waiting for transfers between devices, swap(): return lax.ppermute(array, 'shard', pairs + [(j, i) for i, j in pairs])  1.18 us
    ppermute x4, starting transfers between devices, swap(): return lax.ppermute(array, 'shard', pairs + [(j, i) for i, j in pairs])  0.89 us
    broadcast_in_dim x1, other arithmetic, local(): place = jnp.broadcast_to(coords.astype(F32).reshape(2, 1), (2, chan))  0.66 us
  transfers between devices with their start and end apart: 11, of which 4 were waited for; matrix products, arithmetic and copies ran while one was open for 4% of the time, Pallas kernels for 10%

profile of v7, /device:TPU:0, one launch (start us, length us, event | category | flops | bytes accessed | tf_op | source)
XLA Modules:
  0.0 25.9 jit_solution(1765050625982443500)
XLA Ops:
  0.0 5.0 %collective-permute-start.4 = (bf16[512,256]{1,0:T(8,128)(2,1)}, bf16[512,256]{1,0:T(8,128)(2,1)S(1)}, u32[]{:S(2)}, u32[]{:S(2)}) collective-permute-start(bf16[512,256]{1,0:T(8,128)(2,1)} %bitcast.11), channel_id=1, source_target_pairs={{0,24},{8,16},{16,8},{24,0},{1,25},{9,17},{17,9},{25,1},{2,26},{10... | collective-permute-start | bytes 786440 | tf_op jit(solution)/shard_map/ppermute | solution.py:270
  5.0 0.0 collective-permute-start.5
  5.1 0.0 copy-start.2
  5.1 1.0 %copy-done.2 = bf16[1,32,16,256]{3,2,1,0:T(8,128)(2,1)S(1)} copy-done((bf16[1,32,16,256]{3,2,1,0:T(8,128)(2,1)S(1)}, bf16[1,32,16,256]{3,2,1,0:T(8,128)(2,1)}, u32[]{:S(2)}) %copy-start.2) | copy-done | bytes 262168
  6.1 0.1 shard_map.46
  6.1 0.1 collective-permute-start
  6.2 0.7 %collective-permute-start.1 = (bf16[32,256]{1,0:T(8,128)(2,1)S(1)}, bf16[32,256]{1,0:T(8,128)(2,1)S(1)}, u32[]{:S(2)}, u32[]{:S(2)}) collective-permute-start(bf16[32,256]{1,0:T(8,128)(2,1)S(1)} %get-tuple-element.24), channel_id=1, source_target_pairs={{2,4},{4,2},{3,5},{5,3},{10,12},{12,10},{11,13},{13,11},{18,20},{2... | collective-permute-start | bytes 49160 | tf_op jit(solution)/shard_map/ppermute | solution.py:289
  7.6 0.2 add_sine_fusion.enc
  7.8 0.0 collective-permute-done.got_a
  7.8 0.0 collective-permute-done.1.got_b
  7.8 1.6 %collective-permute-start.2 = (bf16[32,256]{1,0:T(8,128)(2,1)S(1)}, bf16[32,256]{1,0:T(8,128)(2,1)S(1)}, u32[]{:S(2)}, u32[]{:S(2)}) collective-permute-start(bf16[32,256]{1,0:T(8,128)(2,1)S(1)} %shard_map.47), channel_id=1, source_target_pairs={{0,1},{1,0},{2,3},{3,2},{4,5},{5,4},{6,7},{7,6},{8,9},{9,8},{10,11... | collective-permute-start | bytes 49160 | tf_op jit(solution)/shard_map/ppermute | solution.py:300
  9.4 0.7 %convert_bitcast_fusion = f32[2]{0:T(128)S(1)} fusion(s32[1,2]{1,0:T(1,128)} %param.5), kind=kLoop, calls=%fused_computation.13 | loop fusion | flops 2 | bytes 16 | tf_op jit(solution)/shard_map/broadcast_in_dim | solution.py:284
  10.0 1.6 %collective-permute-done.2.refs_0_ = bf16[32,256]{1,0:T(8,128)(2,1)S(1)} collective-permute-done((bf16[32,256]{1,0:T(8,128)(2,1)S(1)}, bf16[32,256]{1,0:T(8,128)(2,1)S(1)}, u32[]{:S(2)}, u32[]{:S(2)}) %collective-permute-start.2) | collective-permute-done | bytes 16416 | tf_op jit(solution)/shard_map/ppermute | solution.py:300
  11.6 0.6 %collective-permute-start.3 = (bf16[64,256]{1,0:T(8,128)(2,1)S(1)}, bf16[64,256]{1,0:T(8,128)(2,1)S(1)}, u32[]{:S(2)}, u32[]{:S(2)}) collective-permute-start(bf16[64,256]{1,0:T(8,128)(2,1)S(1)} %shard_map.48.strip), channel_id=1, source_target_pairs={{0,16},{8,24},{16,0},{24,8},{1,17},{9,25},{17,1},{25,9},{2,18},{10... | collective-permute-start | bytes 98312 | tf_op jit(solution)/shard_map/ppermute | solution.py:270
  12.2 1.5 %collective-permute-start.6 = (bf16[64,256]{1,0:T(8,128)(2,1)S(1)}, bf16[64,256]{1,0:T(8,128)(2,1)S(1)}, u32[]{:S(2)}, u32[]{:S(2)}) collective-permute-start(bf16[64,256]{1,0:T(8,128)(2,1)S(1)} %shard_map.48.strip), channel_id=1, source_target_pairs={{0,8},{8,0},{16,24},{24,16},{1,9},{9,1},{17,25},{25,17},{2,10},{10... | collective-permute-start | bytes 98312 | tf_op jit(solution)/shard_map/ppermute | solution.py:270
  13.8 0.0 collective-permute-done.4.view.far
  13.8 0.1 shard_map.50
  13.8 3.2 %collective-permute-start.9 = (bf16[512,256]{1,0:T(8,128)(2,1)S(1)}, bf16[512,256]{1,0:T(8,128)(2,1)S(1)}, u32[]{:S(2)}, u32[]{:S(2)}) collective-permute-start(bf16[512,256]{1,0:T(8,128)(2,1)S(1)} %collective-permute-done.4.view.far), channel_id=1, source_target_pairs={{0,8},{8,0},{16,24},{24,16},{1,9},{9,1},{17,25},{25,17},{2,10},{10... | collective-permute-start | bytes 786440 | tf_op jit(solution)/shard_map/ppermute | solution.py:270
  17.0 0.1 collective-permute-start.7
  17.1 0.1 broadcast_in_dim.5.coords
  17.2 0.0 copy-start
  17.2 1.7 %copy-done = bf16[1,2,9,512,128]{4,3,2,1,0:T(8,128)(2,1)S(1)} copy-done((bf16[1,2,9,512,128]{4,3,2,1,0:T(8,128)(2,1)S(1)}, bf16[1,2,9,512,128]{4,3,2,1,0:T(8,128)(2,1)}, u32[]{:S(2)}) %copy-start) | copy-done | bytes 2359320
  18.9 0.0 copy-start.1
  18.9 0.6 %shard_map.49 = (f32[512,256]{1,0:T(8,128)S(1)}, f32[512,128]{1,0:T(8,128)S(1)}) custom-call(f32[2,256]{1,0:T(2,128)S(1)} %broadcast_in_dim.5.coords, bf16[512,256]{1,0:T(8,128)(2,1)S(1)} %get-tuple-element.27.own, f32[32,256]{1,0:T(8,128)S(1)} %add_sine_fusion.enc, bf16[64,256]{1,0:T(8,128)(2,1)S(1)} %shard_map.48.strip, ...), custom_call_target="tpu_custom_call" | custom-call | flops 5000000000 | bytes 4000000 | tf_op jit(solution)/shard_map/pallas_call | solution.py:252
  19.5 0.0 collective-permute-done.3.strip.last_strip
  19.5 0.0 collective-permute-done.6.near_strip
  19.5 0.0 collective-permute-done.5.view.near
  19.5 0.0 collective-permute-done.7.far_a
  19.5 1.7 %collective-permute-start.8 = (bf16[96,256]{1,0:T(8,128)(2,1)S(1)}, bf16[96,256]{1,0:T(8,128)(2,1)S(1)}, u32[]{:S(2)}, u32[]{:S(2)}) collective-permute-start(bf16[96,256]{1,0:T(8,128)(2,1)S(1)} %shard_map.51), channel_id=1, source_target_pairs={{0,8},{8,0},{16,24},{24,16},{1,9},{9,1},{17,25},{25,17},{2,10},{10... | collective-permute-start | bytes 147464 | tf_op jit(solution)/shard_map/ppermute | solution.py:270
  21.2 0.1 shard_map.52
  21.3 0.1 collective-permute-start.10
  21.4 1.2 %collective-permute-done.10.near_a = bf16[32,256]{1,0:T(8,128)(2,1)S(1)} collective-permute-done((bf16[32,256]{1,0:T(8,128)(2,1)S(1)}, bf16[32,256]{1,0:T(8,128)(2,1)S(1)}, u32[]{:S(2)}, u32[]{:S(2)}) %collective-permute-start.10) | collective-permute-done | bytes 16416 | tf_op jit(solution)/shard_map/ppermute | solution.py:289
  22.5 0.0 copy-done.1
  22.5 1.2 %shard_map.53 = (f32[512,256]{1,0:T(8,128)S(1)}, f32[512,128]{1,0:T(8,128)S(1)}) custom-call(f32[2,256]{1,0:T(2,128)S(1)} %broadcast_in_dim.5.coords, bf16[512,256]{1,0:T(8,128)(2,1)S(1)} %collective-permute-done.5.view.near, bf16[512,256]{1,0:T(8,128)(2,1)S(1)} %collective-permute-done.4.view.far, f32[32,256]{1,0:T(8,128)S(1)} %add_sine_fusion.enc, ...), custom_call_target="tpu_custom_call" | custom-call | tf_op jit(solution)/shard_map/pallas_call | solution.py:252
  23.8 0.1 collective-permute-done.9.last
  23.8 0.5 %shard_map.54 = (f32[512,256]{1,0:T(8,128)S(1)}, f32[512,128]{1,0:T(8,128)S(1)}) custom-call(f32[2,256]{1,0:T(2,128)S(1)} %broadcast_in_dim.5.coords, bf16[512,256]{1,0:T(8,128)(2,1)S(1)} %collective-permute-done.9.last, f32[32,256]{1,0:T(8,128)S(1)} %add_sine_fusion.enc, bf16[2,9,512,128]{3,2,1,0:T(8,128)(2,1)S(1)} %bitcast.9, ...), custom_call_target="tpu_custom_call" | custom-call | tf_op jit(solution)/shard_map/pallas_call | solution.py:252
  24.4 0.5 %collective-permute-done.8.relayed = bf16[96,256]{1,0:T(8,128)(2,1)S(1)} collective-permute-done((bf16[96,256]{1,0:T(8,128)(2,1)S(1)}, bf16[96,256]{1,0:T(8,128)(2,1)S(1)}, u32[]{:S(2)}, u32[]{:S(2)}) %collective-permute-start.8) | collective-permute-done | bytes 49184 | tf_op jit(solution)/shard_map/ppermute | solution.py:270
  24.9 1.0 %shard_map.55 = bf16[512,256]{1,0:T(8,128)(2,1)} custom-call(f32[32,256]{1,0:T(8,128)S(1)} %add_sine_fusion.enc, bf16[96,256]{1,0:T(8,128)(2,1)S(1)} %collective-permute-done.8.relayed, bf16[2,9,512,128]{3,2,1,0:T(8,128)(2,1)S(1)} %bitcast.10, f32[512,256]{1,0:T(8,128)S(1)} %get-tuple-element.39.base, f32[512,128]{1,0:T(8,128)S(1)} %get-tuple-element.40.joined_in), custom_call_target="tpu_custom_call" | custom-call | tf_op jit(solution)/shard_map/pallas_call | solution.py:252
  (5 shorter events, 0.1 us)
Async XLA Ops:
  0.0 13.8 %collective-permute-start.4 = (bf16[512,256]{1,0:T(8,128)(2,1)}, bf16[512,256]{1,0:T(8,128)(2,1)S(1)}, u32[]{:S(2)}, u32[]{:S(2)}) collective-permute-start(bf16[512,256]{1,0:T(8,128)(2,1)} %bitcast.11), channel_id=1, source_target_pairs={{0,24},{8,16},{16,8},{24,0},{1,25},{9,17},{17,9},{25,1},{2,26},{10... | collective-permute-start | bytes 786440 | tf_op jit(solution)/shard_map/ppermute | solution.py:270
  5.0 14.4 %collective-permute-start.5 = (bf16[512,256]{1,0:T(8,128)(2,1)}, bf16[512,256]{1,0:T(8,128)(2,1)S(1)}, u32[]{:S(2)}, u32[]{:S(2)}) collective-permute-start(bf16[512,256]{1,0:T(8,128)(2,1)} %bitcast.12), channel_id=1, source_target_pairs={{0,8},{8,0},{16,24},{24,16},{1,9},{9,1},{17,25},{25,17},{2,10},{10... | collective-permute-start | bytes 786440 | tf_op jit(solution)/shard_map/ppermute | solution.py:270
  5.1 1.0 %copy-start.2 = (bf16[1,32,16,256]{3,2,1,0:T(8,128)(2,1)S(1)}, bf16[1,32,16,256]{3,2,1,0:T(8,128)(2,1)}, u32[]{:S(2)}) copy-start(bf16[1,32,16,256]{3,2,1,0:T(8,128)(2,1)} %param.4) | copy-start | bytes 786436
  6.1 1.6 %collective-permute-start = (bf16[32,256]{1,0:T(8,128)(2,1)S(1)}, bf16[32,256]{1,0:T(8,128)(2,1)S(1)}, u32[]{:S(2)}, u32[]{:S(2)}) collective-permute-start(bf16[32,256]{1,0:T(8,128)(2,1)S(1)} %get-tuple-element.23), channel_id=1, source_target_pairs={{0,2},{4,6},{2,0},{6,4},{1,3},{5,7},{3,1},{7,5},{8,10},{12,14},{10... | collective-permute-start | bytes 49160 | tf_op jit(solution)/shard_map/ppermute | solution.py:289
  6.2 1.6 %collective-permute-start.1 = (bf16[32,256]{1,0:T(8,128)(2,1)S(1)}, bf16[32,256]{1,0:T(8,128)(2,1)S(1)}, u32[]{:S(2)}, u32[]{:S(2)}) collective-permute-start(bf16[32,256]{1,0:T(8,128)(2,1)S(1)} %get-tuple-element.24), channel_id=1, source_target_pairs={{2,4},{4,2},{3,5},{5,3},{10,12},{12,10},{11,13},{13,11},{18,20},{2... | collective-permute-start | bytes 49160 | tf_op jit(solution)/shard_map/ppermute | solution.py:289
  7.8 3.8 %collective-permute-start.2 = (bf16[32,256]{1,0:T(8,128)(2,1)S(1)}, bf16[32,256]{1,0:T(8,128)(2,1)S(1)}, u32[]{:S(2)}, u32[]{:S(2)}) collective-permute-start(bf16[32,256]{1,0:T(8,128)(2,1)S(1)} %shard_map.47), channel_id=1, source_target_pairs={{0,1},{1,0},{2,3},{3,2},{4,5},{5,4},{6,7},{7,6},{8,9},{9,8},{10,11... | collective-permute-start | bytes 49160 | tf_op jit(solution)/shard_map/ppermute | solution.py:300
  11.6 7.8 %collective-permute-start.3 = (bf16[64,256]{1,0:T(8,128)(2,1)S(1)}, bf16[64,256]{1,0:T(8,128)(2,1)S(1)}, u32[]{:S(2)}, u32[]{:S(2)}) collective-permute-start(bf16[64,256]{1,0:T(8,128)(2,1)S(1)} %shard_map.48.strip), channel_id=1, source_target_pairs={{0,16},{8,24},{16,0},{24,8},{1,17},{9,25},{17,1},{25,9},{2,18},{10... | collective-permute-start | bytes 98312 | tf_op jit(solution)/shard_map/ppermute | solution.py:270
  12.2 7.2 %collective-permute-start.6 = (bf16[64,256]{1,0:T(8,128)(2,1)S(1)}, bf16[64,256]{1,0:T(8,128)(2,1)S(1)}, u32[]{:S(2)}, u32[]{:S(2)}) collective-permute-start(bf16[64,256]{1,0:T(8,128)(2,1)S(1)} %shard_map.48.strip), channel_id=1, source_target_pairs={{0,8},{8,0},{16,24},{24,16},{1,9},{9,1},{17,25},{25,17},{2,10},{10... | collective-permute-start | bytes 98312 | tf_op jit(solution)/shard_map/ppermute | solution.py:270
  13.8 10.0 %collective-permute-start.9 = (bf16[512,256]{1,0:T(8,128)(2,1)S(1)}, bf16[512,256]{1,0:T(8,128)(2,1)S(1)}, u32[]{:S(2)}, u32[]{:S(2)}) collective-permute-start(bf16[512,256]{1,0:T(8,128)(2,1)S(1)} %collective-permute-done.4.view.far), channel_id=1, source_target_pairs={{0,8},{8,0},{16,24},{24,16},{1,9},{9,1},{17,25},{25,17},{2,10},{10... | collective-permute-start | bytes 786440 | tf_op jit(solution)/shard_map/ppermute | solution.py:270
  17.0 2.5 %collective-permute-start.7 = (bf16[32,256]{1,0:T(8,128)(2,1)S(1)}, bf16[32,256]{1,0:T(8,128)(2,1)S(1)}, u32[]{:S(2)}, u32[]{:S(2)}) collective-permute-start(bf16[32,256]{1,0:T(8,128)(2,1)S(1)} %shard_map.50), channel_id=1, source_target_pairs={{0,2},{4,6},{2,0},{6,4},{1,3},{5,7},{3,1},{7,5},{8,10},{12,14},{10... | collective-permute-start | bytes 49160 | tf_op jit(solution)/shard_map/ppermute | solution.py:289
  17.2 1.7 %copy-start = (bf16[1,2,9,512,128]{4,3,2,1,0:T(8,128)(2,1)S(1)}, bf16[1,2,9,512,128]{4,3,2,1,0:T(8,128)(2,1)}, u32[]{:S(2)}) copy-start(bf16[1,2,9,512,128]{4,3,2,1,0:T(8,128)(2,1)} %param.7) | copy-start | bytes 7077892
  18.9 3.7 %copy-start.1 = (bf16[1,2,9,512,128]{4,3,2,1,0:T(8,128)(2,1)S(1)}, bf16[1,2,9,512,128]{4,3,2,1,0:T(8,128)(2,1)}, u32[]{:S(2)}) copy-start(bf16[1,2,9,512,128]{4,3,2,1,0:T(8,128)(2,1)} %param.7) | copy-start | bytes 7077892
  19.5 5.4 %collective-permute-start.8 = (bf16[96,256]{1,0:T(8,128)(2,1)S(1)}, bf16[96,256]{1,0:T(8,128)(2,1)S(1)}, u32[]{:S(2)}, u32[]{:S(2)}) collective-permute-start(bf16[96,256]{1,0:T(8,128)(2,1)S(1)} %shard_map.51), channel_id=1, source_target_pairs={{0,8},{8,0},{16,24},{24,16},{1,9},{9,1},{17,25},{25,17},{2,10},{10... | collective-permute-start | bytes 147464 | tf_op jit(solution)/shard_map/ppermute | solution.py:270
  21.3 1.2 %collective-permute-start.10 = (bf16[32,256]{1,0:T(8,128)(2,1)S(1)}, bf16[32,256]{1,0:T(8,128)(2,1)S(1)}, u32[]{:S(2)}, u32[]{:S(2)}) collective-permute-start(bf16[32,256]{1,0:T(8,128)(2,1)S(1)} %shard_map.52), channel_id=1, source_target_pairs={{0,2},{4,6},{2,0},{6,4},{1,3},{5,7},{3,1},{7,5},{8,10},{12,14},{10... | collective-permute-start | bytes 49160 | tf_op jit(solution)/shard_map/ppermute | solution.py:289

commit v8 on v7

--- a/solution.py
+++ b/solution.py
@@ -308,6 +308,7 @@
         functools.partial(strip_kernel, rows, shards),
         [got_a, got_b, enc, *beyond],
         [shape(rows + len(beyond) * (cols + 16), chan)],
+        cost=pl.CostEstimate(flops=2000000000, bytes_accessed=0, transcendentals=0),
     )[0]
     near_strip, last_strip = across(strip, 1), across(strip, 2)
     far, panel = lax.optimization_barrier((far, panel))
@@ -322,11 +323,10 @@
         )[0]
         return swap(out, 0)
 
-    far_a = beside(far)
 
     scratch = [pltpu.VMEM((pixels, chan), BF16)]
     sums = [shape(pixels, chan, F32), shape(pixels, width, F32)]
-    cost = pl.CostEstimate(flops=5_000_000_000, bytes_accessed=4_000_000, transcendentals=0)
+    cost = pl.CostEstimate(flops=5000000000, bytes_accessed=4_000_000, transcendentals=0)
     base, joined = call(
         functools.partial(own_kernel, rows, cols, shards, pick),
         [place, panel, enc, strip, got_a, weights[0]],
@@ -334,13 +334,14 @@
         scratch,
         cost=cost,
     )
-    last_strip, base = lax.optimization_barrier((last_strip, base))
-    near, base, near_strip, far_a = lax.optimization_barrier((near, base, near_strip, far_a))
+    near, far, base = lax.optimization_barrier((near, far, base))
+    far_a, near_a = beside(far), beside(near)
+    near_a, far_a, last_strip = lax.optimization_barrier((near_a, far_a, last_strip))
+    near_strip, last_strip = lax.optimization_barrier((near_strip, last_strip))
     relayed = call(
         relay_kernel, [last_strip, far_a], [shape(strip.shape[0] + rows, chan)]
     )[0]
     relayed = across(relayed, 1)
-    near_a = beside(near)
     base, joined = call(
         functools.partial(middle_kernel, rows, cols, shards, pick),
         [place, near, far, enc, near_strip, last_strip, near_a, far_a, weights[0], base, joined],

time: 26.3 us -> 26.2 us (level)
  local copies, waits for them, and re-layouts: 2.75 us -> 1.09 us
  waiting for transfers between devices: 3.34 us -> 4.5 us
  starting transfers between devices: 14.6 us -> 15 us
    unnamed x6 -> x4, local copies, waits for them, and re-layouts: 2.68 us -> 1.02 us
    ppermute x6, waiting for transfers between devices: 0.58 us -> 2.07 us  [across(): return lax.ppermute(array, 'src', [(i, i ^ k) for i in range(4)])]
    ppermute x4, starting transfers between devices: 0.89 us -> 1.37 us  [swap(): return lax.ppermute(array, 'shard', pairs + [(j, i) for i, j in pairs])]
    ppermute x4, waiting for transfers between devices: 1.18 us -> 0.84 us  [swap(): return lax.ppermute(array, 'shard', pairs + [(j, i) for i, j in pairs])]
  transfers between devices with their start and end apart: 11 -> 11, of which waited for: 4 -> 5; matrix products, arithmetic and copies ran while one was open for 4% -> 4% of each run, Pallas kernels for 10% -> 10%
where the time goes in v8:
time: 26.2 us; the launch traced here: 25.8 us
  starting transfers between devices  15 us (57%)
  waiting for transfers between devices  4.5 us (17%)
  Pallas kernels  3.58 us (14%)
  local copies, waits for them, and re-layouts  1.09 us (4%)
  other arithmetic  0.86 us (3%)
  between operations  0.74 us (3%)
    ppermute x6, starting transfers between devices, across(): return lax.ppermute(array, 'src', [(i, i ^ k) for i in range(4)])  12.1 us
    pallas_call x10, Pallas kernels, call(): pl.pallas_call(kernel, out_shape=outs, in_specs=[VMEM_SPEC] * len(ins), o...  3.58 us
    ppermute x6, waiting for transfers between devices, across(): return lax.ppermute(array, 'src', [(i, i ^ k) for i in range(4)])  2.07 us
    ppermute x1, waiting for transfers between devices, local(): beyond = [lax.ppermute(edges[0], 'slab', [(0, 1), (1, 0)])]  1.59 us
    ppermute x1, starting transfers between devices, local(): beyond = [lax.ppermute(edges[0], 'slab', [(0, 1), (1, 0)])]  1.56 us
    ppermute x4, starting transfers between devices, swap(): return lax.ppermute(array, 'shard', pairs + [(j, i) for i, j in pairs])  1.37 us
    unnamed x4, local copies, waits for them, and re-layouts  1.02 us
    ppermute x4, waiting for transfers between devices, swap(): return lax.ppermute(array, 'shard', pairs + [(j, i) for i, j in pairs])  0.84 us
  transfers between devices with their start and end apart: 11, of which 5 were waited for; matrix products, arithmetic and copies ran while one was open for 4% of the time, Pallas kernels for 10%

profile of v8, /device:TPU:0, one launch (start us, length us, event | category | flops | bytes accessed | tf_op | source)
XLA Modules:
  0.0 25.8 jit_solution(14794720812258833334)
XLA Ops:
  0.0 5.0 %collective-permute-start.5 = (bf16[512,256]{1,0:T(8,128)(2,1)}, bf16[512,256]{1,0:T(8,128)(2,1)S(1)}, u32[]{:S(2)}, u32[]{:S(2)}) collective-permute-start(bf16[512,256]{1,0:T(8,128)(2,1)} %bitcast.11), channel_id=1, source_target_pairs={{0,24},{8,16},{16,8},{24,0},{1,25},{9,17},{17,9},{25,1},{2,26},{10... | collective-permute-start | bytes 786440 | tf_op jit(solution)/shard_map/ppermute | solution.py:270
  5.0 0.0 collective-permute-start.4
  5.1 0.0 copy-start.1
  5.1 1.0 %copy-done.1 = bf16[1,32,16,256]{3,2,1,0:T(8,128)(2,1)S(1)} copy-done((bf16[1,32,16,256]{3,2,1,0:T(8,128)(2,1)S(1)}, bf16[1,32,16,256]{3,2,1,0:T(8,128)(2,1)}, u32[]{:S(2)}) %copy-start.1) | copy-done | bytes 262168
  6.1 0.1 shard_map.46
  6.1 0.1 collective-permute-start
  6.2 0.7 %collective-permute-start.1 = (bf16[32,256]{1,0:T(8,128)(2,1)S(1)}, bf16[32,256]{1,0:T(8,128)(2,1)S(1)}, u32[]{:S(2)}, u32[]{:S(2)}) collective-permute-start(bf16[32,256]{1,0:T(8,128)(2,1)S(1)} %get-tuple-element.26), channel_id=1, source_target_pairs={{2,4},{4,2},{3,5},{5,3},{10,12},{12,10},{11,13},{13,11},{18,20},{2... | collective-permute-start | bytes 49160 | tf_op jit(solution)/shard_map/ppermute | solution.py:289
  7.6 0.2 add_sine_fusion.enc
  7.8 0.0 collective-permute-done.got_a
  7.8 0.0 collective-permute-done.1.got_b
  7.8 1.6 %collective-permute-start.2 = (bf16[32,256]{1,0:T(8,128)(2,1)S(1)}, bf16[32,256]{1,0:T(8,128)(2,1)S(1)}, u32[]{:S(2)}, u32[]{:S(2)}) collective-permute-start(bf16[32,256]{1,0:T(8,128)(2,1)S(1)} %shard_map.47), channel_id=1, source_target_pairs={{0,1},{1,0},{2,3},{3,2},{4,5},{5,4},{6,7},{7,6},{8,9},{9,8},{10,11... | collective-permute-start | bytes 49160 | tf_op jit(solution)/shard_map/ppermute | solution.py:300
  9.4 0.7 %convert_bitcast_fusion = f32[2]{0:T(128)S(1)} fusion(s32[1,2]{1,0:T(1,128)} %param.5), kind=kLoop, calls=%fused_computation.13 | loop fusion | flops 2 | bytes 16 | tf_op jit(solution)/shard_map/broadcast_in_dim | solution.py:284
  10.0 0.0 copy-start
  10.0 1.6 %collective-permute-done.2.refs_0_ = bf16[32,256]{1,0:T(8,128)(2,1)S(1)} collective-permute-done((bf16[32,256]{1,0:T(8,128)(2,1)S(1)}, bf16[32,256]{1,0:T(8,128)(2,1)S(1)}, u32[]{:S(2)}, u32[]{:S(2)}) %collective-permute-start.2) | collective-permute-done | bytes 16416 | tf_op jit(solution)/shard_map/ppermute | solution.py:300
  11.6 0.6 %collective-permute-start.8 = (bf16[64,256]{1,0:T(8,128)(2,1)S(1)}, bf16[64,256]{1,0:T(8,128)(2,1)S(1)}, u32[]{:S(2)}, u32[]{:S(2)}) collective-permute-start(bf16[64,256]{1,0:T(8,128)(2,1)S(1)} %shard_map.48.strip), channel_id=1, source_target_pairs={{0,16},{8,24},{16,0},{24,8},{1,17},{9,25},{17,1},{25,9},{2,18},{10... | collective-permute-start | bytes 98312 | tf_op jit(solution)/shard_map/ppermute | solution.py:270
  12.2 1.5 %collective-permute-start.3 = (bf16[64,256]{1,0:T(8,128)(2,1)S(1)}, bf16[64,256]{1,0:T(8,128)(2,1)S(1)}, u32[]{:S(2)}, u32[]{:S(2)}) collective-permute-start(bf16[64,256]{1,0:T(8,128)(2,1)S(1)} %shard_map.48.strip), channel_id=1, source_target_pairs={{0,8},{8,0},{16,24},{24,16},{1,9},{9,1},{17,25},{25,17},{2,10},{10... | collective-permute-start | bytes 98312 | tf_op jit(solution)/shard_map/ppermute | solution.py:270
  13.8 0.0 collective-permute-done.5.view.far
  13.8 3.1 %collective-permute-start.10 = (bf16[512,256]{1,0:T(8,128)(2,1)S(1)}, bf16[512,256]{1,0:T(8,128)(2,1)S(1)}, u32[]{:S(2)}, u32[]{:S(2)}) collective-permute-start(bf16[512,256]{1,0:T(8,128)(2,1)S(1)} %collective-permute-done.5.view.far), channel_id=1, source_target_pairs={{0,8},{8,0},{16,24},{24,16},{1,9},{9,1},{17,25},{25,17},{2,10},{10... | collective-permute-start | bytes 786440 | tf_op jit(solution)/shard_map/ppermute | solution.py:270
  16.9 0.1 broadcast_in_dim.5.coords
  17.0 0.0 copy-done
  17.0 0.6 %shard_map.49 = (f32[512,256]{1,0:T(8,128)S(1)}, f32[512,128]{1,0:T(8,128)S(1)}) custom-call(f32[2,256]{1,0:T(2,128)S(1)} %broadcast_in_dim.5.coords, bf16[512,256]{1,0:T(8,128)(2,1)S(1)} %get-tuple-element.30.own, f32[32,256]{1,0:T(8,128)S(1)} %add_sine_fusion.enc, bf16[64,256]{1,0:T(8,128)(2,1)S(1)} %shard_map.48.strip, ...), custom_call_target="tpu_custom_call" | custom-call | flops 5000000000 | bytes 4000000 | tf_op jit(solution)/shard_map/pallas_call | solution.py:252
  17.6 0.0 collective-permute-done.4.view.near
  17.6 0.1 shard_map.50
  17.7 0.1 collective-permute-start.6
  17.8 0.1 shard_map.51
  17.9 0.5 %collective-permute-start.7 = (bf16[32,256]{1,0:T(8,128)(2,1)S(1)}, bf16[32,256]{1,0:T(8,128)(2,1)S(1)}, u32[]{:S(2)}, u32[]{:S(2)}) collective-permute-start(bf16[32,256]{1,0:T(8,128)(2,1)S(1)} %shard_map.51), channel_id=1, source_target_pairs={{0,2},{4,6},{2,0},{6,4},{1,3},{5,7},{3,1},{7,5},{8,10},{12,14},{10... | collective-permute-start | bytes 49160 | tf_op jit(solution)/shard_map/ppermute | solution.py:289
  18.4 0.0 collective-permute-done.8.strip.last_strip
  18.4 0.5 %collective-permute-done.6.near_a = bf16[32,256]{1,0:T(8,128)(2,1)S(1)} collective-permute-done((bf16[32,256]{1,0:T(8,128)(2,1)S(1)}, bf16[32,256]{1,0:T(8,128)(2,1)S(1)}, u32[]{:S(2)}, u32[]{:S(2)}) %collective-permute-start.6) | collective-permute-done | bytes 16416 | tf_op jit(solution)/shard_map/ppermute | solution.py:289
  18.9 0.3 %collective-permute-done.7.far_a = bf16[32,256]{1,0:T(8,128)(2,1)S(1)} collective-permute-done((bf16[32,256]{1,0:T(8,128)(2,1)S(1)}, bf16[32,256]{1,0:T(8,128)(2,1)S(1)}, u32[]{:S(2)}, u32[]{:S(2)}) %collective-permute-start.7) | collective-permute-done | bytes 16416 | tf_op jit(solution)/shard_map/ppermute | solution.py:289
  19.2 0.0 collective-permute-done.3.near_strip
  19.2 1.7 %collective-permute-start.9 = (bf16[96,256]{1,0:T(8,128)(2,1)S(1)}, bf16[96,256]{1,0:T(8,128)(2,1)S(1)}, u32[]{:S(2)}, u32[]{:S(2)}) collective-permute-start(bf16[96,256]{1,0:T(8,128)(2,1)S(1)} %shard_map.52), channel_id=1, source_target_pairs={{0,8},{8,0},{16,24},{24,16},{1,9},{9,1},{17,25},{25,17},{2,10},{10... | collective-permute-start | bytes 147464 | tf_op jit(solution)/shard_map/ppermute | solution.py:270
  21.0 1.2 %shard_map.53 = (f32[512,256]{1,0:T(8,128)S(1)}, f32[512,128]{1,0:T(8,128)S(1)}) custom-call(f32[2,256]{1,0:T(2,128)S(1)} %broadcast_in_dim.5.coords, bf16[512,256]{1,0:T(8,128)(2,1)S(1)} %collective-permute-done.4.view.near, bf16[512,256]{1,0:T(8,128)(2,1)S(1)} %collective-permute-done.5.view.far, f32[32,256]{1,0:T(8,128)S(1)} %add_sine_fusion.enc, ...), custom_call_target="tpu_custom_call" | custom-call | tf_op jit(solution)/shard_map/pallas_call | solution.py:252
  22.2 1.5 %collective-permute-done.10.last = bf16[512,256]{1,0:T(8,128)(2,1)S(1)} collective-permute-done((bf16[512,256]{1,0:T(8,128)(2,1)S(1)}, bf16[512,256]{1,0:T(8,128)(2,1)S(1)}, u32[]{:S(2)}, u32[]{:S(2)}) %collective-permute-start.10) | collective-permute-done | bytes 262176 | tf_op jit(solution)/shard_map/ppermute | solution.py:270
  23.7 0.5 %shard_map.54 = (f32[512,256]{1,0:T(8,128)S(1)}, f32[512,128]{1,0:T(8,128)S(1)}) custom-call(f32[2,256]{1,0:T(2,128)S(1)} %broadcast_in_dim.5.coords, bf16[512,256]{1,0:T(8,128)(2,1)S(1)} %collective-permute-done.10.last, f32[32,256]{1,0:T(8,128)S(1)} %add_sine_fusion.enc, bf16[2,9,512,128]{3,2,1,0:T(8,128)(2,1)S(1)} %bitcast.9, ...), custom_call_target="tpu_custom_call" | custom-call | tf_op jit(solution)/shard_map/pallas_call | solution.py:252
  24.2 0.5 %collective-permute-done.9.relayed = bf16[96,256]{1,0:T(8,128)(2,1)S(1)} collective-permute-done((bf16[96,256]{1,0:T(8,128)(2,1)S(1)}, bf16[96,256]{1,0:T(8,128)(2,1)S(1)}, u32[]{:S(2)}, u32[]{:S(2)}) %collective-permute-start.9) | collective-permute-done | bytes 49184 | tf_op jit(solution)/shard_map/ppermute | solution.py:270
  24.7 1.0 %shard_map.55 = bf16[512,256]{1,0:T(8,128)(2,1)} custom-call(f32[32,256]{1,0:T(8,128)S(1)} %add_sine_fusion.enc, bf16[96,256]{1,0:T(8,128)(2,1)S(1)} %collective-permute-done.9.relayed, bf16[2,9,512,128]{3,2,1,0:T(8,128)(2,1)S(1)} %bitcast.10, f32[512,256]{1,0:T(8,128)S(1)} %get-tuple-element.43.base, f32[512,128]{1,0:T(8,128)S(1)} %get-tuple-element.44.joined_in), custom_call_target="tpu_custom_call" | custom-call | tf_op jit(solution)/shard_map/pallas_call | solution.py:252
  (5 shorter events, 0.1 us)
Async XLA Ops:
  0.0 13.8 %collective-permute-start.5 = (bf16[512,256]{1,0:T(8,128)(2,1)}, bf16[512,256]{1,0:T(8,128)(2,1)S(1)}, u32[]{:S(2)}, u32[]{:S(2)}) collective-permute-start(bf16[512,256]{1,0:T(8,128)(2,1)} %bitcast.11), channel_id=1, source_target_pairs={{0,24},{8,16},{16,8},{24,0},{1,25},{9,17},{17,9},{25,1},{2,26},{10... | collective-permute-start | bytes 786440 | tf_op jit(solution)/shard_map/ppermute | solution.py:270
  5.0 12.6 %collective-permute-start.4 = (bf16[512,256]{1,0:T(8,128)(2,1)}, bf16[512,256]{1,0:T(8,128)(2,1)S(1)}, u32[]{:S(2)}, u32[]{:S(2)}) collective-permute-start(bf16[512,256]{1,0:T(8,128)(2,1)} %bitcast.12), channel_id=1, source_target_pairs={{0,8},{8,0},{16,24},{24,16},{1,9},{9,1},{17,25},{25,17},{2,10},{10... | collective-permute-start | bytes 786440 | tf_op jit(solution)/shard_map/ppermute | solution.py:270
  5.1 1.0 %copy-start.1 = (bf16[1,32,16,256]{3,2,1,0:T(8,128)(2,1)S(1)}, bf16[1,32,16,256]{3,2,1,0:T(8,128)(2,1)}, u32[]{:S(2)}) copy-start(bf16[1,32,16,256]{3,2,1,0:T(8,128)(2,1)} %param.4) | copy-start | bytes 786436
  6.1 1.6 %collective-permute-start = (bf16[32,256]{1,0:T(8,128)(2,1)S(1)}, bf16[32,256]{1,0:T(8,128)(2,1)S(1)}, u32[]{:S(2)}, u32[]{:S(2)}) collective-permute-start(bf16[32,256]{1,0:T(8,128)(2,1)S(1)} %get-tuple-element.25), channel_id=1, source_target_pairs={{0,2},{4,6},{2,0},{6,4},{1,3},{5,7},{3,1},{7,5},{8,10},{12,14},{10... | collective-permute-start | bytes 49160 | tf_op jit(solution)/shard_map/ppermute | solution.py:289
  6.2 1.6 %collective-permute-start.1 = (bf16[32,256]{1,0:T(8,128)(2,1)S(1)}, bf16[32,256]{1,0:T(8,128)(2,1)S(1)}, u32[]{:S(2)}, u32[]{:S(2)}) collective-permute-start(bf16[32,256]{1,0:T(8,128)(2,1)S(1)} %get-tuple-element.26), channel_id=1, source_target_pairs={{2,4},{4,2},{3,5},{5,3},{10,12},{12,10},{11,13},{13,11},{18,20},{2... | collective-permute-start | bytes 49160 | tf_op jit(solution)/shard_map/ppermute | solution.py:289
  7.8 3.8 %collective-permute-start.2 = (bf16[32,256]{1,0:T(8,128)(2,1)S(1)}, bf16[32,256]{1,0:T(8,128)(2,1)S(1)}, u32[]{:S(2)}, u32[]{:S(2)}) collective-permute-start(bf16[32,256]{1,0:T(8,128)(2,1)S(1)} %shard_map.47), channel_id=1, source_target_pairs={{0,1},{1,0},{2,3},{3,2},{4,5},{5,4},{6,7},{7,6},{8,9},{9,8},{10,11... | collective-permute-start | bytes 49160 | tf_op jit(solution)/shard_map/ppermute | solution.py:300
  10.0 6.9 %copy-start = (bf16[1,2,9,512,128]{4,3,2,1,0:T(8,128)(2,1)S(1)}, bf16[1,2,9,512,128]{4,3,2,1,0:T(8,128)(2,1)}, u32[]{:S(2)}) copy-start(bf16[1,2,9,512,128]{4,3,2,1,0:T(8,128)(2,1)} %param.7) | copy-start | bytes 7077892
  11.6 6.8 %collective-permute-start.8 = (bf16[64,256]{1,0:T(8,128)(2,1)S(1)}, bf16[64,256]{1,0:T(8,128)(2,1)S(1)}, u32[]{:S(2)}, u32[]{:S(2)}) collective-permute-start(bf16[64,256]{1,0:T(8,128)(2,1)S(1)} %shard_map.48.strip), channel_id=1, source_target_pairs={{0,16},{8,24},{16,0},{24,8},{1,17},{9,25},{17,1},{25,9},{2,18},{10... | collective-permute-start | bytes 98312 | tf_op jit(solution)/shard_map/ppermute | solution.py:270
  12.2 7.0 %collective-permute-start.3 = (bf16[64,256]{1,0:T(8,128)(2,1)S(1)}, bf16[64,256]{1,0:T(8,128)(2,1)S(1)}, u32[]{:S(2)}, u32[]{:S(2)}) collective-permute-start(bf16[64,256]{1,0:T(8,128)(2,1)S(1)} %shard_map.48.strip), channel_id=1, source_target_pairs={{0,8},{8,0},{16,24},{24,16},{1,9},{9,1},{17,25},{25,17},{2,10},{10... | collective-permute-start | bytes 98312 | tf_op jit(solution)/shard_map/ppermute | solution.py:270
  13.8 9.9 %collective-permute-start.10 = (bf16[512,256]{1,0:T(8,128)(2,1)S(1)}, bf16[512,256]{1,0:T(8,128)(2,1)S(1)}, u32[]{:S(2)}, u32[]{:S(2)}) collective-permute-start(bf16[512,256]{1,0:T(8,128)(2,1)S(1)} %collective-permute-done.5.view.far), channel_id=1, source_target_pairs={{0,8},{8,0},{16,24},{24,16},{1,9},{9,1},{17,25},{25,17},{2,10},{10... | collective-permute-start | bytes 786440 | tf_op jit(solution)/shard_map/ppermute | solution.py:270
  17.7 1.2 %collective-permute-start.6 = (bf16[32,256]{1,0:T(8,128)(2,1)S(1)}, bf16[32,256]{1,0:T(8,128)(2,1)S(1)}, u32[]{:S(2)}, u32[]{:S(2)}) collective-permute-start(bf16[32,256]{1,0:T(8,128)(2,1)S(1)} %shard_map.50), channel_id=1, source_target_pairs={{0,2},{4,6},{2,0},{6,4},{1,3},{5,7},{3,1},{7,5},{8,10},{12,14},{10... | collective-permute-start | bytes 49160 | tf_op jit(solution)/shard_map/ppermute | solution.py:289
  17.9 1.4 %collective-permute-start.7 = (bf16[32,256]{1,0:T(8,128)(2,1)S(1)}, bf16[32,256]{1,0:T(8,128)(2,1)S(1)}, u32[]{:S(2)}, u32[]{:S(2)}) collective-permute-start(bf16[32,256]{1,0:T(8,128)(2,1)S(1)} %shard_map.51), channel_id=1, source_target_pairs={{0,2},{4,6},{2,0},{6,4},{1,3},{5,7},{3,1},{7,5},{8,10},{12,14},{10... | collective-permute-start | bytes 49160 | tf_op jit(solution)/shard_map/ppermute | solution.py:289
  19.2 5.5 %collective-permute-start.9 = (bf16[96,256]{1,0:T(8,128)(2,1)S(1)}, bf16[96,256]{1,0:T(8,128)(2,1)S(1)}, u32[]{:S(2)}, u32[]{:S(2)}) collective-permute-start(bf16[96,256]{1,0:T(8,128)(2,1)S(1)} %shard_map.52), channel_id=1, source_target_pairs={{0,8},{8,0},{16,24},{24,16},{1,9},{9,1},{17,25},{25,17},{2,10},{10... | collective-permute-start | bytes 147464 | tf_op jit(solution)/shard_map/ppermute | solution.py:270

commit v9 on v8

--- a/solution.py
+++ b/solution.py
@@ -69,7 +69,7 @@
 
 
 def corners(left, right, at):
-    fill = jnp.zeros((14, left.shape[1]), F32)
+    fill = jnp.zeros((6, left.shape[1]), F32)
     return jnp.concatenate([left[at : at + 1], right[at : at + 1], fill], axis=0)
 
 
@@ -95,13 +95,13 @@
 
 
 def relay_kernel(strip, far_a, out):
-    size = strip.shape[0]
-    out[0:size, :] = strip[...]
-    out[size:, :] = far_a[...]
+    rows = far_a.shape[0]
+    out[0:rows, :] = far_a[...]
+    out[rows:, :] = strip[0 : out.shape[0] - rows, :]
 
 
 def neighbours(rows, cols, shards, pick, enc, strip, raw_a):
-    extra = cols + 16
+    extra = cols + 8
     size = extra if pick else 2 * extra
     lines = strip[rows : rows + size, :].astype(F32)
     if pick:
@@ -230,9 +230,8 @@
 
 def rim_kernel(rows, cols, shards, pick, enc, relayed, weights, base, joined_in, out, joined):
     chan, width = out.shape[1], joined.shape[1]
-    size = relayed.shape[0] - rows
     last_a, b, before, after = neighbours(
-        rows, cols, shards, pick, enc, relayed.at[0:size], relayed.at[size : size + rows]
+        rows, cols, shards, pick, enc, relayed[rows:, :], relayed[0:rows, :]
     )
     joined[...] = joined_in[...]
     add_columns(rows, cols, joined, weights, last_a, 2, b, 3)
@@ -290,7 +289,7 @@
 
     got_b, got_a = swap(col_b, 1), swap(col_a, 0)
     pick = "slab" if slabs == 2 else None
-    edge = shape(cols + 16, chan)
+    edge = shape(cols + 8, chan)
     edges = call(
         functools.partial(edges_kernel, rows, cols, shards, pick),
         [edge_rows, got_a, got_b, enc],
@@ -307,8 +306,8 @@
     strip = call(
         functools.partial(strip_kernel, rows, shards),
         [got_a, got_b, enc, *beyond],
-        [shape(rows + len(beyond) * (cols + 16), chan)],
-        cost=pl.CostEstimate(flops=2000000000, bytes_accessed=0, transcendentals=0),
+        [shape(rows + len(beyond) * (cols + 8), chan)],
+        cost=pl.CostEstimate(flops=2_000_000_000, bytes_accessed=0, transcendentals=0),
     )[0]
     near_strip, last_strip = across(strip, 1), across(strip, 2)
     far, panel = lax.optimization_barrier((far, panel))

time: 26.2 us -> 26.1 us (level)
  no operation moved by 1% of the time
where the time goes in v9:
time: 26.1 us; the launch traced here: 25.6 us
  starting transfers between devices  15 us (57%)
  waiting for transfers between devices  4.3 us (16%)
  Pallas kernels  3.63 us (14%)
  local copies, waits for them, and re-layouts  1.09 us (4%)
  other arithmetic  0.86 us (3%)
  between operations  0.75 us (3%)
    ppermute x6, starting transfers between devices, across(): return lax.ppermute(array, 'src', [(i, i ^ k) for i in range(4)])  12.1 us
    pallas_call x10, Pallas kernels, call(): pl.pallas_call(kernel, out_shape=outs, in_specs=[VMEM_SPEC] * len(ins), o...  3.63 us
    ppermute x6, waiting for transfers between devices, across(): return lax.ppermute(array, 'src', [(i, i ^ k) for i in range(4)])  1.91 us
    ppermute x1, starting transfers between devices, local(): beyond = [lax.ppermute(edges[0], 'slab', [(0, 1), (1, 0)])]  1.56 us
    ppermute x1, waiting for transfers between devices, local(): beyond = [lax.ppermute(edges[0], 'slab', [(0, 1), (1, 0)])]  1.54 us
    ppermute x4, starting transfers between devices, swap(): return lax.ppermute(array, 'shard', pairs + [(j, i) for i, j in pairs])  1.37 us
    unnamed x4, local copies, waits for them, and re-layouts  1.02 us
    ppermute x4, waiting for transfers between devices, swap(): return lax.ppermute(array, 'shard', pairs + [(j, i) for i, j in pairs])  0.84 us
  transfers between devices with their start and end apart: 11, of which 5 were waited for; matrix products, arithmetic and copies ran while one was open for 4% of the time, Pallas kernels for 10%

profile of v9, /device:TPU:0, one launch (start us, length us, event | category | flops | bytes accessed | tf_op | source)
XLA Modules:
  0.0 25.6 jit_solution(11081704831495016389)
XLA Ops:
  0.0 5.0 %collective-permute-start.5 = (bf16[512,256]{1,0:T(8,128)(2,1)}, bf16[512,256]{1,0:T(8,128)(2,1)S(1)}, u32[]{:S(2)}, u32[]{:S(2)}) collective-permute-start(bf16[512,256]{1,0:T(8,128)(2,1)} %bitcast.11), channel_id=1, source_target_pairs={{0,24},{8,16},{16,8},{24,0},{1,25},{9,17},{17,9},{25,1},{2,26},{10... | collective-permute-start | bytes 786440 | tf_op jit(solution)/shard_map/ppermute | solution.py:269
  5.0 0.0 collective-permute-start.4
  5.1 0.0 copy-start.1
  5.1 1.0 %copy-done.1 = bf16[1,32,16,256]{3,2,1,0:T(8,128)(2,1)S(1)} copy-done((bf16[1,32,16,256]{3,2,1,0:T(8,128)(2,1)S(1)}, bf16[1,32,16,256]{3,2,1,0:T(8,128)(2,1)}, u32[]{:S(2)}) %copy-start.1) | copy-done | bytes 262168
  6.1 0.1 shard_map.46
  6.1 0.1 collective-permute-start
  6.2 0.7 %collective-permute-start.1 = (bf16[32,256]{1,0:T(8,128)(2,1)S(1)}, bf16[32,256]{1,0:T(8,128)(2,1)S(1)}, u32[]{:S(2)}, u32[]{:S(2)}) collective-permute-start(bf16[32,256]{1,0:T(8,128)(2,1)S(1)} %get-tuple-element.26), channel_id=1, source_target_pairs={{2,4},{4,2},{3,5},{5,3},{10,12},{12,10},{11,13},{13,11},{18,20},{2... | collective-permute-start | bytes 49160 | tf_op jit(solution)/shard_map/ppermute | solution.py:288
  7.6 0.2 add_sine_fusion.enc
  7.8 0.0 collective-permute-done.got_a
  7.8 0.0 collective-permute-done.1.got_b
  7.8 1.6 %collective-permute-start.2 = (bf16[24,256]{1,0:T(8,128)(2,1)S(1)}, bf16[24,256]{1,0:T(8,128)(2,1)S(1)}, u32[]{:S(2)}, u32[]{:S(2)}) collective-permute-start(bf16[24,256]{1,0:T(8,128)(2,1)S(1)} %shard_map.47), channel_id=1, source_target_pairs={{0,1},{1,0},{2,3},{3,2},{4,5},{5,4},{6,7},{7,6},{8,9},{9,8},{10,11... | collective-permute-start | bytes 36872 | tf_op jit(solution)/shard_map/ppermute | solution.py:299
  9.4 0.7 %convert_bitcast_fusion = f32[2]{0:T(128)S(1)} fusion(s32[1,2]{1,0:T(1,128)} %param.5), kind=kLoop, calls=%fused_computation.13 | loop fusion | flops 2 | bytes 16 | tf_op jit(solution)/shard_map/broadcast_in_dim | solution.py:283
  10.0 0.0 copy-start
  10.0 1.5 %collective-permute-done.2.refs_0_ = bf16[24,256]{1,0:T(8,128)(2,1)S(1)} collective-permute-done((bf16[24,256]{1,0:T(8,128)(2,1)S(1)}, bf16[24,256]{1,0:T(8,128)(2,1)S(1)}, u32[]{:S(2)}, u32[]{:S(2)}) %collective-permute-start.2) | collective-permute-done | bytes 12320 | tf_op jit(solution)/shard_map/ppermute | solution.py:299
  11.6 0.6 %collective-permute-start.8 = (bf16[56,256]{1,0:T(8,128)(2,1)S(1)}, bf16[56,256]{1,0:T(8,128)(2,1)S(1)}, u32[]{:S(2)}, u32[]{:S(2)}) collective-permute-start(bf16[56,256]{1,0:T(8,128)(2,1)S(1)} %shard_map.48.strip), channel_id=1, source_target_pairs={{0,16},{8,24},{16,0},{24,8},{1,17},{9,25},{17,1},{25,9},{2,18},{10... | collective-permute-start | bytes 86024 | tf_op jit(solution)/shard_map/ppermute | solution.py:269
  12.2 1.5 %collective-permute-start.3 = (bf16[56,256]{1,0:T(8,128)(2,1)S(1)}, bf16[56,256]{1,0:T(8,128)(2,1)S(1)}, u32[]{:S(2)}, u32[]{:S(2)}) collective-permute-start(bf16[56,256]{1,0:T(8,128)(2,1)S(1)} %shard_map.48.strip), channel_id=1, source_target_pairs={{0,8},{8,0},{16,24},{24,16},{1,9},{9,1},{17,25},{25,17},{2,10},{10... | collective-permute-start | bytes 86024 | tf_op jit(solution)/shard_map/ppermute | solution.py:269
  13.7 0.0 collective-permute-done.5.view.far
  13.7 3.2 %collective-permute-start.10 = (bf16[512,256]{1,0:T(8,128)(2,1)S(1)}, bf16[512,256]{1,0:T(8,128)(2,1)S(1)}, u32[]{:S(2)}, u32[]{:S(2)}) collective-permute-start(bf16[512,256]{1,0:T(8,128)(2,1)S(1)} %collective-permute-done.5.view.far), channel_id=1, source_target_pairs={{0,8},{8,0},{16,24},{24,16},{1,9},{9,1},{17,25},{25,17},{2,10},{10... | collective-permute-start | bytes 786440 | tf_op jit(solution)/shard_map/ppermute | solution.py:269
  16.9 0.1 broadcast_in_dim.5.coords
  17.0 0.0 copy-done
  17.0 0.6 %shard_map.49 = (f32[512,256]{1,0:T(8,128)S(1)}, f32[512,128]{1,0:T(8,128)S(1)}) custom-call(f32[2,256]{1,0:T(2,128)S(1)} %broadcast_in_dim.5.coords, bf16[512,256]{1,0:T(8,128)(2,1)S(1)} %get-tuple-element.30.own, f32[32,256]{1,0:T(8,128)S(1)} %add_sine_fusion.enc, bf16[56,256]{1,0:T(8,128)(2,1)S(1)} %shard_map.48.strip, ...), custom_call_target="tpu_custom_call" | custom-call | flops 5000000000 | bytes 4000000 | tf_op jit(solution)/shard_map/pallas_call | solution.py:251
  17.6 0.0 collective-permute-done.4.view.near
  17.6 0.1 shard_map.50
  17.7 0.1 collective-permute-start.6
  17.8 0.1 shard_map.51
  17.8 0.5 %collective-permute-start.7 = (bf16[32,256]{1,0:T(8,128)(2,1)S(1)}, bf16[32,256]{1,0:T(8,128)(2,1)S(1)}, u32[]{:S(2)}, u32[]{:S(2)}) collective-permute-start(bf16[32,256]{1,0:T(8,128)(2,1)S(1)} %shard_map.51), channel_id=1, source_target_pairs={{0,2},{4,6},{2,0},{6,4},{1,3},{5,7},{3,1},{7,5},{8,10},{12,14},{10... | collective-permute-start | bytes 49160 | tf_op jit(solution)/shard_map/ppermute | solution.py:288
  18.4 0.0 collective-permute-done.8.strip.last_strip
  18.4 0.5 %collective-permute-done.6.near_a = bf16[32,256]{1,0:T(8,128)(2,1)S(1)} collective-permute-done((bf16[32,256]{1,0:T(8,128)(2,1)S(1)}, bf16[32,256]{1,0:T(8,128)(2,1)S(1)}, u32[]{:S(2)}, u32[]{:S(2)}) %collective-permute-start.6) | collective-permute-done | bytes 16416 | tf_op jit(solution)/shard_map/ppermute | solution.py:288
  18.9 0.3 %collective-permute-done.7.far_a = bf16[32,256]{1,0:T(8,128)(2,1)S(1)} collective-permute-done((bf16[32,256]{1,0:T(8,128)(2,1)S(1)}, bf16[32,256]{1,0:T(8,128)(2,1)S(1)}, u32[]{:S(2)}, u32[]{:S(2)}) %collective-permute-start.7) | collective-permute-done | bytes 16416 | tf_op jit(solution)/shard_map/ppermute | solution.py:288
  19.2 0.0 collective-permute-done.3.near_strip
  19.2 1.7 %collective-permute-start.9 = (bf16[88,256]{1,0:T(8,128)(2,1)S(1)}, bf16[88,256]{1,0:T(8,128)(2,1)S(1)}, u32[]{:S(2)}, u32[]{:S(2)}) collective-permute-start(bf16[88,256]{1,0:T(8,128)(2,1)S(1)} %shard_map.52), channel_id=1, source_target_pairs={{0,8},{8,0},{16,24},{24,16},{1,9},{9,1},{17,25},{25,17},{2,10},{10... | collective-permute-start | bytes 135176 | tf_op jit(solution)/shard_map/ppermute | solution.py:269
  20.9 1.2 %shard_map.53 = (f32[512,256]{1,0:T(8,128)S(1)}, f32[512,128]{1,0:T(8,128)S(1)}) custom-call(f32[2,256]{1,0:T(2,128)S(1)} %broadcast_in_dim.5.coords, bf16[512,256]{1,0:T(8,128)(2,1)S(1)} %collective-permute-done.4.view.near, bf16[512,256]{1,0:T(8,128)(2,1)S(1)} %collective-permute-done.5.view.far, f32[32,256]{1,0:T(8,128)S(1)} %add_sine_fusion.enc, ...), custom_call_target="tpu_custom_call" | custom-call | tf_op jit(solution)/shard_map/pallas_call | solution.py:251
  22.2 1.5 %collective-permute-done.10.last = bf16[512,256]{1,0:T(8,128)(2,1)S(1)} collective-permute-done((bf16[512,256]{1,0:T(8,128)(2,1)S(1)}, bf16[512,256]{1,0:T(8,128)(2,1)S(1)}, u32[]{:S(2)}, u32[]{:S(2)}) %collective-permute-start.10) | collective-permute-done | bytes 262176 | tf_op jit(solution)/shard_map/ppermute | solution.py:269
  23.7 0.6 %shard_map.54 = (f32[512,256]{1,0:T(8,128)S(1)}, f32[512,128]{1,0:T(8,128)S(1)}) custom-call(f32[2,256]{1,0:T(2,128)S(1)} %broadcast_in_dim.5.coords, bf16[512,256]{1,0:T(8,128)(2,1)S(1)} %collective-permute-done.10.last, f32[32,256]{1,0:T(8,128)S(1)} %add_sine_fusion.enc, bf16[2,9,512,128]{3,2,1,0:T(8,128)(2,1)S(1)} %bitcast.9, ...), custom_call_target="tpu_custom_call" | custom-call | tf_op jit(solution)/shard_map/pallas_call | solution.py:251
  24.2 0.4 %collective-permute-done.9.relayed = bf16[88,256]{1,0:T(8,128)(2,1)S(1)} collective-permute-done((bf16[88,256]{1,0:T(8,128)(2,1)S(1)}, bf16[88,256]{1,0:T(8,128)(2,1)S(1)}, u32[]{:S(2)}, u32[]{:S(2)}) %collective-permute-start.9) | collective-permute-done | bytes 45088 | tf_op jit(solution)/shard_map/ppermute | solution.py:269
  24.6 1.0 %shard_map.55 = bf16[512,256]{1,0:T(8,128)(2,1)} custom-call(f32[32,256]{1,0:T(8,128)S(1)} %add_sine_fusion.enc, bf16[88,256]{1,0:T(8,128)(2,1)S(1)} %collective-permute-done.9.relayed, bf16[2,9,512,128]{3,2,1,0:T(8,128)(2,1)S(1)} %bitcast.10, f32[512,256]{1,0:T(8,128)S(1)} %get-tuple-element.43.base, f32[512,128]{1,0:T(8,128)S(1)} %get-tuple-element.44.joined_in), custom_call_target="tpu_custom_call" | custom-call | tf_op jit(solution)/shard_map/pallas_call | solution.py:251
  (5 shorter events, 0.1 us)
Async XLA Ops:
  0.0 13.7 %collective-permute-start.5 = (bf16[512,256]{1,0:T(8,128)(2,1)}, bf16[512,256]{1,0:T(8,128)(2,1)S(1)}, u32[]{:S(2)}, u32[]{:S(2)}) collective-permute-start(bf16[512,256]{1,0:T(8,128)(2,1)} %bitcast.11), channel_id=1, source_target_pairs={{0,24},{8,16},{16,8},{24,0},{1,25},{9,17},{17,9},{25,1},{2,26},{10... | collective-permute-start | bytes 786440 | tf_op jit(solution)/shard_map/ppermute | solution.py:269
  5.0 12.5 %collective-permute-start.4 = (bf16[512,256]{1,0:T(8,128)(2,1)}, bf16[512,256]{1,0:T(8,128)(2,1)S(1)}, u32[]{:S(2)}, u32[]{:S(2)}) collective-permute-start(bf16[512,256]{1,0:T(8,128)(2,1)} %bitcast.12), channel_id=1, source_target_pairs={{0,8},{8,0},{16,24},{24,16},{1,9},{9,1},{17,25},{25,17},{2,10},{10... | collective-permute-start | bytes 786440 | tf_op jit(solution)/shard_map/ppermute | solution.py:269
  5.1 1.0 %copy-start.1 = (bf16[1,32,16,256]{3,2,1,0:T(8,128)(2,1)S(1)}, bf16[1,32,16,256]{3,2,1,0:T(8,128)(2,1)}, u32[]{:S(2)}) copy-start(bf16[1,32,16,256]{3,2,1,0:T(8,128)(2,1)} %param.4) | copy-start | bytes 786436
  6.1 1.6 %collective-permute-start = (bf16[32,256]{1,0:T(8,128)(2,1)S(1)}, bf16[32,256]{1,0:T(8,128)(2,1)S(1)}, u32[]{:S(2)}, u32[]{:S(2)}) collective-permute-start(bf16[32,256]{1,0:T(8,128)(2,1)S(1)} %get-tuple-element.25), channel_id=1, source_target_pairs={{0,2},{4,6},{2,0},{6,4},{1,3},{5,7},{3,1},{7,5},{8,10},{12,14},{10... | collective-permute-start | bytes 49160 | tf_op jit(solution)/shard_map/ppermute | solution.py:288
  6.2 1.6 %collective-permute-start.1 = (bf16[32,256]{1,0:T(8,128)(2,1)S(1)}, bf16[32,256]{1,0:T(8,128)(2,1)S(1)}, u32[]{:S(2)}, u32[]{:S(2)}) collective-permute-start(bf16[32,256]{1,0:T(8,128)(2,1)S(1)} %get-tuple-element.26), channel_id=1, source_target_pairs={{2,4},{4,2},{3,5},{5,3},{10,12},{12,10},{11,13},{13,11},{18,20},{2... | collective-permute-start | bytes 49160 | tf_op jit(solution)/shard_map/ppermute | solution.py:288
  7.8 3.8 %collective-permute-start.2 = (bf16[24,256]{1,0:T(8,128)(2,1)S(1)}, bf16[24,256]{1,0:T(8,128)(2,1)S(1)}, u32[]{:S(2)}, u32[]{:S(2)}) collective-permute-start(bf16[24,256]{1,0:T(8,128)(2,1)S(1)} %shard_map.47), channel_id=1, source_target_pairs={{0,1},{1,0},{2,3},{3,2},{4,5},{5,4},{6,7},{7,6},{8,9},{9,8},{10,11... | collective-permute-start | bytes 36872 | tf_op jit(solution)/shard_map/ppermute | solution.py:299
  10.0 6.9 %copy-start = (bf16[1,2,9,512,128]{4,3,2,1,0:T(8,128)(2,1)S(1)}, bf16[1,2,9,512,128]{4,3,2,1,0:T(8,128)(2,1)}, u32[]{:S(2)}) copy-start(bf16[1,2,9,512,128]{4,3,2,1,0:T(8,128)(2,1)} %param.7) | copy-start | bytes 7077892
  11.6 6.8 %collective-permute-start.8 = (bf16[56,256]{1,0:T(8,128)(2,1)S(1)}, bf16[56,256]{1,0:T(8,128)(2,1)S(1)}, u32[]{:S(2)}, u32[]{:S(2)}) collective-permute-start(bf16[56,256]{1,0:T(8,128)(2,1)S(1)} %shard_map.48.strip), channel_id=1, source_target_pairs={{0,16},{8,24},{16,0},{24,8},{1,17},{9,25},{17,1},{25,9},{2,18},{10... | collective-permute-start | bytes 86024 | tf_op jit(solution)/shard_map/ppermute | solution.py:269
  12.2 7.0 %collective-permute-start.3 = (bf16[56,256]{1,0:T(8,128)(2,1)S(1)}, bf16[56,256]{1,0:T(8,128)(2,1)S(1)}, u32[]{:S(2)}, u32[]{:S(2)}) collective-permute-start(bf16[56,256]{1,0:T(8,128)(2,1)S(1)} %shard_map.48.strip), channel_id=1, source_target_pairs={{0,8},{8,0},{16,24},{24,16},{1,9},{9,1},{17,25},{25,17},{2,10},{10... | collective-permute-start | bytes 86024 | tf_op jit(solution)/shard_map/ppermute | solution.py:269
  13.7 9.9 %collective-permute-start.10 = (bf16[512,256]{1,0:T(8,128)(2,1)S(1)}, bf16[512,256]{1,0:T(8,128)(2,1)S(1)}, u32[]{:S(2)}, u32[]{:S(2)}) collective-permute-start(bf16[512,256]{1,0:T(8,128)(2,1)S(1)} %collective-permute-done.5.view.far), channel_id=1, source_target_pairs={{0,8},{8,0},{16,24},{24,16},{1,9},{9,1},{17,25},{25,17},{2,10},{10... | collective-permute-start | bytes 786440 | tf_op jit(solution)/shard_map/ppermute | solution.py:269
  17.7 1.2 %collective-permute-start.6 = (bf16[32,256]{1,0:T(8,128)(2,1)S(1)}, bf16[32,256]{1,0:T(8,128)(2,1)S(1)}, u32[]{:S(2)}, u32[]{:S(2)}) collective-permute-start(bf16[32,256]{1,0:T(8,128)(2,1)S(1)} %shard_map.50), channel_id=1, source_target_pairs={{0,2},{4,6},{2,0},{6,4},{1,3},{5,7},{3,1},{7,5},{8,10},{12,14},{10... | collective-permute-start | bytes 49160 | tf_op jit(solution)/shard_map/ppermute | solution.py:288
  17.8 1.4 %collective-permute-start.7 = (bf16[32,256]{1,0:T(8,128)(2,1)S(1)}, bf16[32,256]{1,0:T(8,128)(2,1)S(1)}, u32[]{:S(2)}, u32[]{:S(2)}) collective-permute-start(bf16[32,256]{1,0:T(8,128)(2,1)S(1)} %shard_map.51), channel_id=1, source_target_pairs={{0,2},{4,6},{2,0},{6,4},{1,3},{5,7},{3,1},{7,5},{8,10},{12,14},{10... | collective-permute-start | bytes 49160 | tf_op jit(solution)/shard_map/ppermute | solution.py:288
  19.2 5.4 %collective-permute-start.9 = (bf16[88,256]{1,0:T(8,128)(2,1)S(1)}, bf16[88,256]{1,0:T(8,128)(2,1)S(1)}, u32[]{:S(2)}, u32[]{:S(2)}) collective-permute-start(bf16[88,256]{1,0:T(8,128)(2,1)S(1)} %shard_map.52), channel_id=1, source_target_pairs={{0,8},{8,0},{16,24},{24,16},{1,9},{9,1},{17,25},{25,17},{2,10},{10... | collective-permute-start | bytes 135176 | tf_op jit(solution)/shard_map/ppermute | solution.py:269

commit v10 on v9

--- a/solution.py
+++ b/solution.py
@@ -34,7 +34,7 @@
 
 def column(rows, cols, view, wide, pick_last):
     for c, lanes in tiles(view.shape[1]):
-        wide[c] = view[:, lanes].astype(F32)
+        wide[c, 0 : rows * cols, :] = view[:, lanes].astype(F32)
         first = wide[c, pl.ds(0, rows, stride=cols), :]
         last = wide[c, pl.ds(cols - 1, rows, stride=cols), :]
         yield lanes, jnp.where(pick_last, last, first), jnp.where(pick_last, first, last)
@@ -122,9 +122,9 @@
     return lax.div(index, 2), pl.multiple_of(lax.rem(index, 2) * chan, chan)
 
 
-def inside(rows, cols, k, coords, view, enc, weights, base_in, base, joined, panel):
+def inside(rows, cols, k, coords, view, enc, weights, base_in, base, sums, panel):
     weight = blend_weight(coords, jnp.bitwise_xor(lax.axis_index("src"), k))
-    chan, width = view.shape[1], joined.shape[1]
+    chan, width = view.shape[1], sums.shape[1]
     pixels = rows * cols
     for h in range(rows):
         here = slice(h * cols, (h + 1) * cols)
@@ -146,7 +146,7 @@
     )
     column = lax.rem(lax.broadcasted_iota(jnp.int32, (pixels, width), 0), cols)
     zero = jnp.zeros((cols, width), F32)
-    total = joined[...]
+    total = sums[0:pixels, :]
     for b in (1, 0, 2):
         up, level, down = (taps[:, (3 * b + a) * width : (3 * b + a + 1) * width] for a in range(3))
         part = level + jnp.concatenate([zero, up[: pixels - cols]], axis=0)
@@ -156,17 +156,17 @@
         if b == 2:
             part = jnp.where(column == cols - 1, 0.0, pltpu.roll(part, pixels - 1, 0))
         total = total + part
-    joined[...] = total
-
-
-def add_line(joined, where, line, weights, group, at, taps):
+    sums[0:pixels, :] = total
+
+
+def add_line(sums, where, line, weights, group, at, taps):
     chan, count = line.shape[1], line.shape[0] - 2
     wide = jnp.concatenate([line[i : i + count] for i in range(3)], axis=1).astype(BF16)
     kernel = jnp.concatenate([weights[group, tap, pl.ds(at, chan), :] for tap in taps], axis=0)
-    joined[where, :] += jnp.dot(wide, kernel, preferred_element_type=F32)
-
-
-def add_columns(rows, cols, joined, weights, a, a_view, b, b_view):
+    sums[where, :] += jnp.dot(wide, kernel, preferred_element_type=F32)
+
+
+def add_columns(rows, cols, sums, weights, a, a_view, b, b_view):
     even = lax.rem(lax.axis_index("shard"), 2) == 0
     chan = a.shape[1]
     group, at_a = where_of(a_view, chan)
@@ -178,10 +178,10 @@
     for side, tap, start, at in ((left, 0, 0, at_left), (right, 2, cols - 1, at_right)):
         line = jnp.concatenate([zero, side, zero], axis=0)
         where = pl.ds(start, rows, stride=cols)
-        add_line(joined, where, line, weights, group, at, [3 * i + tap for i in range(3)])
-
-
-def add_rows(rows, cols, pick, joined, weights, view, before, after):
+        add_line(sums, where, line, weights, group, at, [3 * i + tap for i in range(3)])
+
+
+def add_rows(rows, cols, pick, sums, weights, view, before, after):
     group, at = where_of(view, before.shape[1])
     if pick:
         first = lax.axis_index(pick) == 0
@@ -190,7 +190,7 @@
         places = [(before, 0, 0), (after, rows - 1, 6)]
     for line, h, tap in places:
         where = pl.ds(pl.multiple_of(h * cols, cols), cols)
-        add_line(joined, where, line, weights, group, at, [tap + i for i in range(3)])
+        add_line(sums, where, line, weights, group, at, [tap + i for i in range(3)])
 
 
 def silu(x):
@@ -215,7 +215,7 @@
     add_columns(rows, cols, joined, weights, a, 1, b, 1)
     add_rows(rows, cols, pick, joined, weights, 1, before, after)
     here = pl.ds(pl.multiple_of(lax.div(me, 2) * width, width), width)
-    base[:, here] = base[:, here] + silu(joined[...])
+    base[:, here] = base[:, here] + silu(joined[0 : rows * cols, :])
     a, b, before, after = neighbours(rows, cols, shards, pick, enc, last_strip, far_a)
     joined[...] = jnp.zeros_like(joined)
     inside(rows, cols, 3, coords, far, enc, weights, base, base, joined, panel)
@@ -237,7 +237,7 @@
     add_columns(rows, cols, joined, weights, last_a, 2, b, 3)
     add_rows(rows, cols, pick, joined, weights, 3, before, after)
     group = where_of(2, chan)[0]
-    added = silu(joined[...])
+    added = silu(joined[0 : rows * cols, :])
     for c, lanes in tiles(chan):
         here = group == c * LANES // width
         out[:, lanes] = (base[:, lanes] + jnp.where(here, added, 0.0)).astype(BF16)
@@ -278,7 +278,7 @@
         functools.partial(columns_kernel, rows, cols),
         [own],
         [line, line, shape(2 * cols, chan), shape(pixels, chan)],
-        [pltpu.VMEM((chan // LANES, pixels, LANES), F32)],
+        [pltpu.VMEM((chan // LANES, pixels + cols, LANES), F32)],
     )
     place = jnp.broadcast_to(coords.astype(F32).reshape(2, 1), (2, chan))
     shards, slabs = lax.axis_size("shard"), lax.axis_size("slab")
@@ -318,13 +318,13 @@
             functools.partial(inner_kernel, rows, cols),
             [view],
             [line],
-            [pltpu.VMEM((chan // LANES, pixels, LANES), F32)],
+            [pltpu.VMEM((chan // LANES, pixels + cols, LANES), F32)],
         )[0]
         return swap(out, 0)
 
 
     scratch = [pltpu.VMEM((pixels, chan), BF16)]
-    sums = [shape(pixels, chan, F32), shape(pixels, width, F32)]
+    sums = [shape(pixels, chan, F32), shape(pixels + cols, width, F32)]
     cost = pl.CostEstimate(flops=5000000000, bytes_accessed=4_000_000, transcendentals=0)
     base, joined = call(
         functools.partial(own_kernel, rows, cols, shards, pick),
@@ -359,7 +359,7 @@
         functools.partial(rim_kernel, rows, cols, shards, pick),
         [enc, relayed, weights[0], base, joined],
         [shape(pixels, chan)],
-        [pltpu.VMEM((pixels, width), F32)],
+        [pltpu.VMEM((pixels + cols, width), F32)],
     )[0]
     return out.reshape(1, rows, cols, chan)
 

time: 26.1 us -> 26.1 us (level)
  no operation moved by 1% of the time
where the time goes in v10:
time: 26.1 us; the launch traced here: 25.6 us
  starting transfers between devices  15 us (57%)
  waiting for transfers between devices  4.28 us (16%)
  Pallas kernels  3.64 us (14%)
  local copies, waits for them, and re-layouts  1.09 us (4%)
  other arithmetic  0.86 us (3%)
  between operations  0.75 us (3%)
    ppermute x6, starting transfers between devices, across(): return lax.ppermute(array, 'src', [(i, i ^ k) for i in range(4)])  12.1 us
    pallas_call x10, Pallas kernels, call(): pl.pallas_call(kernel, out_shape=outs, in_specs=[VMEM_SPEC] * len(ins), o...  3.64 us
    ppermute x6, waiting for transfers between devices, across(): return lax.ppermute(array, 'src', [(i, i ^ k) for i in range(4)])  1.9 us
    ppermute x1, starting transfers between devices, local(): beyond = [lax.ppermute(edges[0], 'slab', [(0, 1), (1, 0)])]  1.56 us
    ppermute x1, waiting for transfers between devices, local(): beyond = [lax.ppermute(edges[0], 'slab', [(0, 1), (1, 0)])]  1.54 us
    ppermute x4, starting transfers between devices, swap(): return lax.ppermute(array, 'shard', pairs + [(j, i) for i, j in pairs])  1.37 us
    unnamed x4, local copies, waits for them, and re-layouts  1.02 us
    ppermute x4, waiting for transfers between devices, swap(): return lax.ppermute(array, 'shard', pairs + [(j, i) for i, j in pairs])  0.84 us
  transfers between devices with their start and end apart: 11, of which 5 were waited for; matrix products, arithmetic and copies ran while one was open for 4% of the time, Pallas kernels for 10%

profile of v10, /device:TPU:0, one launch (start us, length us, event | category | flops | bytes accessed | tf_op | source)
XLA Modules:
  0.0 25.6 jit_solution(12340267054260455889)
XLA Ops:
  0.0 5.0 %collective-permute-start.5 = (bf16[512,256]{1,0:T(8,128)(2,1)}, bf16[512,256]{1,0:T(8,128)(2,1)S(1)}, u32[]{:S(2)}, u32[]{:S(2)}) collective-permute-start(bf16[512,256]{1,0:T(8,128)(2,1)} %bitcast.11), channel_id=1, source_target_pairs={{0,24},{8,16},{16,8},{24,0},{1,25},{9,17},{17,9},{25,1},{2,26},{10... | collective-permute-start | bytes 786440 | tf_op jit(solution)/shard_map/ppermute | solution.py:269
  5.0 0.0 collective-permute-start.4
  5.1 0.0 copy-start.1
  5.1 1.0 %copy-done.1 = bf16[1,32,16,256]{3,2,1,0:T(8,128)(2,1)S(1)} copy-done((bf16[1,32,16,256]{3,2,1,0:T(8,128)(2,1)S(1)}, bf16[1,32,16,256]{3,2,1,0:T(8,128)(2,1)}, u32[]{:S(2)}) %copy-start.1) | copy-done | bytes 262168
  6.1 0.1 shard_map.46
  6.1 0.1 collective-permute-start
  6.2 0.7 %collective-permute-start.1 = (bf16[32,256]{1,0:T(8,128)(2,1)S(1)}, bf16[32,256]{1,0:T(8,128)(2,1)S(1)}, u32[]{:S(2)}, u32[]{:S(2)}) collective-permute-start(bf16[32,256]{1,0:T(8,128)(2,1)S(1)} %get-tuple-element.26), channel_id=1, source_target_pairs={{2,4},{4,2},{3,5},{5,3},{10,12},{12,10},{11,13},{13,11},{18,20},{2... | collective-permute-start | bytes 49160 | tf_op jit(solution)/shard_map/ppermute | solution.py:288
  7.6 0.2 add_sine_fusion.enc
  7.8 0.0 collective-permute-done.got_a
  7.8 0.0 collective-permute-done.1.got_b
  7.8 1.6 %collective-permute-start.2 = (bf16[24,256]{1,0:T(8,128)(2,1)S(1)}, bf16[24,256]{1,0:T(8,128)(2,1)S(1)}, u32[]{:S(2)}, u32[]{:S(2)}) collective-permute-start(bf16[24,256]{1,0:T(8,128)(2,1)S(1)} %shard_map.47), channel_id=1, source_target_pairs={{0,1},{1,0},{2,3},{3,2},{4,5},{5,4},{6,7},{7,6},{8,9},{9,8},{10,11... | collective-permute-start | bytes 36872 | tf_op jit(solution)/shard_map/ppermute | solution.py:299
  9.4 0.7 %convert_bitcast_fusion = f32[2]{0:T(128)S(1)} fusion(s32[1,2]{1,0:T(1,128)} %param.5), kind=kLoop, calls=%fused_computation.13 | loop fusion | flops 2 | bytes 16 | tf_op jit(solution)/shard_map/broadcast_in_dim | solution.py:283
  10.0 0.0 copy-start
  10.0 1.5 %collective-permute-done.2.refs_0_ = bf16[24,256]{1,0:T(8,128)(2,1)S(1)} collective-permute-done((bf16[24,256]{1,0:T(8,128)(2,1)S(1)}, bf16[24,256]{1,0:T(8,128)(2,1)S(1)}, u32[]{:S(2)}, u32[]{:S(2)}) %collective-permute-start.2) | collective-permute-done | bytes 12320 | tf_op jit(solution)/shard_map/ppermute | solution.py:299
  11.6 0.6 %collective-permute-start.8 = (bf16[56,256]{1,0:T(8,128)(2,1)S(1)}, bf16[56,256]{1,0:T(8,128)(2,1)S(1)}, u32[]{:S(2)}, u32[]{:S(2)}) collective-permute-start(bf16[56,256]{1,0:T(8,128)(2,1)S(1)} %shard_map.48.strip), channel_id=1, source_target_pairs={{0,16},{8,24},{16,0},{24,8},{1,17},{9,25},{17,1},{25,9},{2,18},{10... | collective-permute-start | bytes 86024 | tf_op jit(solution)/shard_map/ppermute | solution.py:269
  12.2 1.5 %collective-permute-start.3 = (bf16[56,256]{1,0:T(8,128)(2,1)S(1)}, bf16[56,256]{1,0:T(8,128)(2,1)S(1)}, u32[]{:S(2)}, u32[]{:S(2)}) collective-permute-start(bf16[56,256]{1,0:T(8,128)(2,1)S(1)} %shard_map.48.strip), channel_id=1, source_target_pairs={{0,8},{8,0},{16,24},{24,16},{1,9},{9,1},{17,25},{25,17},{2,10},{10... | collective-permute-start | bytes 86024 | tf_op jit(solution)/shard_map/ppermute | solution.py:269
  13.7 0.0 collective-permute-done.5.view.far
  13.7 3.2 %collective-permute-start.10 = (bf16[512,256]{1,0:T(8,128)(2,1)S(1)}, bf16[512,256]{1,0:T(8,128)(2,1)S(1)}, u32[]{:S(2)}, u32[]{:S(2)}) collective-permute-start(bf16[512,256]{1,0:T(8,128)(2,1)S(1)} %collective-permute-done.5.view.far), channel_id=1, source_target_pairs={{0,8},{8,0},{16,24},{24,16},{1,9},{9,1},{17,25},{25,17},{2,10},{10... | collective-permute-start | bytes 786440 | tf_op jit(solution)/shard_map/ppermute | solution.py:269
  16.9 0.1 broadcast_in_dim.5.coords
  17.0 0.0 copy-done
  17.0 0.6 %shard_map.49 = (f32[512,256]{1,0:T(8,128)S(1)}, f32[528,128]{1,0:T(8,128)S(1)}) custom-call(f32[2,256]{1,0:T(2,128)S(1)} %broadcast_in_dim.5.coords, bf16[512,256]{1,0:T(8,128)(2,1)S(1)} %get-tuple-element.30.own, f32[32,256]{1,0:T(8,128)S(1)} %add_sine_fusion.enc, bf16[56,256]{1,0:T(8,128)(2,1)S(1)} %shard_map.48.strip, ...), custom_call_target="tpu_custom_call" | custom-call | flops 5000000000 | bytes 4000000 | tf_op jit(solution)/shard_map/pallas_call | solution.py:251
  17.6 0.0 collective-permute-done.4.view.near
  17.6 0.1 shard_map.50
  17.7 0.1 collective-permute-start.6
  17.8 0.1 shard_map.51
  17.8 0.5 %collective-permute-start.7 = (bf16[32,256]{1,0:T(8,128)(2,1)S(1)}, bf16[32,256]{1,0:T(8,128)(2,1)S(1)}, u32[]{:S(2)}, u32[]{:S(2)}) collective-permute-start(bf16[32,256]{1,0:T(8,128)(2,1)S(1)} %shard_map.51), channel_id=1, source_target_pairs={{0,2},{4,6},{2,0},{6,4},{1,3},{5,7},{3,1},{7,5},{8,10},{12,14},{10... | collective-permute-start | bytes 49160 | tf_op jit(solution)/shard_map/ppermute | solution.py:288
  18.4 0.0 collective-permute-done.8.strip.last_strip
  18.4 0.5 %collective-permute-done.6.near_a = bf16[32,256]{1,0:T(8,128)(2,1)S(1)} collective-permute-done((bf16[32,256]{1,0:T(8,128)(2,1)S(1)}, bf16[32,256]{1,0:T(8,128)(2,1)S(1)}, u32[]{:S(2)}, u32[]{:S(2)}) %collective-permute-start.6) | collective-permute-done | bytes 16416 | tf_op jit(solution)/shard_map/ppermute | solution.py:288
  18.9 0.3 %collective-permute-done.7.far_a = bf16[32,256]{1,0:T(8,128)(2,1)S(1)} collective-permute-done((bf16[32,256]{1,0:T(8,128)(2,1)S(1)}, bf16[32,256]{1,0:T(8,128)(2,1)S(1)}, u32[]{:S(2)}, u32[]{:S(2)}) %collective-permute-start.7) | collective-permute-done | bytes 16416 | tf_op jit(solution)/shard_map/ppermute | solution.py:288
  19.2 0.0 collective-permute-done.3.near_strip
  19.2 1.7 %collective-permute-start.9 = (bf16[88,256]{1,0:T(8,128)(2,1)S(1)}, bf16[88,256]{1,0:T(8,128)(2,1)S(1)}, u32[]{:S(2)}, u32[]{:S(2)}) collective-permute-start(bf16[88,256]{1,0:T(8,128)(2,1)S(1)} %shard_map.52), channel_id=1, source_target_pairs={{0,8},{8,0},{16,24},{24,16},{1,9},{9,1},{17,25},{25,17},{2,10},{10... | collective-permute-start | bytes 135176 | tf_op jit(solution)/shard_map/ppermute | solution.py:269
  20.9 1.2 %shard_map.53 = (f32[512,256]{1,0:T(8,128)S(1)}, f32[528,128]{1,0:T(8,128)S(1)}) custom-call(f32[2,256]{1,0:T(2,128)S(1)} %broadcast_in_dim.5.coords, bf16[512,256]{1,0:T(8,128)(2,1)S(1)} %collective-permute-done.4.view.near, bf16[512,256]{1,0:T(8,128)(2,1)S(1)} %collective-permute-done.5.view.far, f32[32,256]{1,0:T(8,128)S(1)} %add_sine_fusion.enc, ...), custom_call_target="tpu_custom_call" | custom-call | tf_op jit(solution)/shard_map/pallas_call | solution.py:251
  22.2 1.5 %collective-permute-done.10.last = bf16[512,256]{1,0:T(8,128)(2,1)S(1)} collective-permute-done((bf16[512,256]{1,0:T(8,128)(2,1)S(1)}, bf16[512,256]{1,0:T(8,128)(2,1)S(1)}, u32[]{:S(2)}, u32[]{:S(2)}) %collective-permute-start.10) | collective-permute-done | bytes 262176 | tf_op jit(solution)/shard_map/ppermute | solution.py:269
  23.7 0.6 %shard_map.54 = (f32[512,256]{1,0:T(8,128)S(1)}, f32[528,128]{1,0:T(8,128)S(1)}) custom-call(f32[2,256]{1,0:T(2,128)S(1)} %broadcast_in_dim.5.coords, bf16[512,256]{1,0:T(8,128)(2,1)S(1)} %collective-permute-done.10.last, f32[32,256]{1,0:T(8,128)S(1)} %add_sine_fusion.enc, bf16[2,9,512,128]{3,2,1,0:T(8,128)(2,1)S(1)} %bitcast.9, ...), custom_call_target="tpu_custom_call" | custom-call | tf_op jit(solution)/shard_map/pallas_call | solution.py:251
  24.2 0.4 %collective-permute-done.9.relayed = bf16[88,256]{1,0:T(8,128)(2,1)S(1)} collective-permute-done((bf16[88,256]{1,0:T(8,128)(2,1)S(1)}, bf16[88,256]{1,0:T(8,128)(2,1)S(1)}, u32[]{:S(2)}, u32[]{:S(2)}) %collective-permute-start.9) | collective-permute-done | bytes 45088 | tf_op jit(solution)/shard_map/ppermute | solution.py:269
  24.6 1.0 %shard_map.55 = bf16[512,256]{1,0:T(8,128)(2,1)} custom-call(f32[32,256]{1,0:T(8,128)S(1)} %add_sine_fusion.enc, bf16[88,256]{1,0:T(8,128)(2,1)S(1)} %collective-permute-done.9.relayed, bf16[2,9,512,128]{3,2,1,0:T(8,128)(2,1)S(1)} %bitcast.10, f32[512,256]{1,0:T(8,128)S(1)} %get-tuple-element.43.base, f32[528,128]{1,0:T(8,128)S(1)} %get-tuple-element.44.joined_in), custom_call_target="tpu_custom_call" | custom-call | tf_op jit(solution)/shard_map/pallas_call | solution.py:251
  (5 shorter events, 0.1 us)
Async XLA Ops:
  0.0 13.7 %collective-permute-start.5 = (bf16[512,256]{1,0:T(8,128)(2,1)}, bf16[512,256]{1,0:T(8,128)(2,1)S(1)}, u32[]{:S(2)}, u32[]{:S(2)}) collective-permute-start(bf16[512,256]{1,0:T(8,128)(2,1)} %bitcast.11), channel_id=1, source_target_pairs={{0,24},{8,16},{16,8},{24,0},{1,25},{9,17},{17,9},{25,1},{2,26},{10... | collective-permute-start | bytes 786440 | tf_op jit(solution)/shard_map/ppermute | solution.py:269
  5.0 12.5 %collective-permute-start.4 = (bf16[512,256]{1,0:T(8,128)(2,1)}, bf16[512,256]{1,0:T(8,128)(2,1)S(1)}, u32[]{:S(2)}, u32[]{:S(2)}) collective-permute-start(bf16[512,256]{1,0:T(8,128)(2,1)} %bitcast.12), channel_id=1, source_target_pairs={{0,8},{8,0},{16,24},{24,16},{1,9},{9,1},{17,25},{25,17},{2,10},{10... | collective-permute-start | bytes 786440 | tf_op jit(solution)/shard_map/ppermute | solution.py:269
  5.1 1.0 %copy-start.1 = (bf16[1,32,16,256]{3,2,1,0:T(8,128)(2,1)S(1)}, bf16[1,32,16,256]{3,2,1,0:T(8,128)(2,1)}, u32[]{:S(2)}) copy-start(bf16[1,32,16,256]{3,2,1,0:T(8,128)(2,1)} %param.4) | copy-start | bytes 786436
  6.1 1.6 %collective-permute-start = (bf16[32,256]{1,0:T(8,128)(2,1)S(1)}, bf16[32,256]{1,0:T(8,128)(2,1)S(1)}, u32[]{:S(2)}, u32[]{:S(2)}) collective-permute-start(bf16[32,256]{1,0:T(8,128)(2,1)S(1)} %get-tuple-element.25), channel_id=1, source_target_pairs={{0,2},{4,6},{2,0},{6,4},{1,3},{5,7},{3,1},{7,5},{8,10},{12,14},{10... | collective-permute-start | bytes 49160 | tf_op jit(solution)/shard_map/ppermute | solution.py:288
  6.2 1.6 %collective-permute-start.1 = (bf16[32,256]{1,0:T(8,128)(2,1)S(1)}, bf16[32,256]{1,0:T(8,128)(2,1)S(1)}, u32[]{:S(2)}, u32[]{:S(2)}) collective-permute-start(bf16[32,256]{1,0:T(8,128)(2,1)S(1)} %get-tuple-element.26), channel_id=1, source_target_pairs={{2,4},{4,2},{3,5},{5,3},{10,12},{12,10},{11,13},{13,11},{18,20},{2... | collective-permute-start | bytes 49160 | tf_op jit(solution)/shard_map/ppermute | solution.py:288
  7.8 3.8 %collective-permute-start.2 = (bf16[24,256]{1,0:T(8,128)(2,1)S(1)}, bf16[24,256]{1,0:T(8,128)(2,1)S(1)}, u32[]{:S(2)}, u32[]{:S(2)}) collective-permute-start(bf16[24,256]{1,0:T(8,128)(2,1)S(1)} %shard_map.47), channel_id=1, source_target_pairs={{0,1},{1,0},{2,3},{3,2},{4,5},{5,4},{6,7},{7,6},{8,9},{9,8},{10,11... | collective-permute-start | bytes 36872 | tf_op jit(solution)/shard_map/ppermute | solution.py:299
  10.0 6.9 %copy-start = (bf16[1,2,9,512,128]{4,3,2,1,0:T(8,128)(2,1)S(1)}, bf16[1,2,9,512,128]{4,3,2,1,0:T(8,128)(2,1)}, u32[]{:S(2)}) copy-start(bf16[1,2,9,512,128]{4,3,2,1,0:T(8,128)(2,1)} %param.7) | copy-start | bytes 7077892
  11.6 6.8 %collective-permute-start.8 = (bf16[56,256]{1,0:T(8,128)(2,1)S(1)}, bf16[56,256]{1,0:T(8,128)(2,1)S(1)}, u32[]{:S(2)}, u32[]{:S(2)}) collective-permute-start(bf16[56,256]{1,0:T(8,128)(2,1)S(1)} %shard_map.48.strip), channel_id=1, source_target_pairs={{0,16},{8,24},{16,0},{24,8},{1,17},{9,25},{17,1},{25,9},{2,18},{10... | collective-permute-start | bytes 86024 | tf_op jit(solution)/shard_map/ppermute | solution.py:269
  12.2 7.0 %collective-permute-start.3 = (bf16[56,256]{1,0:T(8,128)(2,1)S(1)}, bf16[56,256]{1,0:T(8,128)(2,1)S(1)}, u32[]{:S(2)}, u32[]{:S(2)}) collective-permute-start(bf16[56,256]{1,0:T(8,128)(2,1)S(1)} %shard_map.48.strip), channel_id=1, source_target_pairs={{0,8},{8,0},{16,24},{24,16},{1,9},{9,1},{17,25},{25,17},{2,10},{10... | collective-permute-start | bytes 86024 | tf_op jit(solution)/shard_map/ppermute | solution.py:269
  13.7 9.9 %collective-permute-start.10 = (bf16[512,256]{1,0:T(8,128)(2,1)S(1)}, bf16[512,256]{1,0:T(8,128)(2,1)S(1)}, u32[]{:S(2)}, u32[]{:S(2)}) collective-permute-start(bf16[512,256]{1,0:T(8,128)(2,1)S(1)} %collective-permute-done.5.view.far), channel_id=1, source_target_pairs={{0,8},{8,0},{16,24},{24,16},{1,9},{9,1},{17,25},{25,17},{2,10},{10... | collective-permute-start | bytes 786440 | tf_op jit(solution)/shard_map/ppermute | solution.py:269
  17.7 1.2 %collective-permute-start.6 = (bf16[32,256]{1,0:T(8,128)(2,1)S(1)}, bf16[32,256]{1,0:T(8,128)(2,1)S(1)}, u32[]{:S(2)}, u32[]{:S(2)}) collective-permute-start(bf16[32,256]{1,0:T(8,128)(2,1)S(1)} %shard_map.50), channel_id=1, source_target_pairs={{0,2},{4,6},{2,0},{6,4},{1,3},{5,7},{3,1},{7,5},{8,10},{12,14},{10... | collective-permute-start | bytes 49160 | tf_op jit(solution)/shard_map/ppermute | solution.py:288
  17.8 1.4 %collective-permute-start.7 = (bf16[32,256]{1,0:T(8,128)(2,1)S(1)}, bf16[32,256]{1,0:T(8,128)(2,1)S(1)}, u32[]{:S(2)}, u32[]{:S(2)}) collective-permute-start(bf16[32,256]{1,0:T(8,128)(2,1)S(1)} %shard_map.51), channel_id=1, source_target_pairs={{0,2},{4,6},{2,0},{6,4},{1,3},{5,7},{3,1},{7,5},{8,10},{12,14},{10... | collective-permute-start | bytes 49160 | tf_op jit(solution)/shard_map/ppermute | solution.py:288
  19.2 5.4 %collective-permute-start.9 = (bf16[88,256]{1,0:T(8,128)(2,1)S(1)}, bf16[88,256]{1,0:T(8,128)(2,1)S(1)}, u32[]{:S(2)}, u32[]{:S(2)}) collective-permute-start(bf16[88,256]{1,0:T(8,128)(2,1)S(1)} %shard_map.52), channel_id=1, source_target_pairs={{0,8},{8,0},{16,24},{24,16},{1,9},{9,1},{17,25},{25,17},{2,10},{10... | collective-permute-start | bytes 135176 | tf_op jit(solution)/shard_map/ppermute | solution.py:269

commit v11 on v9

--- a/solution.py
+++ b/solution.py
@@ -11,6 +11,7 @@
 BF16, F32 = jnp.bfloat16, jnp.float32
 VMEM_SPEC = pl.BlockSpec(memory_space=pltpu.VMEM)
 LANES = 128
+PARTS = 2
 BLOCKS = 4
 
 
@@ -34,7 +35,7 @@
 
 def column(rows, cols, view, wide, pick_last):
     for c, lanes in tiles(view.shape[1]):
-        wide[c] = view[:, lanes].astype(F32)
+        wide[c, 0 : rows * cols, :] = view[:, lanes].astype(F32)
         first = wide[c, pl.ds(0, rows, stride=cols), :]
         last = wide[c, pl.ds(cols - 1, rows, stride=cols), :]
         yield lanes, jnp.where(pick_last, last, first), jnp.where(pick_last, first, last)
@@ -86,18 +87,22 @@
         outs[1][...] = lines[1].astype(BF16)
 
 
-def strip_kernel(rows, shards, got_a, got_b, enc, *refs):
-    out, at = refs[-1], rows
+def strip_kernel(rows, shards, got_a, got_b, enc, panel, *refs):
+    *beyond, out, longer = refs
+    at = rows
     out[0:rows, :] = pose(shards, got_b, enc, False).astype(BF16)
-    for ref in refs[:-1]:
+    for ref in beyond:
         out[at : at + ref.shape[0], :] = ref[...]
         at += ref.shape[0]
+    size = longer.shape[0] - at
+    longer[0:size, :] = panel[0:size, :]
+    longer[size:, :] = out[...]
 
 
 def relay_kernel(strip, far_a, out):
     rows = far_a.shape[0]
     out[0:rows, :] = far_a[...]
-    out[rows:, :] = strip[0 : out.shape[0] - rows, :]
+    out[rows:, :] = strip[strip.shape[0] - (out.shape[0] - rows) :, :]
 
 
 def neighbours(rows, cols, shards, pick, enc, strip, raw_a):
@@ -124,11 +129,13 @@
 
 def inside(rows, cols, k, coords, view, enc, weights, base_in, base, joined, panel):
     weight = blend_weight(coords, jnp.bitwise_xor(lax.axis_index("src"), k))
-    chan, width = view.shape[1], joined.shape[1]
+    chan, width = panel.shape[1], joined.shape[1]
     pixels = rows * cols
-    for h in range(rows):
+    views = view if isinstance(view, tuple) else (view,)
+    lines = [part[i : i + cols, :] for part in views for i in range(0, part.shape[0], cols)]
+    for h, line in enumerate(lines):
         here = slice(h * cols, (h + 1) * cols)
-        posed = (view[here, :].astype(F32) + enc[h : h + 1, :]).astype(BF16)
+        posed = (line.astype(F32) + enc[h : h + 1, :]).astype(BF16)
         part = weight * posed.astype(F32)
         base[here, :] = part if base_in is None else base_in[here, :] + part
         panel[here, :] = posed
@@ -146,7 +153,7 @@
     )
     column = lax.rem(lax.broadcasted_iota(jnp.int32, (pixels, width), 0), cols)
     zero = jnp.zeros((cols, width), F32)
-    total = joined[...]
+    total = joined[0:pixels, :]
     for b in (1, 0, 2):
         up, level, down = (taps[:, (3 * b + a) * width : (3 * b + a + 1) * width] for a in range(3))
         part = level + jnp.concatenate([zero, up[: pixels - cols]], axis=0)
@@ -156,7 +163,7 @@
         if b == 2:
             part = jnp.where(column == cols - 1, 0.0, pltpu.roll(part, pixels - 1, 0))
         total = total + part
-    joined[...] = total
+    joined[0:pixels, :] = total
 
 
 def add_line(joined, where, line, weights, group, at, taps):
@@ -205,7 +212,7 @@
     add_rows(rows, cols, pick, joined, weights, 0, before, after)
 
 
-def middle_kernel(rows, cols, shards, pick, coords, near, far, enc, near_strip, last_strip, near_a,
+def middle_kernel(rows, cols, shards, pick, direct, coords, near, far, enc, near_strip, last_strip, near_a,
                   far_a, weights, base_in, joined_in, base, joined, panel):
     me = lax.axis_index("src")
     width = joined.shape[1]
@@ -215,20 +222,22 @@
     add_columns(rows, cols, joined, weights, a, 1, b, 1)
     add_rows(rows, cols, pick, joined, weights, 1, before, after)
     here = pl.ds(pl.multiple_of(lax.div(me, 2) * width, width), width)
-    base[:, here] = base[:, here] + silu(joined[...])
-    a, b, before, after = neighbours(rows, cols, shards, pick, enc, last_strip, far_a)
+    base[:, here] = base[:, here] + silu(joined[0 : rows * cols, :])
+    a, b, before, after = neighbours(rows, cols, shards, pick, enc, last_strip[direct:, :], far_a)
     joined[...] = jnp.zeros_like(joined)
     inside(rows, cols, 3, coords, far, enc, weights, base, base, joined, panel)
     add_columns(rows, cols, joined, weights, a, 3, b, 2)
     add_rows(rows, cols, pick, joined, weights, 2, before, after)
 
 
-def last_kernel(rows, cols, coords, last, enc, weights, base_in, joined_in, base, joined, panel):
+def last_kernel(rows, cols, coords, first, last, enc, weights, base_in, joined_in, base, joined, panel):
     joined[...] = joined_in[...]
-    inside(rows, cols, 2, coords, last, enc, weights, base_in, base, joined, panel)
-
-
-def rim_kernel(rows, cols, shards, pick, enc, relayed, weights, base, joined_in, out, joined):
+    first = first[0 : rows * cols - last.shape[0], :]
+    inside(rows, cols, 2, coords, (first, last), enc, weights, base_in, base, joined, panel)
+
+
+def rim_kernel(rows, cols, shards, pick, enc, relayed, weights, base, joined_in, out, joined,
+               ready, sems):
     chan, width = out.shape[1], joined.shape[1]
     last_a, b, before, after = neighbours(
         rows, cols, shards, pick, enc, relayed[rows:, :], relayed[0:rows, :]
@@ -237,22 +246,29 @@
     add_columns(rows, cols, joined, weights, last_a, 2, b, 3)
     add_rows(rows, cols, pick, joined, weights, 3, before, after)
     group = where_of(2, chan)[0]
-    added = silu(joined[...])
-    for c, lanes in tiles(chan):
-        here = group == c * LANES // width
-        out[:, lanes] = (base[:, lanes] + jnp.where(here, added, 0.0)).astype(BF16)
+    size, copies = rows * cols // PARTS, []
+    for i in range(PARTS):
+        some = slice(i * size, (i + 1) * size)
+        added = silu(joined[some, :])
+        for c, lanes in tiles(chan):
+            here = group == c * LANES // width
+            ready[some, lanes] = (base[some, lanes] + jnp.where(here, added, 0.0)).astype(BF16)
+        copies.append(pltpu.make_async_copy(ready.at[some], out.at[some], sems.at[i]))
+        copies[-1].start()
+    for copy in copies:
+        copy.wait()
 
 
 def shape(rows, chan, dtype=BF16):
     return jax.ShapeDtypeStruct((rows, chan), dtype)
 
 
-def call(kernel, ins, outs, scratch=(), cost=None):
+def call(kernel, ins, outs, scratch=(), cost=None, out_spec=VMEM_SPEC):
     return pl.pallas_call(
         kernel,
         out_shape=outs,
         in_specs=[VMEM_SPEC] * len(ins),
-        out_specs=jax.tree.map(lambda _: VMEM_SPEC, outs),
+        out_specs=jax.tree.map(lambda _: out_spec, outs),
         scratch_shapes=list(scratch),
         compiler_params=pltpu.CompilerParams(vmem_limit_bytes=32 * 1024 * 1024),
         cost_estimate=cost,
@@ -278,7 +294,7 @@
         functools.partial(columns_kernel, rows, cols),
         [own],
         [line, line, shape(2 * cols, chan), shape(pixels, chan)],
-        [pltpu.VMEM((chan // LANES, pixels, LANES), F32)],
+        [pltpu.VMEM((chan // LANES, pixels + cols, LANES), F32)],
     )
     place = jnp.broadcast_to(coords.astype(F32).reshape(2, 1), (2, chan))
     shards, slabs = lax.axis_size("shard"), lax.axis_size("slab")
@@ -303,28 +319,30 @@
             lax.ppermute(edges[1], "slab", up),
             lax.ppermute(edges[0], "slab", [(j, i) for i, j in up]),
         ]
-    strip = call(
+    direct = rows // 8 * cols
+    strip_rows = rows + len(beyond) * (cols + 8)
+    strip, longer = call(
         functools.partial(strip_kernel, rows, shards),
-        [got_a, got_b, enc, *beyond],
-        [shape(rows + len(beyond) * (cols + 8), chan)],
+        [got_a, got_b, enc, panel, *beyond],
+        [shape(strip_rows, chan), shape(strip_rows + direct, chan)],
         cost=pl.CostEstimate(flops=2_000_000_000, bytes_accessed=0, transcendentals=0),
-    )[0]
-    near_strip, last_strip = across(strip, 1), across(strip, 2)
+    )
+    near_strip, last_strip = across(strip, 1), across(longer, 2)
     far, panel = lax.optimization_barrier((far, panel))
-    last = across(far, 1)
+    last = across(far[direct:], 1)
 
     def beside(view):
         out = call(
             functools.partial(inner_kernel, rows, cols),
             [view],
             [line],
-            [pltpu.VMEM((chan // LANES, pixels, LANES), F32)],
+            [pltpu.VMEM((chan // LANES, pixels + cols, LANES), F32)],
         )[0]
         return swap(out, 0)
 
 
     scratch = [pltpu.VMEM((pixels, chan), BF16)]
-    sums = [shape(pixels, chan, F32), shape(pixels, width, F32)]
+    sums = [shape(pixels, chan, F32), shape(pixels + cols, width, F32)]
     cost = pl.CostEstimate(flops=5000000000, bytes_accessed=4_000_000, transcendentals=0)
     base, joined = call(
         functools.partial(own_kernel, rows, cols, shards, pick),
@@ -338,11 +356,11 @@
     near_a, far_a, last_strip = lax.optimization_barrier((near_a, far_a, last_strip))
     near_strip, last_strip = lax.optimization_barrier((near_strip, last_strip))
     relayed = call(
-        relay_kernel, [last_strip, far_a], [shape(strip.shape[0] + rows, chan)]
+        relay_kernel, [last_strip, far_a], [shape(strip_rows + rows, chan)]
     )[0]
     relayed = across(relayed, 1)
     base, joined = call(
-        functools.partial(middle_kernel, rows, cols, shards, pick),
+        functools.partial(middle_kernel, rows, cols, shards, pick, direct),
         [place, near, far, enc, near_strip, last_strip, near_a, far_a, weights[0], base, joined],
         sums,
         scratch,
@@ -350,7 +368,7 @@
     )
     base, joined = call(
         functools.partial(last_kernel, rows, cols),
-        [place, last, enc, weights[0], base, joined],
+        [place, last_strip, last, enc, weights[0], base, joined],
         sums,
         scratch,
         cost=pl.CostEstimate(flops=0, bytes_accessed=0, transcendentals=0),
@@ -359,7 +377,12 @@
         functools.partial(rim_kernel, rows, cols, shards, pick),
         [enc, relayed, weights[0], base, joined],
         [shape(pixels, chan)],
-        [pltpu.VMEM((pixels, width), F32)],
+        [
+            pltpu.VMEM((pixels + cols, width), F32),
+            pltpu.VMEM((pixels, chan), BF16),
+            pltpu.SemaphoreType.DMA((PARTS,)),
+        ],
+        out_spec=pl.BlockSpec(memory_space=pl.ANY),
     )[0]
     return out.reshape(1, rows, cols, chan)
 

time: 26.1 us -> 25.9 us (level); the launches traced: 25.6 us -> 25.8 us
  transfers between devices with their start and end apart: 11 -> 11, of which waited for: 5 -> 6; matrix products, arithmetic and copies ran while one was open for 4% -> 4% of each run, Pallas kernels for 10% -> 10%
where the time goes in v11:
time: 25.9 us; the launch traced here: 25.8 us
  starting transfers between devices  15.2 us (59%)
  waiting for transfers between devices  4.26 us (16%)
  Pallas kernels  3.65 us (14%)
  local copies, waits for them, and re-layouts  1.1 us (4%)
  other arithmetic  0.86 us (3%)
  between operations  0.75 us (3%)
    ppermute x6, starting transfers between devices, across(): return lax.ppermute(array, 'src', [(i, i ^ k) for i in range(4)])  12.2 us
    pallas_call x10, Pallas kernels, call(): pl.pallas_call(kernel, out_shape=outs, in_specs=[VMEM_SPEC] * len(ins), o...  3.65 us
    ppermute x6, waiting for transfers between devices, across(): return lax.ppermute(array, 'src', [(i, i ^ k) for i in range(4)])  1.87 us
    ppermute x1, starting transfers between devices, local(): beyond = [lax.ppermute(edges[0], 'slab', [(0, 1), (1, 0)])]  1.56 us
    ppermute x1, waiting for transfers between devices, local(): beyond = [lax.ppermute(edges[0], 'slab', [(0, 1), (1, 0)])]  1.55 us
    ppermute x4, starting transfers between devices, swap(): return lax.ppermute(array, 'shard', pairs + [(j, i) for i, j in pairs])  1.37 us
    unnamed x4, local copies, waits for them, and re-layouts  1.02 us
    ppermute x4, waiting for transfers between devices, swap(): return lax.ppermute(array, 'shard', pairs + [(j, i) for i, j in pairs])  0.84 us
  transfers between devices with their start and end apart: 11, of which 6 were waited for; matrix products, arithmetic and copies ran while one was open for 4% of the time, Pallas kernels for 10%

profile of v11, /device:TPU:0, one launch (start us, length us, event | category | flops | bytes accessed | tf_op | source)
XLA Modules:
  0.0 25.8 jit_solution(7111985738140401767)
XLA Ops:
  0.0 5.0 %collective-permute-start.5 = (bf16[512,256]{1,0:T(8,128)(2,1)}, bf16[512,256]{1,0:T(8,128)(2,1)S(1)}, u32[]{:S(2)}, u32[]{:S(2)}) collective-permute-start(bf16[512,256]{1,0:T(8,128)(2,1)} %bitcast.11), channel_id=1, source_target_pairs={{0,24},{8,16},{16,8},{24,0},{1,25},{9,17},{17,9},{25,1},{2,26},{10... | collective-permute-start | bytes 786440 | tf_op jit(solution)/shard_map/ppermute | solution.py:285
  5.0 0.0 collective-permute-start.4
  5.1 0.0 copy-start.1
  5.1 1.0 %copy-done.1 = bf16[1,32,16,256]{3,2,1,0:T(8,128)(2,1)S(1)} copy-done((bf16[1,32,16,256]{3,2,1,0:T(8,128)(2,1)S(1)}, bf16[1,32,16,256]{3,2,1,0:T(8,128)(2,1)}, u32[]{:S(2)}) %copy-start.1) | copy-done | bytes 262168
  6.1 0.1 shard_map.46
  6.1 0.1 collective-permute-start
  6.2 0.7 %collective-permute-start.1 = (bf16[32,256]{1,0:T(8,128)(2,1)S(1)}, bf16[32,256]{1,0:T(8,128)(2,1)S(1)}, u32[]{:S(2)}, u32[]{:S(2)}) collective-permute-start(bf16[32,256]{1,0:T(8,128)(2,1)S(1)} %get-tuple-element.28), channel_id=1, source_target_pairs={{2,4},{4,2},{3,5},{5,3},{10,12},{12,10},{11,13},{13,11},{18,20},{2... | collective-permute-start | bytes 49160 | tf_op jit(solution)/shard_map/ppermute | solution.py:304
  7.6 0.2 add_sine_fusion.enc
  7.8 0.0 collective-permute-done.got_a
  7.8 0.0 collective-permute-done.1.got_b
  7.8 1.6 %collective-permute-start.2 = (bf16[24,256]{1,0:T(8,128)(2,1)S(1)}, bf16[24,256]{1,0:T(8,128)(2,1)S(1)}, u32[]{:S(2)}, u32[]{:S(2)}) collective-permute-start(bf16[24,256]{1,0:T(8,128)(2,1)S(1)} %shard_map.47), channel_id=1, source_target_pairs={{0,1},{1,0},{2,3},{3,2},{4,5},{5,4},{6,7},{7,6},{8,9},{9,8},{10,11... | collective-permute-start | bytes 36872 | tf_op jit(solution)/shard_map/ppermute | solution.py:315
  9.4 0.7 %convert_bitcast_fusion = f32[2]{0:T(128)S(1)} fusion(s32[1,2]{1,0:T(1,128)} %param.5), kind=kLoop, calls=%fused_computation.13 | loop fusion | flops 2 | bytes 16 | tf_op jit(solution)/shard_map/broadcast_in_dim | solution.py:299
  10.0 1.5 %collective-permute-done.2.refs_0_ = bf16[24,256]{1,0:T(8,128)(2,1)S(1)} collective-permute-done((bf16[24,256]{1,0:T(8,128)(2,1)S(1)}, bf16[24,256]{1,0:T(8,128)(2,1)S(1)}, u32[]{:S(2)}, u32[]{:S(2)}) %collective-permute-start.2) | collective-permute-done | bytes 12320 | tf_op jit(solution)/shard_map/ppermute | solution.py:315
  11.6 0.0 copy-start
  11.6 0.6 %collective-permute-start.8 = (bf16[120,256]{1,0:T(8,128)(2,1)S(1)}, bf16[120,256]{1,0:T(8,128)(2,1)S(1)}, u32[]{:S(2)}, u32[]{:S(2)}) collective-permute-start(bf16[120,256]{1,0:T(8,128)(2,1)S(1)} %get-tuple-element.37), channel_id=1, source_target_pairs={{0,16},{8,24},{16,0},{24,8},{1,17},{9,25},{17,1},{25,9},{2,18},{10... | collective-permute-start | bytes 184328 | tf_op jit(solution)/shard_map/ppermute | solution.py:285
  12.2 1.5 %collective-permute-start.3 = (bf16[56,256]{1,0:T(8,128)(2,1)S(1)}, bf16[56,256]{1,0:T(8,128)(2,1)S(1)}, u32[]{:S(2)}, u32[]{:S(2)}) collective-permute-start(bf16[56,256]{1,0:T(8,128)(2,1)S(1)} %get-tuple-element.31.strip), channel_id=1, source_target_pairs={{0,8},{8,0},{16,24},{24,16},{1,9},{9,1},{17,25},{25,17},{2,10},{10... | collective-permute-start | bytes 86024 | tf_op jit(solution)/shard_map/ppermute | solution.py:285
  13.7 0.0 collective-permute-done.5.view.far
  13.8 3.2 %collective-permute-start.10 = (bf16[448,256]{1,0:T(8,128)(2,1)S(1)}, bf16[448,256]{1,0:T(8,128)(2,1)S(1)}, u32[]{:S(2)}, u32[]{:S(2)}) collective-permute-start(bf16[448,256]{1,0:T(8,128)(2,1)S(1)} %slice.3), channel_id=1, source_target_pairs={{0,8},{8,0},{16,24},{24,16},{1,9},{9,1},{17,25},{25,17},{2,10},{10... | collective-permute-start | bytes 688136 | tf_op jit(solution)/shard_map/ppermute | solution.py:285
  17.0 0.1 broadcast_in_dim.5.coords
  17.1 0.0 copy-done
  17.1 0.6 %shard_map.49 = (f32[512,256]{1,0:T(8,128)S(1)}, f32[528,128]{1,0:T(8,128)S(1)}) custom-call(f32[2,256]{1,0:T(2,128)S(1)} %broadcast_in_dim.5.coords, bf16[512,256]{1,0:T(8,128)(2,1)S(1)} %get-tuple-element.33.panel.own, f32[32,256]{1,0:T(8,128)S(1)} %add_sine_fusion.enc, bf16[56,256]{1,0:T(8,128)(2,1)S(1)} %get-tuple-element.31.strip, ...), custom_call_target="tpu_custom_call" | custom-call | flops 5000000000 | bytes 4000000 | tf_op jit(solution)/shard_map/pallas_call | solution.py:267
  17.7 0.3 %collective-permute-done.4.view.near = bf16[512,256]{1,0:T(8,128)(2,1)S(1)} collective-permute-done((bf16[512,256]{1,0:T(8,128)(2,1)}, bf16[512,256]{1,0:T(8,128)(2,1)S(1)}, u32[]{:S(2)}, u32[]{:S(2)}) %collective-permute-start.4) | collective-permute-done | bytes 262176 | tf_op jit(solution)/shard_map/ppermute | solution.py:285
  17.9 0.1 shard_map.50
  18.0 0.1 collective-permute-start.6
  18.1 0.1 shard_map.51
  18.1 0.6 %collective-permute-start.7 = (bf16[32,256]{1,0:T(8,128)(2,1)S(1)}, bf16[32,256]{1,0:T(8,128)(2,1)S(1)}, u32[]{:S(2)}, u32[]{:S(2)}) collective-permute-start(bf16[32,256]{1,0:T(8,128)(2,1)S(1)} %shard_map.51), channel_id=1, source_target_pairs={{0,2},{4,6},{2,0},{6,4},{1,3},{5,7},{3,1},{7,5},{8,10},{12,14},{10... | collective-permute-start | bytes 49160 | tf_op jit(solution)/shard_map/ppermute | solution.py:304
  18.7 0.0 collective-permute-done.8.strip.last_strip.first
  18.7 0.5 %collective-permute-done.6.near_a = bf16[32,256]{1,0:T(8,128)(2,1)S(1)} collective-permute-done((bf16[32,256]{1,0:T(8,128)(2,1)S(1)}, bf16[32,256]{1,0:T(8,128)(2,1)S(1)}, u32[]{:S(2)}, u32[]{:S(2)}) %collective-permute-start.6) | collective-permute-done | bytes 16416 | tf_op jit(solution)/shard_map/ppermute | solution.py:304
  19.3 0.3 %collective-permute-done.7.far_a = bf16[32,256]{1,0:T(8,128)(2,1)S(1)} collective-permute-done((bf16[32,256]{1,0:T(8,128)(2,1)S(1)}, bf16[32,256]{1,0:T(8,128)(2,1)S(1)}, u32[]{:S(2)}, u32[]{:S(2)}) %collective-permute-start.7) | collective-permute-done | bytes 16416 | tf_op jit(solution)/shard_map/ppermute | solution.py:304
  19.5 0.0 collective-permute-done.3.near_strip
  19.6 1.8 %collective-permute-start.9 = (bf16[88,256]{1,0:T(8,128)(2,1)S(1)}, bf16[88,256]{1,0:T(8,128)(2,1)S(1)}, u32[]{:S(2)}, u32[]{:S(2)}) collective-permute-start(bf16[88,256]{1,0:T(8,128)(2,1)S(1)} %shard_map.52), channel_id=1, source_target_pairs={{0,8},{8,0},{16,24},{24,16},{1,9},{9,1},{17,25},{25,17},{2,10},{10... | collective-permute-start | bytes 135176 | tf_op jit(solution)/shard_map/ppermute | solution.py:285
  21.4 1.2 %shard_map.53 = (f32[512,256]{1,0:T(8,128)S(1)}, f32[528,128]{1,0:T(8,128)S(1)}) custom-call(f32[2,256]{1,0:T(2,128)S(1)} %broadcast_in_dim.5.coords, bf16[512,256]{1,0:T(8,128)(2,1)S(1)} %collective-permute-done.4.view.near, bf16[512,256]{1,0:T(8,128)(2,1)S(1)} %collective-permute-done.5.view.far, f32[32,256]{1,0:T(8,128)S(1)} %add_sine_fusion.enc, ...), custom_call_target="tpu_custom_call" | custom-call | tf_op jit(solution)/shard_map/pallas_call | solution.py:267
  22.6 1.2 %collective-permute-done.10.last = bf16[448,256]{1,0:T(8,128)(2,1)S(1)} collective-permute-done((bf16[448,256]{1,0:T(8,128)(2,1)S(1)}, bf16[448,256]{1,0:T(8,128)(2,1)S(1)}, u32[]{:S(2)}, u32[]{:S(2)}) %collective-permute-start.10) | collective-permute-done | bytes 229408 | tf_op jit(solution)/shard_map/ppermute | solution.py:285
  23.8 0.6 %shard_map.54 = (f32[512,256]{1,0:T(8,128)S(1)}, f32[528,128]{1,0:T(8,128)S(1)}) custom-call(f32[2,256]{1,0:T(2,128)S(1)} %broadcast_in_dim.5.coords, bf16[120,256]{1,0:T(8,128)(2,1)S(1)} %collective-permute-done.8.strip.last_strip.first, bf16[448,256]{1,0:T(8,128)(2,1)S(1)} %collective-permute-done.10.last, f32[32,256]{1,0:T(8,128)S(1)} %add_sine_fusion.enc, ...), custom_call_target="tpu_custom_call" | custom-call | tf_op jit(solution)/shard_map/pallas_call | solution.py:267
  24.4 0.4 %collective-permute-done.9.relayed = bf16[88,256]{1,0:T(8,128)(2,1)S(1)} collective-permute-done((bf16[88,256]{1,0:T(8,128)(2,1)S(1)}, bf16[88,256]{1,0:T(8,128)(2,1)S(1)}, u32[]{:S(2)}, u32[]{:S(2)}) %collective-permute-start.9) | collective-permute-done | bytes 45088 | tf_op jit(solution)/shard_map/ppermute | solution.py:285
  24.8 1.0 %shard_map.55 = bf16[512,256]{1,0:T(8,128)(2,1)} custom-call(f32[32,256]{1,0:T(8,128)S(1)} %add_sine_fusion.enc, bf16[88,256]{1,0:T(8,128)(2,1)S(1)} %collective-permute-done.9.relayed, bf16[2,9,512,128]{3,2,1,0:T(8,128)(2,1)S(1)} %bitcast.10, f32[512,256]{1,0:T(8,128)S(1)} %get-tuple-element.47.base, f32[528,128]{1,0:T(8,128)S(1)} %get-tuple-element.48.joined_in), custom_call_target="tpu_custom_call" | custom-call | tf_op jit(solution)/shard_map/pallas_call | solution.py:267
  (6 shorter events, 0.1 us)
Async XLA Ops:
  0.0 13.7 %collective-permute-start.5 = (bf16[512,256]{1,0:T(8,128)(2,1)}, bf16[512,256]{1,0:T(8,128)(2,1)S(1)}, u32[]{:S(2)}, u32[]{:S(2)}) collective-permute-start(bf16[512,256]{1,0:T(8,128)(2,1)} %bitcast.11), channel_id=1, source_target_pairs={{0,24},{8,16},{16,8},{24,0},{1,25},{9,17},{17,9},{25,1},{2,26},{10... | collective-permute-start | bytes 786440 | tf_op jit(solution)/shard_map/ppermute | solution.py:285
  5.0 12.9 %collective-permute-start.4 = (bf16[512,256]{1,0:T(8,128)(2,1)}, bf16[512,256]{1,0:T(8,128)(2,1)S(1)}, u32[]{:S(2)}, u32[]{:S(2)}) collective-permute-start(bf16[512,256]{1,0:T(8,128)(2,1)} %bitcast.12), channel_id=1, source_target_pairs={{0,8},{8,0},{16,24},{24,16},{1,9},{9,1},{17,25},{25,17},{2,10},{10... | collective-permute-start | bytes 786440 | tf_op jit(solution)/shard_map/ppermute | solution.py:285
  5.1 1.0 %copy-start.1 = (bf16[1,32,16,256]{3,2,1,0:T(8,128)(2,1)S(1)}, bf16[1,32,16,256]{3,2,1,0:T(8,128)(2,1)}, u32[]{:S(2)}) copy-start(bf16[1,32,16,256]{3,2,1,0:T(8,128)(2,1)} %param.4) | copy-start | bytes 786436
  6.1 1.6 %collective-permute-start = (bf16[32,256]{1,0:T(8,128)(2,1)S(1)}, bf16[32,256]{1,0:T(8,128)(2,1)S(1)}, u32[]{:S(2)}, u32[]{:S(2)}) collective-permute-start(bf16[32,256]{1,0:T(8,128)(2,1)S(1)} %get-tuple-element.27), channel_id=1, source_target_pairs={{0,2},{4,6},{2,0},{6,4},{1,3},{5,7},{3,1},{7,5},{8,10},{12,14},{10... | collective-permute-start | bytes 49160 | tf_op jit(solution)/shard_map/ppermute | solution.py:304
  6.2 1.6 %collective-permute-start.1 = (bf16[32,256]{1,0:T(8,128)(2,1)S(1)}, bf16[32,256]{1,0:T(8,128)(2,1)S(1)}, u32[]{:S(2)}, u32[]{:S(2)}) collective-permute-start(bf16[32,256]{1,0:T(8,128)(2,1)S(1)} %get-tuple-element.28), channel_id=1, source_target_pairs={{2,4},{4,2},{3,5},{5,3},{10,12},{12,10},{11,13},{13,11},{18,20},{2... | collective-permute-start | bytes 49160 | tf_op jit(solution)/shard_map/ppermute | solution.py:304
  7.8 3.8 %collective-permute-start.2 = (bf16[24,256]{1,0:T(8,128)(2,1)S(1)}, bf16[24,256]{1,0:T(8,128)(2,1)S(1)}, u32[]{:S(2)}, u32[]{:S(2)}) collective-permute-start(bf16[24,256]{1,0:T(8,128)(2,1)S(1)} %shard_map.47), channel_id=1, source_target_pairs={{0,1},{1,0},{2,3},{3,2},{4,5},{5,4},{6,7},{7,6},{8,9},{9,8},{10,11... | collective-permute-start | bytes 36872 | tf_op jit(solution)/shard_map/ppermute | solution.py:315
  11.6 5.5 %copy-start = (bf16[1,2,9,512,128]{4,3,2,1,0:T(8,128)(2,1)S(1)}, bf16[1,2,9,512,128]{4,3,2,1,0:T(8,128)(2,1)}, u32[]{:S(2)}) copy-start(bf16[1,2,9,512,128]{4,3,2,1,0:T(8,128)(2,1)} %param.7) | copy-start | bytes 7077892
  11.6 7.1 %collective-permute-start.8 = (bf16[120,256]{1,0:T(8,128)(2,1)S(1)}, bf16[120,256]{1,0:T(8,128)(2,1)S(1)}, u32[]{:S(2)}, u32[]{:S(2)}) collective-permute-start(bf16[120,256]{1,0:T(8,128)(2,1)S(1)} %get-tuple-element.37), channel_id=1, source_target_pairs={{0,16},{8,24},{16,0},{24,8},{1,17},{9,25},{17,1},{25,9},{2,18},{10... | collective-permute-start | bytes 184328 | tf_op jit(solution)/shard_map/ppermute | solution.py:285
  12.2 7.3 %collective-permute-start.3 = (bf16[56,256]{1,0:T(8,128)(2,1)S(1)}, bf16[56,256]{1,0:T(8,128)(2,1)S(1)}, u32[]{:S(2)}, u32[]{:S(2)}) collective-permute-start(bf16[56,256]{1,0:T(8,128)(2,1)S(1)} %get-tuple-element.31.strip), channel_id=1, source_target_pairs={{0,8},{8,0},{16,24},{24,16},{1,9},{9,1},{17,25},{25,17},{2,10},{10... | collective-permute-start | bytes 86024 | tf_op jit(solution)/shard_map/ppermute | solution.py:285
  13.8 10.0 %collective-permute-start.10 = (bf16[448,256]{1,0:T(8,128)(2,1)S(1)}, bf16[448,256]{1,0:T(8,128)(2,1)S(1)}, u32[]{:S(2)}, u32[]{:S(2)}) collective-permute-start(bf16[448,256]{1,0:T(8,128)(2,1)S(1)} %slice.3), channel_id=1, source_target_pairs={{0,8},{8,0},{16,24},{24,16},{1,9},{9,1},{17,25},{25,17},{2,10},{10... | collective-permute-start | bytes 688136 | tf_op jit(solution)/shard_map/ppermute | solution.py:285
  18.0 1.2 %collective-permute-start.6 = (bf16[32,256]{1,0:T(8,128)(2,1)S(1)}, bf16[32,256]{1,0:T(8,128)(2,1)S(1)}, u32[]{:S(2)}, u32[]{:S(2)}) collective-permute-start(bf16[32,256]{1,0:T(8,128)(2,1)S(1)} %shard_map.50), channel_id=1, source_target_pairs={{0,2},{4,6},{2,0},{6,4},{1,3},{5,7},{3,1},{7,5},{8,10},{12,14},{10... | collective-permute-start | bytes 49160 | tf_op jit(solution)/shard_map/ppermute | solution.py:304
  18.1 1.4 %collective-permute-start.7 = (bf16[32,256]{1,0:T(8,128)(2,1)S(1)}, bf16[32,256]{1,0:T(8,128)(2,1)S(1)}, u32[]{:S(2)}, u32[]{:S(2)}) collective-permute-start(bf16[32,256]{1,0:T(8,128)(2,1)S(1)} %shard_map.51), channel_id=1, source_target_pairs={{0,2},{4,6},{2,0},{6,4},{1,3},{5,7},{3,1},{7,5},{8,10},{12,14},{10... | collective-permute-start | bytes 49160 | tf_op jit(solution)/shard_map/ppermute | solution.py:304
  19.6 5.2 %collective-permute-start.9 = (bf16[88,256]{1,0:T(8,128)(2,1)S(1)}, bf16[88,256]{1,0:T(8,128)(2,1)S(1)}, u32[]{:S(2)}, u32[]{:S(2)}) collective-permute-start(bf16[88,256]{1,0:T(8,128)(2,1)S(1)} %shard_map.52), channel_id=1, source_target_pairs={{0,8},{8,0},{16,24},{24,16},{1,9},{9,1},{17,25},{25,17},{2,10},{10... | collective-permute-start | bytes 135176 | tf_op jit(solution)/shard_map/ppermute | solution.py:285

commit v12 on v11

--- a/solution.py
+++ b/solution.py
@@ -11,7 +11,7 @@
 BF16, F32 = jnp.bfloat16, jnp.float32
 VMEM_SPEC = pl.BlockSpec(memory_space=pltpu.VMEM)
 LANES = 128
-PARTS = 2
+PARTS = 4
 BLOCKS = 4
 
 

time: 25.9 us -> 25.9 us (level)
  no operation moved by 1% of the time
where the time goes in v12:
time: 25.9 us; the launch traced here: 25.8 us
  starting transfers between devices  15.2 us (59%)
  waiting for transfers between devices  4.26 us (16%)
  Pallas kernels  3.66 us (14%)
  local copies, waits for them, and re-layouts  1.1 us (4%)
  other arithmetic  0.86 us (3%)
  between operations  0.75 us (3%)
    ppermute x6, starting transfers between devices, across(): return lax.ppermute(array, 'src', [(i, i ^ k) for i in range(4)])  12.2 us
    pallas_call x10, Pallas kernels, call(): pl.pallas_call(kernel, out_shape=outs, in_specs=[VMEM_SPEC] * len(ins), o...  3.66 us
    ppermute x6, waiting for transfers between devices, across(): return lax.ppermute(array, 'src', [(i, i ^ k) for i in range(4)])  1.87 us
    ppermute x1, starting transfers between devices, local(): beyond = [lax.ppermute(edges[0], 'slab', [(0, 1), (1, 0)])]  1.56 us
    ppermute x1, waiting for transfers between devices, local(): beyond = [lax.ppermute(edges[0], 'slab', [(0, 1), (1, 0)])]  1.55 us
    ppermute x4, starting transfers between devices, swap(): return lax.ppermute(array, 'shard', pairs + [(j, i) for i, j in pairs])  1.37 us
    unnamed x4, local copies, waits for them, and re-layouts  1.02 us
    ppermute x4, waiting for transfers between devices, swap(): return lax.ppermute(array, 'shard', pairs + [(j, i) for i, j in pairs])  0.84 us
  transfers between devices with their start and end apart: 11, of which 6 were waited for; matrix products, arithmetic and copies ran while one was open for 4% of the time, Pallas kernels for 10%

profile of v12, /device:TPU:0, one launch (start us, length us, event | category | flops | bytes accessed | tf_op | source)
XLA Modules:
  0.0 25.8 jit_solution(10048338774050791840)
XLA Ops:
  0.0 5.0 %collective-permute-start.5 = (bf16[512,256]{1,0:T(8,128)(2,1)}, bf16[512,256]{1,0:T(8,128)(2,1)S(1)}, u32[]{:S(2)}, u32[]{:S(2)}) collective-permute-start(bf16[512,256]{1,0:T(8,128)(2,1)} %bitcast.11), channel_id=1, source_target_pairs={{0,24},{8,16},{16,8},{24,0},{1,25},{9,17},{17,9},{25,1},{2,26},{10... | collective-permute-start | bytes 786440 | tf_op jit(solution)/shard_map/ppermute | solution.py:285
  5.0 0.0 collective-permute-start.4
  5.1 0.0 copy-start.1
  5.1 1.0 %copy-done.1 = bf16[1,32,16,256]{3,2,1,0:T(8,128)(2,1)S(1)} copy-done((bf16[1,32,16,256]{3,2,1,0:T(8,128)(2,1)S(1)}, bf16[1,32,16,256]{3,2,1,0:T(8,128)(2,1)}, u32[]{:S(2)}) %copy-start.1) | copy-done | bytes 262168
  6.1 0.1 shard_map.46
  6.1 0.1 collective-permute-start
  6.2 0.7 %collective-permute-start.1 = (bf16[32,256]{1,0:T(8,128)(2,1)S(1)}, bf16[32,256]{1,0:T(8,128)(2,1)S(1)}, u32[]{:S(2)}, u32[]{:S(2)}) collective-permute-start(bf16[32,256]{1,0:T(8,128)(2,1)S(1)} %get-tuple-element.28), channel_id=1, source_target_pairs={{2,4},{4,2},{3,5},{5,3},{10,12},{12,10},{11,13},{13,11},{18,20},{2... | collective-permute-start | bytes 49160 | tf_op jit(solution)/shard_map/ppermute | solution.py:304
  7.6 0.2 add_sine_fusion.enc
  7.8 0.0 collective-permute-done.got_a
  7.8 0.0 collective-permute-done.1.got_b
  7.8 1.6 %collective-permute-start.2 = (bf16[24,256]{1,0:T(8,128)(2,1)S(1)}, bf16[24,256]{1,0:T(8,128)(2,1)S(1)}, u32[]{:S(2)}, u32[]{:S(2)}) collective-permute-start(bf16[24,256]{1,0:T(8,128)(2,1)S(1)} %shard_map.47), channel_id=1, source_target_pairs={{0,1},{1,0},{2,3},{3,2},{4,5},{5,4},{6,7},{7,6},{8,9},{9,8},{10,11... | collective-permute-start | bytes 36872 | tf_op jit(solution)/shard_map/ppermute | solution.py:315
  9.4 0.7 %convert_bitcast_fusion = f32[2]{0:T(128)S(1)} fusion(s32[1,2]{1,0:T(1,128)} %param.5), kind=kLoop, calls=%fused_computation.13 | loop fusion | flops 2 | bytes 16 | tf_op jit(solution)/shard_map/broadcast_in_dim | solution.py:299
  10.0 1.5 %collective-permute-done.2.refs_0_ = bf16[24,256]{1,0:T(8,128)(2,1)S(1)} collective-permute-done((bf16[24,256]{1,0:T(8,128)(2,1)S(1)}, bf16[24,256]{1,0:T(8,128)(2,1)S(1)}, u32[]{:S(2)}, u32[]{:S(2)}) %collective-permute-start.2) | collective-permute-done | bytes 12320 | tf_op jit(solution)/shard_map/ppermute | solution.py:315
  11.6 0.0 copy-start
  11.6 0.6 %collective-permute-start.8 = (bf16[120,256]{1,0:T(8,128)(2,1)S(1)}, bf16[120,256]{1,0:T(8,128)(2,1)S(1)}, u32[]{:S(2)}, u32[]{:S(2)}) collective-permute-start(bf16[120,256]{1,0:T(8,128)(2,1)S(1)} %get-tuple-element.37), channel_id=1, source_target_pairs={{0,16},{8,24},{16,0},{24,8},{1,17},{9,25},{17,1},{25,9},{2,18},{10... | collective-permute-start | bytes 184328 | tf_op jit(solution)/shard_map/ppermute | solution.py:285
  12.2 1.5 %collective-permute-start.3 = (bf16[56,256]{1,0:T(8,128)(2,1)S(1)}, bf16[56,256]{1,0:T(8,128)(2,1)S(1)}, u32[]{:S(2)}, u32[]{:S(2)}) collective-permute-start(bf16[56,256]{1,0:T(8,128)(2,1)S(1)} %get-tuple-element.31.strip), channel_id=1, source_target_pairs={{0,8},{8,0},{16,24},{24,16},{1,9},{9,1},{17,25},{25,17},{2,10},{10... | collective-permute-start | bytes 86024 | tf_op jit(solution)/shard_map/ppermute | solution.py:285
  13.7 0.0 collective-permute-done.5.view.far
  13.8 3.2 %collective-permute-start.10 = (bf16[448,256]{1,0:T(8,128)(2,1)S(1)}, bf16[448,256]{1,0:T(8,128)(2,1)S(1)}, u32[]{:S(2)}, u32[]{:S(2)}) collective-permute-start(bf16[448,256]{1,0:T(8,128)(2,1)S(1)} %slice.3), channel_id=1, source_target_pairs={{0,8},{8,0},{16,24},{24,16},{1,9},{9,1},{17,25},{25,17},{2,10},{10... | collective-permute-start | bytes 688136 | tf_op jit(solution)/shard_map/ppermute | solution.py:285
  17.0 0.1 broadcast_in_dim.5.coords
  17.1 0.0 copy-done
  17.1 0.6 %shard_map.49 = (f32[512,256]{1,0:T(8,128)S(1)}, f32[528,128]{1,0:T(8,128)S(1)}) custom-call(f32[2,256]{1,0:T(2,128)S(1)} %broadcast_in_dim.5.coords, bf16[512,256]{1,0:T(8,128)(2,1)S(1)} %get-tuple-element.33.panel.own, f32[32,256]{1,0:T(8,128)S(1)} %add_sine_fusion.enc, bf16[56,256]{1,0:T(8,128)(2,1)S(1)} %get-tuple-element.31.strip, ...), custom_call_target="tpu_custom_call" | custom-call | flops 5000000000 | bytes 4000000 | tf_op jit(solution)/shard_map/pallas_call | solution.py:267
  17.7 0.3 %collective-permute-done.4.view.near = bf16[512,256]{1,0:T(8,128)(2,1)S(1)} collective-permute-done((bf16[512,256]{1,0:T(8,128)(2,1)}, bf16[512,256]{1,0:T(8,128)(2,1)S(1)}, u32[]{:S(2)}, u32[]{:S(2)}) %collective-permute-start.4) | collective-permute-done | bytes 262176 | tf_op jit(solution)/shard_map/ppermute | solution.py:285
  17.9 0.1 shard_map.50
  18.0 0.1 collective-permute-start.6
  18.1 0.1 shard_map.51
  18.1 0.6 %collective-permute-start.7 = (bf16[32,256]{1,0:T(8,128)(2,1)S(1)}, bf16[32,256]{1,0:T(8,128)(2,1)S(1)}, u32[]{:S(2)}, u32[]{:S(2)}) collective-permute-start(bf16[32,256]{1,0:T(8,128)(2,1)S(1)} %shard_map.51), channel_id=1, source_target_pairs={{0,2},{4,6},{2,0},{6,4},{1,3},{5,7},{3,1},{7,5},{8,10},{12,14},{10... | collective-permute-start | bytes 49160 | tf_op jit(solution)/shard_map/ppermute | solution.py:304
  18.7 0.0 collective-permute-done.8.strip.last_strip.first
  18.7 0.5 %collective-permute-done.6.near_a = bf16[32,256]{1,0:T(8,128)(2,1)S(1)} collective-permute-done((bf16[32,256]{1,0:T(8,128)(2,1)S(1)}, bf16[32,256]{1,0:T(8,128)(2,1)S(1)}, u32[]{:S(2)}, u32[]{:S(2)}) %collective-permute-start.6) | collective-permute-done | bytes 16416 | tf_op jit(solution)/shard_map/ppermute | solution.py:304
  19.3 0.3 %collective-permute-done.7.far_a = bf16[32,256]{1,0:T(8,128)(2,1)S(1)} collective-permute-done((bf16[32,256]{1,0:T(8,128)(2,1)S(1)}, bf16[32,256]{1,0:T(8,128)(2,1)S(1)}, u32[]{:S(2)}, u32[]{:S(2)}) %collective-permute-start.7) | collective-permute-done | bytes 16416 | tf_op jit(solution)/shard_map/ppermute | solution.py:304
  19.5 0.0 collective-permute-done.3.near_strip
  19.6 1.8 %collective-permute-start.9 = (bf16[88,256]{1,0:T(8,128)(2,1)S(1)}, bf16[88,256]{1,0:T(8,128)(2,1)S(1)}, u32[]{:S(2)}, u32[]{:S(2)}) collective-permute-start(bf16[88,256]{1,0:T(8,128)(2,1)S(1)} %shard_map.52), channel_id=1, source_target_pairs={{0,8},{8,0},{16,24},{24,16},{1,9},{9,1},{17,25},{25,17},{2,10},{10... | collective-permute-start | bytes 135176 | tf_op jit(solution)/shard_map/ppermute | solution.py:285
  21.4 1.2 %shard_map.53 = (f32[512,256]{1,0:T(8,128)S(1)}, f32[528,128]{1,0:T(8,128)S(1)}) custom-call(f32[2,256]{1,0:T(2,128)S(1)} %broadcast_in_dim.5.coords, bf16[512,256]{1,0:T(8,128)(2,1)S(1)} %collective-permute-done.4.view.near, bf16[512,256]{1,0:T(8,128)(2,1)S(1)} %collective-permute-done.5.view.far, f32[32,256]{1,0:T(8,128)S(1)} %add_sine_fusion.enc, ...), custom_call_target="tpu_custom_call" | custom-call | tf_op jit(solution)/shard_map/pallas_call | solution.py:267
  22.6 1.2 %collective-permute-done.10.last = bf16[448,256]{1,0:T(8,128)(2,1)S(1)} collective-permute-done((bf16[448,256]{1,0:T(8,128)(2,1)S(1)}, bf16[448,256]{1,0:T(8,128)(2,1)S(1)}, u32[]{:S(2)}, u32[]{:S(2)}) %collective-permute-start.10) | collective-permute-done | bytes 229408 | tf_op jit(solution)/shard_map/ppermute | solution.py:285
  23.8 0.6 %shard_map.54 = (f32[512,256]{1,0:T(8,128)S(1)}, f32[528,128]{1,0:T(8,128)S(1)}) custom-call(f32[2,256]{1,0:T(2,128)S(1)} %broadcast_in_dim.5.coords, bf16[120,256]{1,0:T(8,128)(2,1)S(1)} %collective-permute-done.8.strip.last_strip.first, bf16[448,256]{1,0:T(8,128)(2,1)S(1)} %collective-permute-done.10.last, f32[32,256]{1,0:T(8,128)S(1)} %add_sine_fusion.enc, ...), custom_call_target="tpu_custom_call" | custom-call | tf_op jit(solution)/shard_map/pallas_call | solution.py:267
  24.4 0.4 %collective-permute-done.9.relayed = bf16[88,256]{1,0:T(8,128)(2,1)S(1)} collective-permute-done((bf16[88,256]{1,0:T(8,128)(2,1)S(1)}, bf16[88,256]{1,0:T(8,128)(2,1)S(1)}, u32[]{:S(2)}, u32[]{:S(2)}) %collective-permute-start.9) | collective-permute-done | bytes 45088 | tf_op jit(solution)/shard_map/ppermute | solution.py:285
  24.8 1.0 %shard_map.55 = bf16[512,256]{1,0:T(8,128)(2,1)} custom-call(f32[32,256]{1,0:T(8,128)S(1)} %add_sine_fusion.enc, bf16[88,256]{1,0:T(8,128)(2,1)S(1)} %collective-permute-done.9.relayed, bf16[2,9,512,128]{3,2,1,0:T(8,128)(2,1)S(1)} %bitcast.10, f32[512,256]{1,0:T(8,128)S(1)} %get-tuple-element.47.base, f32[528,128]{1,0:T(8,128)S(1)} %get-tuple-element.48.joined_in), custom_call_target="tpu_custom_call" | custom-call | tf_op jit(solution)/shard_map/pallas_call | solution.py:267
  (6 shorter events, 0.1 us)
Async XLA Ops:
  0.0 13.7 %collective-permute-start.5 = (bf16[512,256]{1,0:T(8,128)(2,1)}, bf16[512,256]{1,0:T(8,128)(2,1)S(1)}, u32[]{:S(2)}, u32[]{:S(2)}) collective-permute-start(bf16[512,256]{1,0:T(8,128)(2,1)} %bitcast.11), channel_id=1, source_target_pairs={{0,24},{8,16},{16,8},{24,0},{1,25},{9,17},{17,9},{25,1},{2,26},{10... | collective-permute-start | bytes 786440 | tf_op jit(solution)/shard_map/ppermute | solution.py:285
  5.0 12.9 %collective-permute-start.4 = (bf16[512,256]{1,0:T(8,128)(2,1)}, bf16[512,256]{1,0:T(8,128)(2,1)S(1)}, u32[]{:S(2)}, u32[]{:S(2)}) collective-permute-start(bf16[512,256]{1,0:T(8,128)(2,1)} %bitcast.12), channel_id=1, source_target_pairs={{0,8},{8,0},{16,24},{24,16},{1,9},{9,1},{17,25},{25,17},{2,10},{10... | collective-permute-start | bytes 786440 | tf_op jit(solution)/shard_map/ppermute | solution.py:285
  5.1 1.0 %copy-start.1 = (bf16[1,32,16,256]{3,2,1,0:T(8,128)(2,1)S(1)}, bf16[1,32,16,256]{3,2,1,0:T(8,128)(2,1)}, u32[]{:S(2)}) copy-start(bf16[1,32,16,256]{3,2,1,0:T(8,128)(2,1)} %param.4) | copy-start | bytes 786436
  6.1 1.6 %collective-permute-start = (bf16[32,256]{1,0:T(8,128)(2,1)S(1)}, bf16[32,256]{1,0:T(8,128)(2,1)S(1)}, u32[]{:S(2)}, u32[]{:S(2)}) collective-permute-start(bf16[32,256]{1,0:T(8,128)(2,1)S(1)} %get-tuple-element.27), channel_id=1, source_target_pairs={{0,2},{4,6},{2,0},{6,4},{1,3},{5,7},{3,1},{7,5},{8,10},{12,14},{10... | collective-permute-start | bytes 49160 | tf_op jit(solution)/shard_map/ppermute | solution.py:304
  6.2 1.6 %collective-permute-start.1 = (bf16[32,256]{1,0:T(8,128)(2,1)S(1)}, bf16[32,256]{1,0:T(8,128)(2,1)S(1)}, u32[]{:S(2)}, u32[]{:S(2)}) collective-permute-start(bf16[32,256]{1,0:T(8,128)(2,1)S(1)} %get-tuple-element.28), channel_id=1, source_target_pairs={{2,4},{4,2},{3,5},{5,3},{10,12},{12,10},{11,13},{13,11},{18,20},{2... | collective-permute-start | bytes 49160 | tf_op jit(solution)/shard_map/ppermute | solution.py:304
  7.8 3.8 %collective-permute-start.2 = (bf16[24,256]{1,0:T(8,128)(2,1)S(1)}, bf16[24,256]{1,0:T(8,128)(2,1)S(1)}, u32[]{:S(2)}, u32[]{:S(2)}) collective-permute-start(bf16[24,256]{1,0:T(8,128)(2,1)S(1)} %shard_map.47), channel_id=1, source_target_pairs={{0,1},{1,0},{2,3},{3,2},{4,5},{5,4},{6,7},{7,6},{8,9},{9,8},{10,11... | collective-permute-start | bytes 36872 | tf_op jit(solution)/shard_map/ppermute | solution.py:315
  11.6 5.5 %copy-start = (bf16[1,2,9,512,128]{4,3,2,1,0:T(8,128)(2,1)S(1)}, bf16[1,2,9,512,128]{4,3,2,1,0:T(8,128)(2,1)}, u32[]{:S(2)}) copy-start(bf16[1,2,9,512,128]{4,3,2,1,0:T(8,128)(2,1)} %param.7) | copy-start | bytes 7077892
  11.6 7.1 %collective-permute-start.8 = (bf16[120,256]{1,0:T(8,128)(2,1)S(1)}, bf16[120,256]{1,0:T(8,128)(2,1)S(1)}, u32[]{:S(2)}, u32[]{:S(2)}) collective-permute-start(bf16[120,256]{1,0:T(8,128)(2,1)S(1)} %get-tuple-element.37), channel_id=1, source_target_pairs={{0,16},{8,24},{16,0},{24,8},{1,17},{9,25},{17,1},{25,9},{2,18},{10... | collective-permute-start | bytes 184328 | tf_op jit(solution)/shard_map/ppermute | solution.py:285
  12.2 7.3 %collective-permute-start.3 = (bf16[56,256]{1,0:T(8,128)(2,1)S(1)}, bf16[56,256]{1,0:T(8,128)(2,1)S(1)}, u32[]{:S(2)}, u32[]{:S(2)}) collective-permute-start(bf16[56,256]{1,0:T(8,128)(2,1)S(1)} %get-tuple-element.31.strip), channel_id=1, source_target_pairs={{0,8},{8,0},{16,24},{24,16},{1,9},{9,1},{17,25},{25,17},{2,10},{10... | collective-permute-start | bytes 86024 | tf_op jit(solution)/shard_map/ppermute | solution.py:285
  13.8 10.0 %collective-permute-start.10 = (bf16[448,256]{1,0:T(8,128)(2,1)S(1)}, bf16[448,256]{1,0:T(8,128)(2,1)S(1)}, u32[]{:S(2)}, u32[]{:S(2)}) collective-permute-start(bf16[448,256]{1,0:T(8,128)(2,1)S(1)} %slice.3), channel_id=1, source_target_pairs={{0,8},{8,0},{16,24},{24,16},{1,9},{9,1},{17,25},{25,17},{2,10},{10... | collective-permute-start | bytes 688136 | tf_op jit(solution)/shard_map/ppermute | solution.py:285
  18.0 1.2 %collective-permute-start.6 = (bf16[32,256]{1,0:T(8,128)(2,1)S(1)}, bf16[32,256]{1,0:T(8,128)(2,1)S(1)}, u32[]{:S(2)}, u32[]{:S(2)}) collective-permute-start(bf16[32,256]{1,0:T(8,128)(2,1)S(1)} %shard_map.50), channel_id=1, source_target_pairs={{0,2},{4,6},{2,0},{6,4},{1,3},{5,7},{3,1},{7,5},{8,10},{12,14},{10... | collective-permute-start | bytes 49160 | tf_op jit(solution)/shard_map/ppermute | solution.py:304
  18.1 1.4 %collective-permute-start.7 = (bf16[32,256]{1,0:T(8,128)(2,1)S(1)}, bf16[32,256]{1,0:T(8,128)(2,1)S(1)}, u32[]{:S(2)}, u32[]{:S(2)}) collective-permute-start(bf16[32,256]{1,0:T(8,128)(2,1)S(1)} %shard_map.51), channel_id=1, source_target_pairs={{0,2},{4,6},{2,0},{6,4},{1,3},{5,7},{3,1},{7,5},{8,10},{12,14},{10... | collective-permute-start | bytes 49160 | tf_op jit(solution)/shard_map/ppermute | solution.py:304
  19.6 5.2 %collective-permute-start.9 = (bf16[88,256]{1,0:T(8,128)(2,1)S(1)}, bf16[88,256]{1,0:T(8,128)(2,1)S(1)}, u32[]{:S(2)}, u32[]{:S(2)}) collective-permute-start(bf16[88,256]{1,0:T(8,128)(2,1)S(1)} %shard_map.52), channel_id=1, source_target_pairs={{0,8},{8,0},{16,24},{24,16},{1,9},{9,1},{17,25},{25,17},{2,10},{10... | collective-permute-start | bytes 135176 | tf_op jit(solution)/shard_map/ppermute | solution.py:285

commit v13 on v11

--- a/solution.py
+++ b/solution.py
@@ -12,7 +12,7 @@
 VMEM_SPEC = pl.BlockSpec(memory_space=pltpu.VMEM)
 LANES = 128
 PARTS = 2
-BLOCKS = 4
+BLOCKS = 2
 
 
 def encoding(rowpos, chan_count):

time: 25.9 us -> 25.9 us (level)
  no operation moved by 1% of the time
where the time goes in v13:
time: 25.9 us; the launch traced here: 25.8 us
  starting transfers between devices  15.2 us (59%)
  waiting for transfers between devices  4.34 us (17%)
  Pallas kernels  3.57 us (14%)
  local copies, waits for them, and re-layouts  1.1 us (4%)
  other arithmetic  0.86 us (3%)
  between operations  0.75 us (3%)
    ppermute x6, starting transfers between devices, across(): return lax.ppermute(array, 'src', [(i, i ^ k) for i in range(4)])  12.2 us
    pallas_call x10, Pallas kernels, call(): pl.pallas_call(kernel, out_shape=outs, in_specs=[VMEM_SPEC] * len(ins), o...  3.57 us
    ppermute x6, waiting for transfers between devices, across(): return lax.ppermute(array, 'src', [(i, i ^ k) for i in range(4)])  1.95 us
    ppermute x1, starting transfers between devices, local(): beyond = [lax.ppermute(edges[0], 'slab', [(0, 1), (1, 0)])]  1.56 us
    ppermute x1, waiting for transfers between devices, local(): beyond = [lax.ppermute(edges[0], 'slab', [(0, 1), (1, 0)])]  1.55 us
    ppermute x4, starting transfers between devices, swap(): return lax.ppermute(array, 'shard', pairs + [(j, i) for i, j in pairs])  1.37 us
    unnamed x4, local copies, waits for them, and re-layouts  1.02 us
    ppermute x4, waiting for transfers between devices, swap(): return lax.ppermute(array, 'shard', pairs + [(j, i) for i, j in pairs])  0.84 us
  transfers between devices with their start and end apart: 11, of which 6 were waited for; matrix products, arithmetic and copies ran while one was open for 4% of the time, Pallas kernels for 10%

profile of v13, /device:TPU:0, one launch (start us, length us, event | category | flops | bytes accessed | tf_op | source)
XLA Modules:
  0.0 25.8 jit_solution(4798390521191923192)
XLA Ops:
  0.0 5.0 %collective-permute-start.5 = (bf16[512,256]{1,0:T(8,128)(2,1)}, bf16[512,256]{1,0:T(8,128)(2,1)S(1)}, u32[]{:S(2)}, u32[]{:S(2)}) collective-permute-start(bf16[512,256]{1,0:T(8,128)(2,1)} %bitcast.11), channel_id=1, source_target_pairs={{0,24},{8,16},{16,8},{24,0},{1,25},{9,17},{17,9},{25,1},{2,26},{10... | collective-permute-start | bytes 786440 | tf_op jit(solution)/shard_map/ppermute | solution.py:285
  5.0 0.0 collective-permute-start.4
  5.1 0.0 copy-start.1
  5.1 1.0 %copy-done.1 = bf16[1,32,16,256]{3,2,1,0:T(8,128)(2,1)S(1)} copy-done((bf16[1,32,16,256]{3,2,1,0:T(8,128)(2,1)S(1)}, bf16[1,32,16,256]{3,2,1,0:T(8,128)(2,1)}, u32[]{:S(2)}) %copy-start.1) | copy-done | bytes 262168
  6.1 0.1 shard_map.46
  6.1 0.1 collective-permute-start
  6.2 0.7 %collective-permute-start.1 = (bf16[32,256]{1,0:T(8,128)(2,1)S(1)}, bf16[32,256]{1,0:T(8,128)(2,1)S(1)}, u32[]{:S(2)}, u32[]{:S(2)}) collective-permute-start(bf16[32,256]{1,0:T(8,128)(2,1)S(1)} %get-tuple-element.28), channel_id=1, source_target_pairs={{2,4},{4,2},{3,5},{5,3},{10,12},{12,10},{11,13},{13,11},{18,20},{2... | collective-permute-start | bytes 49160 | tf_op jit(solution)/shard_map/ppermute | solution.py:304
  7.6 0.2 add_sine_fusion.enc
  7.8 0.0 collective-permute-done.got_a
  7.8 0.0 collective-permute-done.1.got_b
  7.8 1.6 %collective-permute-start.2 = (bf16[24,256]{1,0:T(8,128)(2,1)S(1)}, bf16[24,256]{1,0:T(8,128)(2,1)S(1)}, u32[]{:S(2)}, u32[]{:S(2)}) collective-permute-start(bf16[24,256]{1,0:T(8,128)(2,1)S(1)} %shard_map.47), channel_id=1, source_target_pairs={{0,1},{1,0},{2,3},{3,2},{4,5},{5,4},{6,7},{7,6},{8,9},{9,8},{10,11... | collective-permute-start | bytes 36872 | tf_op jit(solution)/shard_map/ppermute | solution.py:315
  9.4 0.7 %convert_bitcast_fusion = f32[2]{0:T(128)S(1)} fusion(s32[1,2]{1,0:T(1,128)} %param.5), kind=kLoop, calls=%fused_computation.13 | loop fusion | flops 2 | bytes 16 | tf_op jit(solution)/shard_map/broadcast_in_dim | solution.py:299
  10.0 1.5 %collective-permute-done.2.refs_0_ = bf16[24,256]{1,0:T(8,128)(2,1)S(1)} collective-permute-done((bf16[24,256]{1,0:T(8,128)(2,1)S(1)}, bf16[24,256]{1,0:T(8,128)(2,1)S(1)}, u32[]{:S(2)}, u32[]{:S(2)}) %collective-permute-start.2) | collective-permute-done | bytes 12320 | tf_op jit(solution)/shard_map/ppermute | solution.py:315
  11.6 0.0 copy-start
  11.6 0.6 %collective-permute-start.8 = (bf16[120,256]{1,0:T(8,128)(2,1)S(1)}, bf16[120,256]{1,0:T(8,128)(2,1)S(1)}, u32[]{:S(2)}, u32[]{:S(2)}) collective-permute-start(bf16[120,256]{1,0:T(8,128)(2,1)S(1)} %get-tuple-element.37), channel_id=1, source_target_pairs={{0,16},{8,24},{16,0},{24,8},{1,17},{9,25},{17,1},{25,9},{2,18},{10... | collective-permute-start | bytes 184328 | tf_op jit(solution)/shard_map/ppermute | solution.py:285
  12.2 1.5 %collective-permute-start.3 = (bf16[56,256]{1,0:T(8,128)(2,1)S(1)}, bf16[56,256]{1,0:T(8,128)(2,1)S(1)}, u32[]{:S(2)}, u32[]{:S(2)}) collective-permute-start(bf16[56,256]{1,0:T(8,128)(2,1)S(1)} %get-tuple-element.31.strip), channel_id=1, source_target_pairs={{0,8},{8,0},{16,24},{24,16},{1,9},{9,1},{17,25},{25,17},{2,10},{10... | collective-permute-start | bytes 86024 | tf_op jit(solution)/shard_map/ppermute | solution.py:285
  13.7 0.0 collective-permute-done.5.view.far
  13.8 3.2 %collective-permute-start.10 = (bf16[448,256]{1,0:T(8,128)(2,1)S(1)}, bf16[448,256]{1,0:T(8,128)(2,1)S(1)}, u32[]{:S(2)}, u32[]{:S(2)}) collective-permute-start(bf16[448,256]{1,0:T(8,128)(2,1)S(1)} %slice.3), channel_id=1, source_target_pairs={{0,8},{8,0},{16,24},{24,16},{1,9},{9,1},{17,25},{25,17},{2,10},{10... | collective-permute-start | bytes 688136 | tf_op jit(solution)/shard_map/ppermute | solution.py:285
  17.0 0.1 broadcast_in_dim.5.coords
  17.1 0.0 copy-done
  17.1 0.6 %shard_map.49 = (f32[512,256]{1,0:T(8,128)S(1)}, f32[528,128]{1,0:T(8,128)S(1)}) custom-call(f32[2,256]{1,0:T(2,128)S(1)} %broadcast_in_dim.5.coords, bf16[512,256]{1,0:T(8,128)(2,1)S(1)} %get-tuple-element.33.panel.own, f32[32,256]{1,0:T(8,128)S(1)} %add_sine_fusion.enc, bf16[56,256]{1,0:T(8,128)(2,1)S(1)} %get-tuple-element.31.strip, ...), custom_call_target="tpu_custom_call" | custom-call | flops 5000000000 | bytes 4000000 | tf_op jit(solution)/shard_map/pallas_call | solution.py:267
  17.7 0.3 %collective-permute-done.4.view.near = bf16[512,256]{1,0:T(8,128)(2,1)S(1)} collective-permute-done((bf16[512,256]{1,0:T(8,128)(2,1)}, bf16[512,256]{1,0:T(8,128)(2,1)S(1)}, u32[]{:S(2)}, u32[]{:S(2)}) %collective-permute-start.4) | collective-permute-done | bytes 262176 | tf_op jit(solution)/shard_map/ppermute | solution.py:285
  17.9 0.1 shard_map.50
  18.0 0.1 collective-permute-start.6
  18.1 0.1 shard_map.51
  18.1 0.6 %collective-permute-start.7 = (bf16[32,256]{1,0:T(8,128)(2,1)S(1)}, bf16[32,256]{1,0:T(8,128)(2,1)S(1)}, u32[]{:S(2)}, u32[]{:S(2)}) collective-permute-start(bf16[32,256]{1,0:T(8,128)(2,1)S(1)} %shard_map.51), channel_id=1, source_target_pairs={{0,2},{4,6},{2,0},{6,4},{1,3},{5,7},{3,1},{7,5},{8,10},{12,14},{10... | collective-permute-start | bytes 49160 | tf_op jit(solution)/shard_map/ppermute | solution.py:304
  18.7 0.0 collective-permute-done.8.strip.last_strip.first
  18.7 0.5 %collective-permute-done.6.near_a = bf16[32,256]{1,0:T(8,128)(2,1)S(1)} collective-permute-done((bf16[32,256]{1,0:T(8,128)(2,1)S(1)}, bf16[32,256]{1,0:T(8,128)(2,1)S(1)}, u32[]{:S(2)}, u32[]{:S(2)}) %collective-permute-start.6) | collective-permute-done | bytes 16416 | tf_op jit(solution)/shard_map/ppermute | solution.py:304
  19.3 0.3 %collective-permute-done.7.far_a = bf16[32,256]{1,0:T(8,128)(2,1)S(1)} collective-permute-done((bf16[32,256]{1,0:T(8,128)(2,1)S(1)}, bf16[32,256]{1,0:T(8,128)(2,1)S(1)}, u32[]{:S(2)}, u32[]{:S(2)}) %collective-permute-start.7) | collective-permute-done | bytes 16416 | tf_op jit(solution)/shard_map/ppermute | solution.py:304
  19.5 0.0 collective-permute-done.3.near_strip
  19.6 1.8 %collective-permute-start.9 = (bf16[88,256]{1,0:T(8,128)(2,1)S(1)}, bf16[88,256]{1,0:T(8,128)(2,1)S(1)}, u32[]{:S(2)}, u32[]{:S(2)}) collective-permute-start(bf16[88,256]{1,0:T(8,128)(2,1)S(1)} %shard_map.52), channel_id=1, source_target_pairs={{0,8},{8,0},{16,24},{24,16},{1,9},{9,1},{17,25},{25,17},{2,10},{10... | collective-permute-start | bytes 135176 | tf_op jit(solution)/shard_map/ppermute | solution.py:285
  21.4 1.2 %shard_map.53 = (f32[512,256]{1,0:T(8,128)S(1)}, f32[528,128]{1,0:T(8,128)S(1)}) custom-call(f32[2,256]{1,0:T(2,128)S(1)} %broadcast_in_dim.5.coords, bf16[512,256]{1,0:T(8,128)(2,1)S(1)} %collective-permute-done.4.view.near, bf16[512,256]{1,0:T(8,128)(2,1)S(1)} %collective-permute-done.5.view.far, f32[32,256]{1,0:T(8,128)S(1)} %add_sine_fusion.enc, ...), custom_call_target="tpu_custom_call" | custom-call | tf_op jit(solution)/shard_map/pallas_call | solution.py:267
  22.5 1.3 %collective-permute-done.10.last = bf16[448,256]{1,0:T(8,128)(2,1)S(1)} collective-permute-done((bf16[448,256]{1,0:T(8,128)(2,1)S(1)}, bf16[448,256]{1,0:T(8,128)(2,1)S(1)}, u32[]{:S(2)}, u32[]{:S(2)}) %collective-permute-start.10) | collective-permute-done | bytes 229408 | tf_op jit(solution)/shard_map/ppermute | solution.py:285
  23.8 0.5 %shard_map.54 = (f32[512,256]{1,0:T(8,128)S(1)}, f32[528,128]{1,0:T(8,128)S(1)}) custom-call(f32[2,256]{1,0:T(2,128)S(1)} %broadcast_in_dim.5.coords, bf16[120,256]{1,0:T(8,128)(2,1)S(1)} %collective-permute-done.8.strip.last_strip.first, bf16[448,256]{1,0:T(8,128)(2,1)S(1)} %collective-permute-done.10.last, f32[32,256]{1,0:T(8,128)S(1)} %add_sine_fusion.enc, ...), custom_call_target="tpu_custom_call" | custom-call | tf_op jit(solution)/shard_map/pallas_call | solution.py:267
  24.3 0.4 %collective-permute-done.9.relayed = bf16[88,256]{1,0:T(8,128)(2,1)S(1)} collective-permute-done((bf16[88,256]{1,0:T(8,128)(2,1)S(1)}, bf16[88,256]{1,0:T(8,128)(2,1)S(1)}, u32[]{:S(2)}, u32[]{:S(2)}) %collective-permute-start.9) | collective-permute-done | bytes 45088 | tf_op jit(solution)/shard_map/ppermute | solution.py:285
  24.8 1.0 %shard_map.55 = bf16[512,256]{1,0:T(8,128)(2,1)} custom-call(f32[32,256]{1,0:T(8,128)S(1)} %add_sine_fusion.enc, bf16[88,256]{1,0:T(8,128)(2,1)S(1)} %collective-permute-done.9.relayed, bf16[2,9,512,128]{3,2,1,0:T(8,128)(2,1)S(1)} %bitcast.10, f32[512,256]{1,0:T(8,128)S(1)} %get-tuple-element.47.base, f32[528,128]{1,0:T(8,128)S(1)} %get-tuple-element.48.joined_in), custom_call_target="tpu_custom_call" | custom-call | tf_op jit(solution)/shard_map/pallas_call | solution.py:267
  (6 shorter events, 0.1 us)
Async XLA Ops:
  0.0 13.7 %collective-permute-start.5 = (bf16[512,256]{1,0:T(8,128)(2,1)}, bf16[512,256]{1,0:T(8,128)(2,1)S(1)}, u32[]{:S(2)}, u32[]{:S(2)}) collective-permute-start(bf16[512,256]{1,0:T(8,128)(2,1)} %bitcast.11), channel_id=1, source_target_pairs={{0,24},{8,16},{16,8},{24,0},{1,25},{9,17},{17,9},{25,1},{2,26},{10... | collective-permute-start | bytes 786440 | tf_op jit(solution)/shard_map/ppermute | solution.py:285
  5.0 12.9 %collective-permute-start.4 = (bf16[512,256]{1,0:T(8,128)(2,1)}, bf16[512,256]{1,0:T(8,128)(2,1)S(1)}, u32[]{:S(2)}, u32[]{:S(2)}) collective-permute-start(bf16[512,256]{1,0:T(8,128)(2,1)} %bitcast.12), channel_id=1, source_target_pairs={{0,8},{8,0},{16,24},{24,16},{1,9},{9,1},{17,25},{25,17},{2,10},{10... | collective-permute-start | bytes 786440 | tf_op jit(solution)/shard_map/ppermute | solution.py:285
  5.1 1.0 %copy-start.1 = (bf16[1,32,16,256]{3,2,1,0:T(8,128)(2,1)S(1)}, bf16[1,32,16,256]{3,2,1,0:T(8,128)(2,1)}, u32[]{:S(2)}) copy-start(bf16[1,32,16,256]{3,2,1,0:T(8,128)(2,1)} %param.4) | copy-start | bytes 786436
  6.1 1.6 %collective-permute-start = (bf16[32,256]{1,0:T(8,128)(2,1)S(1)}, bf16[32,256]{1,0:T(8,128)(2,1)S(1)}, u32[]{:S(2)}, u32[]{:S(2)}) collective-permute-start(bf16[32,256]{1,0:T(8,128)(2,1)S(1)} %get-tuple-element.27), channel_id=1, source_target_pairs={{0,2},{4,6},{2,0},{6,4},{1,3},{5,7},{3,1},{7,5},{8,10},{12,14},{10... | collective-permute-start | bytes 49160 | tf_op jit(solution)/shard_map/ppermute | solution.py:304
  6.2 1.6 %collective-permute-start.1 = (bf16[32,256]{1,0:T(8,128)(2,1)S(1)}, bf16[32,256]{1,0:T(8,128)(2,1)S(1)}, u32[]{:S(2)}, u32[]{:S(2)}) collective-permute-start(bf16[32,256]{1,0:T(8,128)(2,1)S(1)} %get-tuple-element.28), channel_id=1, source_target_pairs={{2,4},{4,2},{3,5},{5,3},{10,12},{12,10},{11,13},{13,11},{18,20},{2... | collective-permute-start | bytes 49160 | tf_op jit(solution)/shard_map/ppermute | solution.py:304
  7.8 3.8 %collective-permute-start.2 = (bf16[24,256]{1,0:T(8,128)(2,1)S(1)}, bf16[24,256]{1,0:T(8,128)(2,1)S(1)}, u32[]{:S(2)}, u32[]{:S(2)}) collective-permute-start(bf16[24,256]{1,0:T(8,128)(2,1)S(1)} %shard_map.47), channel_id=1, source_target_pairs={{0,1},{1,0},{2,3},{3,2},{4,5},{5,4},{6,7},{7,6},{8,9},{9,8},{10,11... | collective-permute-start | bytes 36872 | tf_op jit(solution)/shard_map/ppermute | solution.py:315
  11.6 5.5 %copy-start = (bf16[1,2,9,512,128]{4,3,2,1,0:T(8,128)(2,1)S(1)}, bf16[1,2,9,512,128]{4,3,2,1,0:T(8,128)(2,1)}, u32[]{:S(2)}) copy-start(bf16[1,2,9,512,128]{4,3,2,1,0:T(8,128)(2,1)} %param.7) | copy-start | bytes 7077892
  11.6 7.1 %collective-permute-start.8 = (bf16[120,256]{1,0:T(8,128)(2,1)S(1)}, bf16[120,256]{1,0:T(8,128)(2,1)S(1)}, u32[]{:S(2)}, u32[]{:S(2)}) collective-permute-start(bf16[120,256]{1,0:T(8,128)(2,1)S(1)} %get-tuple-element.37), channel_id=1, source_target_pairs={{0,16},{8,24},{16,0},{24,8},{1,17},{9,25},{17,1},{25,9},{2,18},{10... | collective-permute-start | bytes 184328 | tf_op jit(solution)/shard_map/ppermute | solution.py:285
  12.2 7.3 %collective-permute-start.3 = (bf16[56,256]{1,0:T(8,128)(2,1)S(1)}, bf16[56,256]{1,0:T(8,128)(2,1)S(1)}, u32[]{:S(2)}, u32[]{:S(2)}) collective-permute-start(bf16[56,256]{1,0:T(8,128)(2,1)S(1)} %get-tuple-element.31.strip), channel_id=1, source_target_pairs={{0,8},{8,0},{16,24},{24,16},{1,9},{9,1},{17,25},{25,17},{2,10},{10... | collective-permute-start | bytes 86024 | tf_op jit(solution)/shard_map/ppermute | solution.py:285
  13.8 10.0 %collective-permute-start.10 = (bf16[448,256]{1,0:T(8,128)(2,1)S(1)}, bf16[448,256]{1,0:T(8,128)(2,1)S(1)}, u32[]{:S(2)}, u32[]{:S(2)}) collective-permute-start(bf16[448,256]{1,0:T(8,128)(2,1)S(1)} %slice.3), channel_id=1, source_target_pairs={{0,8},{8,0},{16,24},{24,16},{1,9},{9,1},{17,25},{25,17},{2,10},{10... | collective-permute-start | bytes 688136 | tf_op jit(solution)/shard_map/ppermute | solution.py:285
  18.0 1.2 %collective-permute-start.6 = (bf16[32,256]{1,0:T(8,128)(2,1)S(1)}, bf16[32,256]{1,0:T(8,128)(2,1)S(1)}, u32[]{:S(2)}, u32[]{:S(2)}) collective-permute-start(bf16[32,256]{1,0:T(8,128)(2,1)S(1)} %shard_map.50), channel_id=1, source_target_pairs={{0,2},{4,6},{2,0},{6,4},{1,3},{5,7},{3,1},{7,5},{8,10},{12,14},{10... | collective-permute-start | bytes 49160 | tf_op jit(solution)/shard_map/ppermute | solution.py:304
  18.1 1.4 %collective-permute-start.7 = (bf16[32,256]{1,0:T(8,128)(2,1)S(1)}, bf16[32,256]{1,0:T(8,128)(2,1)S(1)}, u32[]{:S(2)}, u32[]{:S(2)}) collective-permute-start(bf16[32,256]{1,0:T(8,128)(2,1)S(1)} %shard_map.51), channel_id=1, source_target_pairs={{0,2},{4,6},{2,0},{6,4},{1,3},{5,7},{3,1},{7,5},{8,10},{12,14},{10... | collective-permute-start | bytes 49160 | tf_op jit(solution)/shard_map/ppermute | solution.py:304
  19.6 5.2 %collective-permute-start.9 = (bf16[88,256]{1,0:T(8,128)(2,1)S(1)}, bf16[88,256]{1,0:T(8,128)(2,1)S(1)}, u32[]{:S(2)}, u32[]{:S(2)}) collective-permute-start(bf16[88,256]{1,0:T(8,128)(2,1)S(1)} %shard_map.52), channel_id=1, source_target_pairs={{0,8},{8,0},{16,24},{24,16},{1,9},{9,1},{17,25},{25,17},{2,10},{10... | collective-permute-start | bytes 135176 | tf_op jit(solution)/shard_map/ppermute | solution.py:285
